TPU v7x, 512 devices: a whole 4x8x8 slice. The times are simulated.
512 devices in a mesh: dp: 32 (over y_lo, z, core), section: 4 (over x), mp: 4 (over y_hi).
Axes of the slice: x: 4, y: 8 (y_hi: 4, y_lo: 2; y = y_hi * 2 + y_lo), z: 8, core: 2. Of those that a mesh axis runs over, the one named last changes fastest.
Arguments:
- saved_inputs: bfloat16 [4, 2, 384, 16, 5120], P('section', None, 'dp', None, 'mp'), may hold values from -150 to 150
- norm_gains: float32 [4, 5120], P('section', 'mp'), may hold values from 0.1 to 1.9
- conv_taps: bfloat16 [4, 15, 5120], P('section', None, 'mp'), may hold values from -1 to 1
- head_weight: bfloat16 [5120, 1024], P('mp'), as said below
- queries: bfloat16 [2, 384, 1024], P(None, 'dp', 'mp'), may hold values from -12 to 12
- key_embeds: bfloat16 [2, 384, 1024], P(None, 'dp', 'mp'), may hold values from -12 to 12
- positives: int32 [2, 384], P(None, 'dp'), may hold values from 0 to 383, each once within a row
- pair_weights: float32 [2, 384], P(None, 'dp'), may hold values from 64 to 256
Outputs:
- input_grads: bfloat16 [4, 2, 384, 16, 5120], P('section', None, 'dp', None, 'mp')
- tap_grads: float32 [4, 15, 5120], P('section', None, 'mp')
- key_grads: float32 [2, 384, 1024], P(None, 'dp', 'mp')
Inputs may be any that keep to these rules, and one draw needn't show every extreme that they name: positives[m] names each of the 384 texts of micro-batch m exactly once. `head_weight`: every entry lies within -6 / sqrt(5120) and 6 / sqrt(5120).
All inputs are finite; a program needn't handle non-finite values.
Results may differ from a plain program's by a relative error of at most 0.025.
Values may be sent and summed in bfloat16 or wider, within the bound.
No kernel may reach another device: no remote copies, remote signals or barrier semaphores. Data moves between devices by JAX's collectives and lax.ppermute only.
A program may use at most 64 MiB of HBM per device.

v0:
```python
import math

import jax
import jax.numpy as jnp
from jax import lax
from jax.sharding import PartitionSpec as P

D = 5120
EMB = 1024
FRAMES = 16


epsilon = 1e-05


def from_behind(value, axis, steps):
    count = lax.axis_size(axis)
    leading, last = (max(0, -steps), min(count, count - steps))
    return lax.ppermute(value, axis, [(source, source + steps) for source in range(leading, last)])


def frame_conv(signal, weights_wide):
    kernel_size = weights_wide.shape[0]
    half_width = kernel_size // 2
    frame_count = signal.shape[1]
    padded = jnp.pad(signal, ((0, 0), (half_width, half_width), (0, 0)))
    running = jnp.zeros_like(signal)
    for offset in range(kernel_size):
        running = running + weights_wide[offset] * padded[:, offset : offset + frame_count, :]
    return (running, padded)


def frame_conv_back(incoming, weights_wide):
    kernel_size = weights_wide.shape[0]
    half_width = kernel_size // 2
    frame_count = incoming.shape[1]
    padded = jnp.pad(incoming, ((0, 0), (half_width, half_width), (0, 0)))
    running = jnp.zeros_like(incoming)
    for offset in range(kernel_size):
        start_at = 2 * half_width - offset
        running = running + weights_wide[offset] * padded[:, start_at : start_at + frame_count, :]
    return running


def section_step(inputs, norm_gain, weights_wide, upstream, row_sum, row_square):
    inputs_wide = inputs.astype(jnp.float32)
    row_mean = (row_sum / D)[..., None]
    variance = (row_square / D)[..., None] - row_mean * row_mean
    inv_std = lax.rsqrt(variance + epsilon)
    normed = (inputs_wide - row_mean) * inv_std
    hidden = normed * norm_gain
    conv_out, padded = frame_conv(hidden, weights_wide)
    sigmoid_gate = jax.nn.sigmoid(conv_out)
    upstream_wide = upstream.astype(jnp.float32)
    grad_conv = upstream_wide * sigmoid_gate * (1.0 + conv_out * (1.0 - sigmoid_gate))
    frame_count = inputs.shape[1]
    tap_grad = jnp.stack(
        [
            jnp.sum(grad_conv * padded[:, offset : offset + frame_count, :], axis=(0, 1))
            for offset in range(weights_wide.shape[0])
        ]
    )
    grad_normed = frame_conv_back(grad_conv, weights_wide) * norm_gain
    sum_first, sum_second = lax.psum(
        (jnp.sum(grad_normed, axis=-1), jnp.sum(grad_normed * normed, axis=-1)), "mp"
    )
    grad_in = upstream_wide + inv_std * (
        grad_normed - (sum_first / D)[..., None] - normed * (sum_second / D)[..., None]
    )
    return (grad_in.astype(jnp.bfloat16), tap_grad)


def pair_loss_grads(queries_now, keys_now, positives_now, weights_now, head_weight):
    score_scale = 1.0 / math.sqrt(EMB)
    contract_last = (((1,), (1,)), ((), ()))
    contract_first = (((0,), (0,)), ((), ()))
    query_full = lax.all_gather(queries_now, "mp", axis=1, tiled=True)
    key_full = lax.all_gather(keys_now, "mp", axis=1, tiled=True)
    all_keys = lax.all_gather(key_full, "dp", axis=0, tiled=True)
    scores = (
        lax.dot_general(query_full, all_keys, contract_last, preferred_element_type=jnp.float32)
        * score_scale
    )
    pair_count = scores.shape[1]
    row_max = jnp.max(scores, axis=1, keepdims=True)
    exp_scores = jnp.exp(scores - row_max)
    softmax_probs = exp_scores / jnp.sum(exp_scores, axis=1, keepdims=True)
    positive_hot = (
        positives_now[:, None] == jnp.arange(pair_count, dtype=jnp.int32)[None, :]
    ).astype(jnp.float32)
    pair_grad = (weights_now[:, None] * (softmax_probs - positive_hot)).astype(jnp.bfloat16)
    query_grad = (
        jnp.dot(pair_grad, all_keys, preferred_element_type=jnp.float32) * score_scale
    ).astype(jnp.bfloat16)
    key_grad = lax.psum_scatter(
        (
            lax.dot_general(
                pair_grad, queries_now, contract_first, preferred_element_type=jnp.float32
            )
            * score_scale
        ).astype(jnp.bfloat16),
        "dp",
        scatter_dimension=0,
        tiled=True,
    ).astype(jnp.float32)
    pooled = lax.dot_general(
        query_grad, head_weight, contract_last, preferred_element_type=jnp.float32
    )
    frame_grad = (pooled / FRAMES).astype(jnp.bfloat16)
    return (key_grad, frame_grad)


def per_device(
    saved_inputs, norm_gains, conv_taps, head_weight, queries, key_embeds, positives, pair_weights
):
    micro_count = saved_inputs.shape[1]
    key_list = []
    frame_list = []
    for micro_index in range(micro_count):
        key_grad, frame_grad = pair_loss_grads(
            queries[micro_index],
            key_embeds[micro_index],
            positives[micro_index],
            pair_weights[micro_index],
            head_weight,
        )
        key_list.append(key_grad)
        frame_list.append(frame_grad)
    key_grads = jnp.stack(key_list)
    frame_grads = jnp.stack(frame_list)
    section_count = lax.axis_size("section")
    section_now = lax.axis_index("section")
    is_last = section_now == section_count - 1
    inputs_all = saved_inputs[0]
    norm_gain = norm_gains[0]
    weights_wide = conv_taps[0].astype(jnp.float32)
    results = jnp.zeros(inputs_all.shape, jnp.bfloat16)
    tap_total = jnp.zeros(weights_wide.shape, jnp.float32)
    incoming = jnp.zeros(inputs_all.shape[1:], jnp.bfloat16)
    tick_count = section_count + micro_count - 1
    for tick_index in range(tick_count):
        slot_raw = tick_index - (section_count - 1 - section_now)
        is_valid = (slot_raw >= 0) & (slot_raw < micro_count)
        slot_index = jnp.clip(slot_raw, 0, micro_count - 1)
        inputs_now = lax.dynamic_index_in_dim(inputs_all, slot_index, 0, keepdims=False)
        head_rows = lax.dynamic_index_in_dim(frame_grads, slot_index, 0, keepdims=False)
        from_head = jnp.broadcast_to(head_rows[:, None, :], incoming.shape)
        upstream = jnp.where(is_last, from_head, incoming)
        inputs_now_wide = inputs_now.astype(jnp.float32)
        row_sum, row_square = lax.psum(
            (
                jnp.sum(inputs_now_wide, axis=-1),
                jnp.sum(inputs_now_wide * inputs_now_wide, axis=-1),
            ),
            "mp",
        )
        grad_in, tap_grad = section_step(
            inputs_now, norm_gain, weights_wide, upstream, row_sum, row_square
        )
        current = lax.dynamic_index_in_dim(results, slot_index, 0, keepdims=False)
        results = lax.dynamic_update_index_in_dim(
            results, jnp.where(is_valid, grad_in, current), slot_index, 0
        )
        tap_total = tap_total + jnp.where(is_valid, tap_grad, 0.0)
        if tick_index + 1 < tick_count:
            incoming = from_behind(grad_in, "section", -1)
    tap_grads = lax.psum(tap_total.astype(jnp.bfloat16), "dp").astype(jnp.float32)
    return (results[None], tap_grads[None], key_grads)


def solution(mesh):
    return jax.shard_map(
        per_device,
        mesh=mesh,
        in_specs=(
            P("section", None, "dp", None, "mp"),
            P("section", "mp"),
            P("section", None, "mp"),
            P("mp", None),
            P(None, "dp", "mp"),
            P(None, "dp", "mp"),
            P(None, "dp"),
            P(None, "dp"),
        ),
        out_specs=(
            P("section", None, "dp", None, "mp"),
            P("section", None, "mp"),
            P(None, "dp", "mp"),
        ),
        check_vma=False,
    )
```

profile of v0, /device:TPU:1, one launch (start us, length us, event | category | flops | bytes accessed | tf_op | source)
XLA Modules:
  0.0 618.0 jit_solution(15103321486277463573)
XLA Ops:
  3.9 14.2 %all-gather = bf16[1,12,1024]{2,1,0:T(8,128)(2,1)S(1)} all-gather(bf16[1,12,256]{2,1,0:T(8,128)(2,1)S(1)} %copy.22), channel_id=2, replica_groups=mesh['dp'=32,'section'=4,'mp'=4] {'mp'}, dimensions={2}, use_global_device_ids=true | all-gather | bytes 30720 | tf_op jit(solution)/shard_map/all_gather | solution.py:77
  18.1 10.8 %all-gather.3 = bf16[1,12,1024]{2,1,0:T(8,128)(2,1)S(1)} all-gather(bf16[1,12,256]{2,1,0:T(8,128)(2,1)S(1)} %copy.23), channel_id=5, replica_groups=mesh['dp'=32,'section'=4,'mp'=4] {'mp'}, dimensions={2}, use_global_device_ids=true | all-gather | bytes 30720 | tf_op jit(solution)/shard_map/all_gather | solution.py:77
  28.9 8.1 %all-gather.4 = bf16[1,12,1024]{2,0,1:T(2,128)(2,1)S(1)} all-gather(bf16[1,12,256]{2,0,1:T(2,128)(2,1)S(1)} %get-tuple-element.170), channel_id=6, replica_groups=mesh['dp'=32,'section'=4,'mp'=4] {'mp'}, dimensions={2}, use_global_device_ids=true | all-gather | bytes 30720 | tf_op jit(solution)/shard_map/all_gather | solution.py:78
  37.0 8.3 %all-gather.1 = bf16[1,12,1024]{2,0,1:T(2,128)(2,1)S(1)} all-gather(bf16[1,12,256]{2,0,1:T(2,128)(2,1)S(1)} %get-tuple-element.171), channel_id=3, replica_groups=mesh['dp'=32,'section'=4,'mp'=4] {'mp'}, dimensions={2}, use_global_device_ids=true | all-gather | bytes 30720 | tf_op jit(solution)/shard_map/all_gather | solution.py:78
  45.3 53.7 %all-gather.2 = bf16[1,384,1024]{2,0,1:T(2,128)(2,1)S(1)} all-gather(bf16[1,12,1024]{2,0,1:T(2,128)(2,1)S(1)} %all-gather.1), channel_id=4, replica_groups=mesh['dp'=32,'section'=4,'mp'=4] {'dp'}, dimensions={1}, use_global_device_ids=true | all-gather | bytes 811008 | tf_op jit(solution)/shard_map/all_gather | solution.py:79
  99.0 34.9 %all-gather.5 = bf16[1,384,1024]{2,0,1:T(2,128)(2,1)S(1)} all-gather(bf16[1,12,1024]{2,0,1:T(2,128)(2,1)S(1)} %all-gather.4), channel_id=7, replica_groups=mesh['dp'=32,'section'=4,'mp'=4] {'dp'}, dimensions={1}, use_global_device_ids=true | all-gather | bytes 811008 | tf_op jit(solution)/shard_map/all_gather | solution.py:79
  136.4 54.8 %fusion.252 = (bf16[16,256]{1,0:T(8,128)(2,1)S(1)}, bf16[16,256]{1,0:T(8,128)(2,1)S(1)}) fusion(bf16[384,256]{1,0:T(8,128)(2,1)S(1)} %fusion.17, bf16[384,256]{1,0:T(8,128)(2,1)S(1)} %fusion.16), kind=kCustom, calls=%all-reduce-scatter.2 | all-reduce-scatter fusion | flops 262145 | bytes 411648
  192.6 4.9 collective-permute-start.17
  197.4 3.5 collective-permute-start.16
  200.9 6.4 %collective-permute-start.11 = (bf16[12,256]{1,0:T(8,128)(2,1)S(1)}, bf16[12,256]{1,0:T(8,128)(2,1)S(1)}, u32[]{:S(2)}, u32[]{:S(2)}) collective-permute-start(bf16[12,256]{1,0:T(8,128)(2,1)S(1)} %slice.902), channel_id=1, source_target_pairs={{0,128},{16,144},{32,160},{48,176},{64,192},{80,208},{96,224},{112... | collective-permute-start | bytes 18440
  218.5 13.1 %all-reduce.19 = (f32[12,16]{1,0:T(8,128)S(1)}, f32[12,16]{1,0:T(8,128)S(1)}) all-reduce(f32[12,16]{1,0:T(8,128)S(1)} %get-tuple-element.102, f32[12,16]{1,0:T(8,128)S(1)} %fusion.20), channel_id=1, replica_groups=mesh['dp'=32,'section'=4,'mp'=4] {'mp'}, use_global_device_ids=true, to_apply=%region_7.8 | all-reduce | flops 384 | bytes 3072 | tf_op jit(solution)/shard_map/psum | solution.py:150
  233.1 4.6 multiply_reduce_fusion.60
  237.7 4.6 multiply_reduce_fusion.67
  242.3 14.8 %all-reduce.18 = (f32[12,16]{1,0:T(8,128)S(1)}, f32[12,16]{1,0:T(8,128)S(1)}, f32[12,16]{1,0:T(8,128)S(1)}, f32[12,16]{1,0:T(8,128)S(1)}) all-reduce(f32[12,16]{1,0:T(8,128)S(1)} %get-tuple-element.83, f32[12,16]{1,0:T(8,128)S(1)} %get-tuple-element.96, ...), channel_id=1, replica_groups=mesh['dp'=32,'section'=4,'mp'=4] {'mp'}, use_global_device_ids=true, to_apply=%region_11.12 | all-reduce | flops 768 | bytes 6144 | tf_op jit(solution)/shard_map/psum | solution.py:64
  259.9 3.7 collective-permute-start.15
  263.6 10.0 %collective-permute-start.14 = (bf16[16,256]{1,0:T(8,128)(2,1)S(1)}, bf16[16,256]{1,0:T(8,128)(2,1)S(1)}, u32[]{:S(2)}, u32[]{:S(2)}) collective-permute-start(bf16[16,256]{1,0:T(8,128)(2,1)S(1)} %get-tuple-element.143), channel_id=1, source_target_pairs={{0,48},{16,64},{32,80},{48,96},{64,112},{80,128},{96,144},{112,160... | collective-permute-start | bytes 24584
  306.9 12.3 %concatenate.1 = bf16[140,256]{1,0:T(8,128)(2,1)} concatenate(bf16[12,256]{1,0:T(8,128)(2,1)} %copy-done.33, bf16[16,256]{1,0:T(8,128)(2,1)} %copy-done.30, bf16[16,256]{1,0:T(8,128)(2,1)} %copy-done.31, bf16[16,256]{1,0:T(8,128)(2,1)} %copy-done.32, bf16[16,256]{1,0:T(8,128)(2,1)} %copy-done.34, bf16[16,256]{1,0:T(8,128)(2,1)} %copy-done.35, bf16[16,256]{1,0:T(8,128)(2,1)} %copy-done.37, ...), dimensions={0} | concatenate | bytes 143360
  319.2 12.2 %concatenate = bf16[140,256]{1,0:T(8,128)(2,1)} concatenate(bf16[12,256]{1,0:T(8,128)(2,1)} %copy-done.29, bf16[16,256]{1,0:T(8,128)(2,1)} %copy-done.36, bf16[16,256]{1,0:T(8,128)(2,1)} %copy-done.38, bf16[16,256]{1,0:T(8,128)(2,1)} %copy-done.40, bf16[16,256]{1,0:T(8,128)(2,1)} %collective-permute-done.7, bf16[16,256]{1,0:T(8,128)(2,1)} %collective-permute-done.6, ...), dimensions={0} | concatenate | bytes 143360
  333.6 16.9 %multiply_reduce_fusion.45 = (f32[1280]{0:T(1024)}, f32[1280]{0:T(1024)}, f32[1280]{0:T(1024)}, f32[1280]{0:T(1024)}, f32[1280]{0:T(1024)}, /*index=5*/f32[1280]...) fusion(f32[12,16,1280]{2,1,0:T(8,128)} %fusion.36, ...), kind=kLoop, calls=%fused_computation.419 | loop fusion | flops 16448000 | bytes 2636801 | tf_op jit(solution)/shard_map/reduce_sum | solution.py:59
  350.5 4.3 multiply_reduce_fusion.52
  354.8 15.5 %all-reduce.17 = (f32[12,16]{1,0:T(8,128)}, f32[12,16]{1,0:T(8,128)}, f32[12,16]{1,0:T(8,128)}, f32[12,16]{1,0:T(8,128)}) all-reduce(f32[12,16]{1,0:T(8,128)} %get-tuple-element.85, f32[12,16]{1,0:T(8,128)} %get-tuple-element.95, f32[12,16]{1,0:T(8,128)} %get-tuple-element.104, ...), channel_id=1, replica_groups=mesh['dp'=32,'section'=4,'mp'=4] {'mp'}, use_global_device_ids=true, to_apply=%region_19.20 | all-reduce | flops 768 | bytes 6144 | tf_op jit(solution)/shard_map/psum | solution.py:64
  386.8 5.6 multiply_reduce_fusion.30
  392.3 4.3 multiply_reduce_fusion.37
  396.6 15.5 %all-reduce.16 = (f32[12,16]{1,0:T(8,128)}, f32[12,16]{1,0:T(8,128)}, f32[12,16]{1,0:T(8,128)}, f32[12,16]{1,0:T(8,128)}) all-reduce(f32[12,16]{1,0:T(8,128)} %get-tuple-element.87, f32[12,16]{1,0:T(8,128)} %get-tuple-element.94, f32[12,16]{1,0:T(8,128)} %get-tuple-element.105, ...), channel_id=1, replica_groups=mesh['dp'=32,'section'=4,'mp'=4] {'mp'}, use_global_device_ids=true, to_apply=%region_27.28 | all-reduce | flops 768 | bytes 6144 | tf_op jit(solution)/shard_map/psum | solution.py:64
  422.2 5.3 collective-permute-done.2
  427.5 5.6 multiply_reduce_fusion.15
  433.1 4.3 multiply_reduce_fusion.22
  437.4 14.5 %all-reduce.15 = (f32[12,16]{1,0:T(8,128)}, f32[12,16]{1,0:T(8,128)}, f32[12,16]{1,0:T(8,128)}, f32[12,16]{1,0:T(8,128)}) all-reduce(f32[12,16]{1,0:T(8,128)} %get-tuple-element.89, f32[12,16]{1,0:T(8,128)} %get-tuple-element.93, f32[12,16]{1,0:T(8,128)S(1)} %copy-done.25, ...), channel_id=1, replica_groups=mesh['dp'=32,'section'=4,'mp'=4] {'mp'}, use_global_device_ids=true, to_apply=%region_35.36 | all-reduce | flops 768 | bytes 6144 | tf_op jit(solution)/shard_map/psum | solution.py:64
  466.1 4.0 multiply_reduce_fusion
  475.0 3.7 multiply_reduce_fusion.7
  478.6 14.9 %all-reduce.14 = (f32[12,16]{1,0:T(8,128)S(1)}, f32[12,16]{1,0:T(8,128)S(1)}) all-reduce(f32[12,16]{1,0:T(8,128)S(1)} %get-tuple-element.91, f32[12,16]{1,0:T(8,128)S(1)} %get-tuple-element.92), channel_id=1, replica_groups=mesh['dp'=32,'section'=4,'mp'=4] {'mp'}, use_global_device_ids=true, to_apply=%region_43.44 | all-reduce | flops 384 | bytes 3072 | tf_op jit(solution)/shard_map/psum | solution.py:64
  495.5 119.0 %psum.167 = bf16[1,15,1280]{2,0,1:T(2,128)(2,1)S(1)} all-reduce(bf16[1,15,1280]{2,0,1:T(2,128)(2,1)S(1)} %broadcast_in_dim.121), channel_id=1, replica_groups=mesh['dp'=32,'section'=4,'mp'=4] {'dp'}, use_global_device_ids=true, to_apply=%region_119.120 | all-reduce | flops 19200 | bytes 76800 | tf_op jit(solution)/shard_map/psum | solution.py:167
  (269 shorter events, 107.2 us)
Async XLA Ops:
  0.6 208.7 %copy-start = (bf16[1280,1024]{1,0:T(8,128)(2,1)S(1)}, bf16[1280,1024]{1,0:T(8,128)(2,1)}, u32[]{:S(2)}) copy-start(bf16[1280,1024]{1,0:T(8,128)(2,1)} %param.11) | copy-start | bytes 7864324
  99.0 36.5 %copy-start.9 = (bf16[1,384,1024]{2,0,1:T(2,128)(2,1)}, bf16[1,384,1024]{2,0,1:T(2,128)(2,1)S(1)}, u32[]{:S(2)}) copy-start(bf16[1,384,1024]{2,0,1:T(2,128)(2,1)S(1)} %all-gather.2) | copy-start | bytes 2359300
  191.3 82.4 %collective-permute-start.18 = (bf16[16,256]{1,0:T(8,128)(2,1)S(1)}, bf16[16,256]{1,0:T(8,128)(2,1)S(1)}, u32[]{:S(2)}, u32[]{:S(2)}) collective-permute-start(bf16[16,256]{1,0:T(8,128)(2,1)S(1)} %get-tuple-element.143), channel_id=1, source_target_pairs={{0,112},{16,128},{32,144},{48,160},{64,176},{80,192},{96,208},{112... | collective-permute-start | bytes 24584
  192.6 83.3 %collective-permute-start.17 = (bf16[16,256]{1,0:T(8,128)(2,1)S(1)}, bf16[16,256]{1,0:T(8,128)(2,1)S(1)}, u32[]{:S(2)}, u32[]{:S(2)}) collective-permute-start(bf16[16,256]{1,0:T(8,128)(2,1)S(1)} %get-tuple-element.143), channel_id=1, source_target_pairs={{0,96},{16,112},{32,128},{48,144},{64,160},{80,176},{96,192},{112,... | collective-permute-start | bytes 24584
  197.4 80.7 %collective-permute-start.16 = (bf16[16,256]{1,0:T(8,128)(2,1)S(1)}, bf16[16,256]{1,0:T(8,128)(2,1)S(1)}, u32[]{:S(2)}, u32[]{:S(2)}) collective-permute-start(bf16[16,256]{1,0:T(8,128)(2,1)S(1)} %get-tuple-element.143), channel_id=1, source_target_pairs={{0,80},{16,96},{32,112},{48,128},{64,144},{80,160},{96,176},{112,1... | collective-permute-start | bytes 24584
  200.9 58.9 %collective-permute-start.11 = (bf16[12,256]{1,0:T(8,128)(2,1)S(1)}, bf16[12,256]{1,0:T(8,128)(2,1)S(1)}, u32[]{:S(2)}, u32[]{:S(2)}) collective-permute-start(bf16[12,256]{1,0:T(8,128)(2,1)S(1)} %slice.902), channel_id=1, source_target_pairs={{0,128},{16,144},{32,160},{48,176},{64,192},{80,208},{96,224},{112... | collective-permute-start | bytes 18440
  207.3 56.3 %collective-permute-start.19 = (bf16[12,256]{1,0:T(8,128)(2,1)S(1)}, bf16[12,256]{1,0:T(8,128)(2,1)S(1)}, u32[]{:S(2)}, u32[]{:S(2)}) collective-permute-start(bf16[12,256]{1,0:T(8,128)(2,1)S(1)} %slice.903), channel_id=1, source_target_pairs={{0,128},{16,144},{32,160},{48,176},{64,192},{80,208},{96,224},{112... | collective-permute-start | bytes 18440
  257.1 26.8 %copy-start.2 = (bf16[1,2,12,16,1280]{4,3,2,1,0:T(8,128)(2,1)S(1)}, bf16[1,2,12,16,1280]{4,3,2,1,0:T(8,128)(2,1)}, u32[]{:S(2)}) copy-start(bf16[1,2,12,16,1280]{4,3,2,1,0:T(8,128)(2,1)} %param.8) | copy-start | bytes 2949124
  259.9 36.1 %copy-start.7 = (bf16[2,12,16,1280]{3,2,1,0:T(8,128)(2,1)}, bf16[2,12,16,1280]{3,2,1,0:T(8,128)(2,1)S(1)}, u32[]{:S(2)}) copy-start(bf16[2,12,16,1280]{3,2,1,0:T(8,128)(2,1)S(1)} %get-tuple-element.160) | copy-start | bytes 2949124
  259.9 36.0 %copy-start.29 = (bf16[12,256]{1,0:T(8,128)(2,1)}, bf16[12,256]{1,0:T(8,128)(2,1)S(1)}, u32[]{:S(2)}) copy-start(bf16[12,256]{1,0:T(8,128)(2,1)S(1)} %collective-permute-done.11) | copy-start | bytes 18436
  259.9 20.0 %collective-permute-start.15 = (bf16[16,256]{1,0:T(8,128)(2,1)S(1)}, bf16[16,256]{1,0:T(8,128)(2,1)S(1)}, u32[]{:S(2)}, u32[]{:S(2)}) collective-permute-start(bf16[16,256]{1,0:T(8,128)(2,1)S(1)} %get-tuple-element.143), channel_id=1, source_target_pairs={{0,64},{16,80},{32,96},{48,112},{64,128},{80,144},{96,160},{112,17... | collective-permute-start | bytes 24584
  263.6 32.2 %copy-start.33 = (bf16[12,256]{1,0:T(8,128)(2,1)}, bf16[12,256]{1,0:T(8,128)(2,1)S(1)}, u32[]{:S(2)}) copy-start(bf16[12,256]{1,0:T(8,128)(2,1)S(1)} %collective-permute-done.19) | copy-start | bytes 18436
  263.6 18.1 %collective-permute-start.14 = (bf16[16,256]{1,0:T(8,128)(2,1)S(1)}, bf16[16,256]{1,0:T(8,128)(2,1)S(1)}, u32[]{:S(2)}, u32[]{:S(2)}) collective-permute-start(bf16[16,256]{1,0:T(8,128)(2,1)S(1)} %get-tuple-element.143), channel_id=1, source_target_pairs={{0,48},{16,64},{32,80},{48,96},{64,112},{80,128},{96,144},{112,160... | collective-permute-start | bytes 24584
  273.7 22.2 %copy-start.30 = (bf16[16,256]{1,0:T(8,128)(2,1)}, bf16[16,256]{1,0:T(8,128)(2,1)S(1)}, u32[]{:S(2)}) copy-start(bf16[16,256]{1,0:T(8,128)(2,1)S(1)} %collective-permute-done.18) | copy-start | bytes 24580
  273.7 11.6 %collective-permute-start.13 = (bf16[16,256]{1,0:T(8,128)(2,1)S(1)}, bf16[16,256]{1,0:T(8,128)(2,1)S(1)}, u32[]{:S(2)}, u32[]{:S(2)}) collective-permute-start(bf16[16,256]{1,0:T(8,128)(2,1)S(1)} %get-tuple-element.143), channel_id=1, source_target_pairs={{0,32},{16,48},{32,64},{48,80},{64,96},{80,112},{96,128},{112,144}... | collective-permute-start | bytes 24584
  275.9 20.0 %copy-start.31 = (bf16[16,256]{1,0:T(8,128)(2,1)}, bf16[16,256]{1,0:T(8,128)(2,1)S(1)}, u32[]{:S(2)}) copy-start(bf16[16,256]{1,0:T(8,128)(2,1)S(1)} %collective-permute-done.17) | copy-start | bytes 24580
  275.9 11.9 %collective-permute-start.12 = (bf16[16,256]{1,0:T(8,128)(2,1)S(1)}, bf16[16,256]{1,0:T(8,128)(2,1)S(1)}, u32[]{:S(2)}, u32[]{:S(2)}) collective-permute-start(bf16[16,256]{1,0:T(8,128)(2,1)S(1)} %get-tuple-element.143), channel_id=1, source_target_pairs={{0,16},{16,32},{32,48},{48,64},{64,80},{80,96},{96,112},{112,128},... | collective-permute-start | bytes 24584
  278.1 12.0 %collective-permute-start.10 = (bf16[16,256]{1,0:T(8,128)(2,1)S(1)}, bf16[16,256]{1,0:T(8,128)(2,1)S(1)}, u32[]{:S(2)}, u32[]{:S(2)}) collective-permute-start(bf16[16,256]{1,0:T(8,128)(2,1)S(1)} %get-tuple-element.144), channel_id=1, source_target_pairs={{0,112},{16,128},{32,144},{48,160},{64,176},{80,192},{96,208},{112... | collective-permute-start | bytes 24584
  279.9 12.3 %collective-permute-start.9 = (bf16[16,256]{1,0:T(8,128)(2,1)S(1)}, bf16[16,256]{1,0:T(8,128)(2,1)S(1)}, u32[]{:S(2)}, u32[]{:S(2)}) collective-permute-start(bf16[16,256]{1,0:T(8,128)(2,1)S(1)} %get-tuple-element.144), channel_id=1, source_target_pairs={{0,96},{16,112},{32,128},{48,144},{64,160},{80,176},{96,192},{112,... | collective-permute-start | bytes 24584
  281.7 12.6 %collective-permute-start.8 = (bf16[16,256]{1,0:T(8,128)(2,1)S(1)}, bf16[16,256]{1,0:T(8,128)(2,1)S(1)}, u32[]{:S(2)}, u32[]{:S(2)}) collective-permute-start(bf16[16,256]{1,0:T(8,128)(2,1)S(1)} %get-tuple-element.144), channel_id=1, source_target_pairs={{0,80},{16,96},{32,112},{48,128},{64,144},{80,160},{96,176},{112,1... | collective-permute-start | bytes 24584
  285.2 34.0 %collective-permute-start.7 = (bf16[16,256]{1,0:T(8,128)(2,1)S(1)}, bf16[16,256]{1,0:T(8,128)(2,1)}, u32[]{:S(2)}, u32[]{:S(2)}) collective-permute-start(bf16[16,256]{1,0:T(8,128)(2,1)S(1)} %get-tuple-element.144), channel_id=1, source_target_pairs={{0,64},{16,80},{32,96},{48,112},{64,128},{80,144},{96,160},{112,17... | collective-permute-start | bytes 24584
  287.7 31.5 %collective-permute-start.6 = (bf16[16,256]{1,0:T(8,128)(2,1)S(1)}, bf16[16,256]{1,0:T(8,128)(2,1)}, u32[]{:S(2)}, u32[]{:S(2)}) collective-permute-start(bf16[16,256]{1,0:T(8,128)(2,1)S(1)} %get-tuple-element.144), channel_id=1, source_target_pairs={{0,48},{16,64},{32,80},{48,96},{64,112},{80,128},{96,144},{112,160... | collective-permute-start | bytes 24584
  290.1 29.1 %collective-permute-start.5 = (bf16[16,256]{1,0:T(8,128)(2,1)S(1)}, bf16[16,256]{1,0:T(8,128)(2,1)}, u32[]{:S(2)}, u32[]{:S(2)}) collective-permute-start(bf16[16,256]{1,0:T(8,128)(2,1)S(1)} %get-tuple-element.144), channel_id=1, source_target_pairs={{0,32},{16,48},{32,64},{48,80},{64,96},{80,112},{96,128},{112,144}... | collective-permute-start | bytes 24584
  292.2 27.0 %collective-permute-start.4 = (bf16[16,256]{1,0:T(8,128)(2,1)S(1)}, bf16[16,256]{1,0:T(8,128)(2,1)}, u32[]{:S(2)}, u32[]{:S(2)}) collective-permute-start(bf16[16,256]{1,0:T(8,128)(2,1)S(1)} %get-tuple-element.144), channel_id=1, source_target_pairs={{0,16},{16,32},{32,48},{48,64},{64,80},{80,96},{96,112},{112,128},... | collective-permute-start | bytes 24584
  294.3 39.3 %collective-permute-start = (bf16[12,16,1280]{2,1,0:T(8,128)(2,1)}, bf16[12,16,1280]{2,1,0:T(8,128)(2,1)}, u32[]{:S(2)}, u32[]{:S(2)}) collective-permute-start(bf16[12,16,1280]{2,1,0:T(8,128)(2,1)} %get-tuple-element.161), channel_id=1, source_target_pairs={{4,0},{8,4},{12,8},{5,1},{9,5},{13,9},{6,2},{10,6},{14,10},{7,3},{... | collective-permute-start | bytes 1474568 | tf_op jit(solution)/shard_map/ppermute | solution.py:19
  331.5 19.1 %copy-start.3 = (bf16[1,2,12,16,1280]{4,3,2,1,0:T(8,128)(2,1)S(1)}, bf16[1,2,12,16,1280]{4,3,2,1,0:T(8,128)(2,1)}, u32[]{:S(2)}) copy-start(bf16[1,2,12,16,1280]{4,3,2,1,0:T(8,128)(2,1)} %param.8) | copy-start | bytes 2949124
  375.9 10.8 %collective-permute-start.1 = (bf16[12,16,1280]{2,1,0:T(8,128)(2,1)}, bf16[12,16,1280]{2,1,0:T(8,128)(2,1)}, u32[]{:S(2)}, u32[]{:S(2)}) collective-permute-start(bf16[12,16,1280]{2,1,0:T(8,128)(2,1)} %get-tuple-element.158), channel_id=1, source_target_pairs={{4,0},{8,4},{12,8},{5,1},{9,5},{13,9},{6,2},{10,6},{14,10},{7,3},{... | collective-permute-start | bytes 1474568 | tf_op jit(solution)/shard_map/ppermute | solution.py:19
  417.6 9.9 %collective-permute-start.2 = (bf16[12,16,1280]{2,1,0:T(8,128)(2,1)}, bf16[12,16,1280]{2,1,0:T(8,128)(2,1)}, u32[]{:S(2)}, u32[]{:S(2)}) collective-permute-start(bf16[12,16,1280]{2,1,0:T(8,128)(2,1)} %get-tuple-element.155), channel_id=1, source_target_pairs={{4,0},{8,4},{12,8},{5,1},{9,5},{13,9},{6,2},{10,6},{14,10},{7,3},{... | collective-permute-start | bytes 1474568 | tf_op jit(solution)/shard_map/ppermute | solution.py:19
  456.4 9.8 %collective-permute-start.3 = (bf16[12,16,1280]{2,1,0:T(8,128)(2,1)}, bf16[12,16,1280]{2,1,0:T(8,128)(2,1)S(1)}, u32[]{:S(2)}, u32[]{:S(2)}) collective-permute-start(bf16[12,16,1280]{2,1,0:T(8,128)(2,1)} %get-tuple-element.152), channel_id=1, source_target_pairs={{4,0},{8,4},{12,8},{5,1},{9,5},{13,9},{6,2},{10,6},{14,10},{7,3},{... | collective-permute-start | bytes 1474568 | tf_op jit(solution)/shard_map/ppermute | solution.py:19
  470.1 24.4 %copy-start.10 = (f32[15,1280]{1,0:T(8,128)S(1)}, f32[15,1280]{1,0:T(8,128)}, u32[]{:S(2)}) copy-start(f32[15,1280]{1,0:T(8,128)} %stack.297) | copy-start | bytes 230404
  472.6 21.0 %copy-start.27 = (f32[1,1280]{1,0:T(1,128)S(1)}, f32[1,1280]{1,0:T(1,128)}, u32[]{:S(2)}) copy-start(f32[1,1280]{1,0:T(1,128)} %stack.338) | copy-start | bytes 15364
  473.2 20.4 %copy-start.28 = (f32[1,1280]{1,0:T(1,128)S(1)}, f32[1,1280]{1,0:T(1,128)}, u32[]{:S(2)}) copy-start(f32[1,1280]{1,0:T(1,128)} %stack.336) | copy-start | bytes 15364
  (36 other events, 243.9 us)
where the time goes:
time: 625 us; the launch traced here: 618 us
  blocking collectives  392 us (63%)
  other arithmetic  89.6 us (14%)
  local copies, waits for them, and re-layouts  60.6 us (10%)
  starting transfers between devices  56.5 us (9%)
  waiting for transfers between devices  10.1 us (2%)
  matrix products  6.43 us (1%)
    psum x1, blocking collectives, per_device(): lax.psum(tap_total.astype(jnp.bfloat16), 'dp').astype(jnp.float32)  119 us
    all_gather x2, blocking collectives, pair_loss_grads(): all_keys = lax.all_gather(key_full, 'dp', axis=0, tiled=True)  88.6 us
    psum x5, blocking collectives, section_step(): lax.psum((jnp.sum(grad_normed, axis=-1), jnp.sum(grad_normed * normed, ax...  75.3 us
    reduce_sum x10, other arithmetic, section_step(): jnp.sum(grad_conv * padded[:, offset:offset + frame_count, :], axis=(0, 1))  57.7 us
    unnamed x1, blocking collectives  54.8 us
    unnamed x16, starting transfers between devices  50.9 us
    unnamed x105, local copies, waits for them, and re-layouts  29.4 us
    all_gather x2, blocking collectives, pair_loss_grads(): query_full = lax.all_gather(queries_now, 'mp', axis=1, tiled=True)  25 us
  transfers between devices with their start and end apart: 20, of which 3 were waited for; matrix products, arithmetic and copies ran while one was open for 12% of the time, Pallas kernels for 0%

commit v1 on v0

v1 whole, which is shorter than its diff:
```python
import functools

import jax
import jax.numpy as jnp
from jax import lax
from jax.experimental import pallas as pl
from jax.experimental.pallas import tpu as pltpu
from jax.sharding import PartitionSpec as P

D = 5120
EMB = 1024
FRAMES = 16
KERNEL = 15
HALF = KERNEL // 2
SECTIONS = 4
MP = 4
DP = 32
MICRO = 2
SHARD = 12
OWN = SHARD // SECTIONS
CLIPS = MICRO * OWN
ROWS = CLIPS * FRAMES
TEXTS = DP * MICRO * SHARD
WIDE = D // MP
SLICE = EMB // MP
LANES = 128
BLOCKS = WIDE // LANES
PAD = 8
SCORE_SCALE = 1.0 / 32.0
EPSILON = 1e-05
F32 = jnp.float32
BF16 = jnp.bfloat16

NT = (((1,), (1,)), ((), ()))
VMEM = pl.BlockSpec(memory_space=pltpu.VMEM)
PARAMS = pltpu.CompilerParams(vmem_limit_bytes=40 * 1024 * 1024)


def lane_sums(partial):
    ones = jnp.ones((PAD, LANES), F32)
    return lax.dot_general(
        ones, partial, NT, preferred_element_type=F32, precision=lax.Precision.HIGHEST
    )


def lanes_of(block):
    return pl.ds(pl.multiple_of(block * LANES, LANES), LANES)


def wide_rows(row):
    turned = jnp.concatenate([row, jnp.zeros((PAD - 1, LANES), F32)], 0).T
    return jnp.broadcast_to(turned[:, 0:1], (LANES, LANES))


def sums_kernel(x0, x1, x2, x3, texts, query, out):
    rows = []
    for x in (x0, x1, x2, x3):
        total = jnp.zeros((ROWS, LANES), F32)
        square = jnp.zeros((ROWS, LANES), F32)
        for block in range(BLOCKS):
            value = x[0:ROWS, block * LANES : (block + 1) * LANES].astype(F32)
            total = total + value
            square = square + value * value
        rows.append(lane_sums(total)[0:1])
        rows.append(lane_sums(square)[0:1])
    stats = jnp.concatenate(rows, 0)
    stats = jnp.concatenate([stats, jnp.zeros((PAD, LANES - ROWS), F32)], 1)
    scores = lax.dot_general(
        query[...], texts[:, 0:SLICE], NT, preferred_element_type=F32
    )[0:PAD]
    for peer in range(MP):
        out[peer, :, 0:TEXTS] = scores
        out[peer, :, TEXTS:] = stats


def softmax_kernel(parts, texts, valid, positive, weight, query_grad, pair_grad):
    scores = parts[0, :, 0:TEXTS]
    for peer in range(1, MP):
        scores = scores + parts[peer, :, 0:TEXTS]
    scores = jnp.where(valid[...] > 0.0, scores * SCORE_SCALE, -1e30)
    exp_scores = jnp.exp(scores - jnp.max(scores, axis=1, keepdims=True))
    probs = exp_scores / jnp.sum(exp_scores, axis=1, keepdims=True)
    column = lax.broadcasted_iota(jnp.int32, (PAD, TEXTS), 1)
    hot = jnp.where(column == positive[:, 0:1], 1.0, 0.0)
    grad = weight[:, 0:1] * (probs - hot)
    grad = jnp.concatenate([grad, jnp.zeros((PAD, TEXTS), F32)], 0).astype(BF16)
    pair_grad[...] = grad
    result = jnp.dot(grad, texts[:, 0:SLICE], preferred_element_type=F32) * SCORE_SCALE
    result = result.astype(BF16)
    for peer in range(MP):
        query_grad[peer] = result


def forward_kernel(
    parts, x0, x1, x2, x3, normed_out, gate_out, inv_out, taps_out, natural, mean_rows, inv_rows
):
    stats = parts[0, :, TEXTS:]
    for peer in range(1, MP):
        stats = stats + parts[peer, :, TEXTS:]
    natural[...] = jnp.zeros_like(natural)
    for hop, x in enumerate((x0, x1, x2, x3)):
        mean = stats[2 * hop : 2 * hop + 1] / D
        variance = stats[2 * hop + 1 : 2 * hop + 2] / D - mean * mean
        mean_rows[...] = wide_rows(mean)
        inv_rows[...] = wide_rows(lax.rsqrt(variance + EPSILON))
        for f in range(FRAMES):
            inv_out[hop, f] = inv_rows[pl.ds(f, PAD, stride=FRAMES), :]

        def block_step(block, carry, hop=hop, x=x):
            lanes = lanes_of(block)
            value = x[0:ROWS, lanes].astype(F32)
            natural[0:ROWS, :] = (value - mean_rows[0:ROWS, :]) * inv_rows[0:ROWS, :]
            weights = x[ROWS : ROWS + 16, lanes].astype(F32)
            taps_out[hop, :, lanes] = weights
            taps = [
                jnp.broadcast_to(weights[k : k + 1], (PAD, LANES)) for k in range(KERNEL + 1)
            ]
            hidden = []
            for f in range(FRAMES):
                normed = natural[pl.ds(f, PAD, stride=FRAMES), :]
                normed_out[hop, block, f] = normed
                hidden.append(normed * taps[KERNEL])
            for f in range(FRAMES):
                conv = None
                for k in range(KERNEL):
                    if 0 <= f + k - HALF < FRAMES:
                        term = taps[k] * hidden[f + k - HALF]
                        conv = term if conv is None else conv + term
                gate = jax.nn.sigmoid(conv)
                gate_out[hop, block, f] = gate * (1.0 + conv * (1.0 - gate))
            return carry

        lax.fori_loop(0, BLOCKS, block_step, 0)


def back_block(upstream, block, normed, gate, taps_in, grad_out, tap_out, first, second):
    lanes = lanes_of(block)
    weights = taps_in[0, :, lanes]
    taps = [jnp.broadcast_to(weights[k : k + 1], (PAD, LANES)) for k in range(KERNEL + 1)]
    gain = taps[KERNEL]
    grad_conv = [upstream[f] * gate[0, block, f] for f in range(FRAMES)]
    for f in range(FRAMES):
        conv = None
        for k in range(KERNEL):
            if 0 <= f - k + HALF < FRAMES:
                term = taps[k] * grad_conv[f - k + HALF]
                conv = term if conv is None else conv + term
        conv = conv * gain
        grad_out[block, f] = conv
        first[f] += conv
        second[f] += conv * normed[0, block, f]
    hidden = [normed[0, block, f] * gain for f in range(FRAMES)]
    for k in range(KERNEL):
        total = None
        for f in range(FRAMES):
            if 0 <= f + k - HALF < FRAMES:
                term = grad_conv[f] * hidden[f + k - HALF]
                total = term if total is None else total + term
        tap_out[k : k + 1, lanes] = jnp.sum(total, axis=0, keepdims=True)
    tap_out[KERNEL : KERNEL + 1, lanes] = jnp.zeros((1, LANES), F32)


def write_sums(first, second, sums_out):
    row = lax.broadcasted_iota(jnp.int32, (PAD, LANES), 0)
    sums = jnp.where(
        row == 0,
        lane_sums(first[...].reshape(LANES, LANES)),
        lane_sums(second[...].reshape(LANES, LANES)),
    )
    for peer in range(MP):
        sums_out[peer] = sums


def head_kernel(
    hops, query_grad, weight, normed, gate, taps_in, up_out, grad_out, tap_out, sums_out, first, second
):
    first[...] = jnp.zeros_like(first)
    second[...] = jnp.zeros_like(second)

    def block_step(block, carry):
        rows = weight[pl.ds(pl.multiple_of(block * LANES, LANES), LANES), :]
        pooled = None
        for peer in range(MP):
            term = lax.dot_general(
                query_grad[peer],
                rows[:, peer * SLICE : (peer + 1) * SLICE],
                NT,
                preferred_element_type=F32,
            )
            pooled = term if pooled is None else pooled + term
        head = (pooled[0:PAD] / FRAMES).astype(BF16).astype(F32)
        for f in range(FRAMES):
            up_out[block, f] = head
        back_block(
            [head] * FRAMES, block, normed, gate, taps_in, grad_out, tap_out, first, second
        )
        return carry

    lax.fori_loop(0, BLOCKS, block_step, 0)
    write_sums(first, second, sums_out)


def read_sums(parts, inv, first_rows, second_rows):
    sums = parts[0]
    for peer in range(1, MP):
        sums = sums + parts[peer]
    sums = sums / D
    first_rows[...] = inv[0] * wide_rows(sums[0:1]).reshape(FRAMES, PAD, LANES)
    second_rows[...] = inv[0] * wide_rows(sums[1:2]).reshape(FRAMES, PAD, LANES)


def corrected(block, up, grad, normed, inv, first_rows, second_rows, natural, result):
    values = []
    for f in range(FRAMES):
        value = (
            up[block, f]
            + inv[0, f] * grad[block, f]
            - first_rows[f]
            - normed[0, block, f] * second_rows[f]
        )
        natural[pl.ds(f, PAD, stride=FRAMES), :] = value
        values.append(value)
    result[:, lanes_of(block)] = natural[0:ROWS, :].astype(BF16)
    return values


def step_kernel(
    hops, parts, up, grad, normed_before, inv_before, normed, gate, taps_in,
    result, up_out, grad_out, tap_out, sums_out,
    first, second, first_rows, second_rows, natural,
):
    first[...] = jnp.zeros_like(first)
    second[...] = jnp.zeros_like(second)
    read_sums(parts, inv_before, first_rows, second_rows)

    def block_step(block, carry):
        values = corrected(
            block, up, grad, normed_before, inv_before, first_rows, second_rows, natural, result
        )
        for f in range(FRAMES):
            up_out[block, f] = values[f]
        back_block(values, block, normed, gate, taps_in, grad_out, tap_out, first, second)
        return carry

    lax.fori_loop(0, BLOCKS, block_step, 0)
    write_sums(first, second, sums_out)


def last_kernel(
    hops, parts, up, grad, normed_before, inv_before, result, first_rows, second_rows, natural
):
    read_sums(parts, inv_before, first_rows, second_rows)

    def block_step(block, carry):
        corrected(
            block, up, grad, normed_before, inv_before, first_rows, second_rows, natural, result
        )
        return carry

    lax.fori_loop(0, BLOCKS, block_step, 0)


FRAME_MAJOR = (BLOCKS, FRAMES, PAD, LANES)
ROW_TILE = pltpu.VMEM((FRAMES, PAD, LANES), F32)
NATURAL = pltpu.VMEM((LANES, LANES), F32)


def shape(dims, dtype=F32):
    return jax.ShapeDtypeStruct(dims, dtype)


def cost(flops, moved):
    return pl.CostEstimate(flops=flops, bytes_accessed=moved, transcendentals=0)


def whole(*dims):
    return pl.BlockSpec(dims, lambda i, hops: (0,) * len(dims))


def at_hop(section, *dims):
    return pl.BlockSpec(
        (1,) + dims, lambda i, hops: (hops[section],) + (0,) * len(dims)
    )


def section_call(kernel, hops, operands, in_specs, outs, scratch, name):
    return pl.pallas_call(
        kernel,
        out_shape=outs,
        grid_spec=pltpu.PrefetchScalarGridSpec(
            num_scalar_prefetch=1,
            grid=(1,),
            in_specs=in_specs,
            out_specs=[whole(*out.shape) for out in outs],
            scratch_shapes=scratch,
        ),
        compiler_params=PARAMS,
        name=name,
    )(hops, *operands)


def rotate(value, steps):
    pairs = [(source, (source + steps) % SECTIONS) for source in range(SECTIONS)]
    return lax.ppermute(value, "section", pairs)


def per_device(
    saved_inputs, norm_gains, conv_taps, head_weight, queries, key_embeds, positives, pair_weights
):
    section_now = lax.axis_index("section")
    hops = jnp.stack([(section_now - t) % SECTIONS for t in range(SECTIONS)]).astype(jnp.int32)
    inputs_all = saved_inputs[0]

    small = jnp.concatenate([conv_taps[0], norm_gains.astype(BF16)], 0)
    sections = []
    for steps in range(SECTIONS):
        target = (section_now + steps) % SECTIONS
        block = lax.dynamic_slice_in_dim(inputs_all, OWN * target, OWN, 1)
        block = jnp.concatenate([block.reshape(ROWS, WIDE), small], 0)
        sections.append(rotate(block, steps) if steps else block)

    pairs = jnp.concatenate([key_embeds, queries], -1).reshape(MICRO * SHARD, 2 * SLICE)
    pairs = jnp.broadcast_to(pairs[None], (DP,) + pairs.shape)
    texts = lax.all_to_all(pairs, "dp", 0, 0).reshape(TEXTS, 2 * SLICE)

    own_queries = lax.dynamic_slice_in_dim(queries, OWN * section_now, OWN, 1)
    own_queries = jnp.pad(own_queries.reshape(CLIPS, SLICE), ((0, 16 - CLIPS), (0, 0)))
    own_positives = lax.dynamic_slice_in_dim(positives, OWN * section_now, OWN, 1)
    own_weights = lax.dynamic_slice_in_dim(pair_weights, OWN * section_now, OWN, 1)
    micro = jnp.arange(MICRO, dtype=jnp.int32)[:, None]
    column = (own_positives // SHARD) * (MICRO * SHARD) + micro * SHARD + own_positives % SHARD
    column = jnp.pad(column.reshape(CLIPS), (0, PAD - CLIPS), constant_values=-1)
    column = jnp.broadcast_to(column[:, None], (PAD, LANES))
    own_weights = jnp.pad(own_weights.reshape(CLIPS), (0, PAD - CLIPS))
    own_weights = jnp.broadcast_to(own_weights[:, None], (PAD, LANES))
    text_micro = (jnp.arange(TEXTS) // SHARD) % MICRO
    clip_micro = jnp.minimum(jnp.arange(PAD) // OWN, MICRO - 1)
    valid = (clip_micro[:, None] == text_micro[None, :]).astype(F32)

    parts = pl.pallas_call(
        sums_kernel,
        out_shape=shape((MP, PAD, TEXTS + LANES)),
        in_specs=[VMEM] * 6,
        out_specs=VMEM,
        compiler_params=PARAMS,
        name="row_sums_and_scores",
    )(*sections, texts, own_queries)
    parts = lax.all_to_all(parts, "mp", 0, 0)

    query_grad, pair_grad = pl.pallas_call(
        softmax_kernel,
        out_shape=(shape((MP, 16, SLICE), BF16), shape((16, TEXTS), BF16)),
        in_specs=[VMEM] * 5,
        out_specs=(VMEM, VMEM),
        compiler_params=PARAMS,
        name="softmax_grads",
    )(parts, texts, valid, column, own_weights)
    query_grad = lax.all_to_all(query_grad, "mp", 0, 0)

    normed, gate, inv, taps = pl.pallas_call(
        forward_kernel,
        out_shape=(
            shape((SECTIONS,) + FRAME_MAJOR),
            shape((SECTIONS,) + FRAME_MAJOR),
            shape((SECTIONS, FRAMES, PAD, LANES)),
            shape((SECTIONS, 16, WIDE)),
        ),
        in_specs=[VMEM] * 5,
        out_specs=(VMEM,) * 4,
        scratch_shapes=[NATURAL] * 3,
        compiler_params=PARAMS,
        cost_estimate=cost(10**9, 6 * 10**6),
        name="sections_forward",
    )(parts, *sections)

    outs = [shape(FRAME_MAJOR), shape(FRAME_MAJOR), shape((16, WIDE)), shape((MP, PAD, LANES))]
    now = lambda t: [
        at_hop(t, *FRAME_MAJOR),
        at_hop(t, *FRAME_MAJOR),
        at_hop(t, 16, WIDE),
    ]
    before = lambda t: [
        whole(MP, PAD, LANES),
        whole(*FRAME_MAJOR),
        whole(*FRAME_MAJOR),
        at_hop(t, *FRAME_MAJOR),
        at_hop(t, FRAMES, PAD, LANES),
    ]
    tap_list = [None] * SECTIONS
    result_list = [None] * SECTIONS
    up, grad, tap_list[3], sums = section_call(
        head_kernel,
        hops,
        (query_grad, head_weight, normed, gate, taps),
        [whole(MP, 16, SLICE), whole(WIDE, EMB)] + now(3),
        outs,
        [ROW_TILE] * 2,
        "head_and_section",
    )
    for t in (2, 1, 0):
        sums = lax.all_to_all(sums, "mp", 0, 0)
        result_list[t + 1], up, grad, tap_list[t], sums = section_call(
            step_kernel,
            hops,
            (sums, up, grad, normed, inv, normed, gate, taps),
            before(t + 1) + now(t),
            [shape((ROWS, WIDE), BF16)] + outs,
            [ROW_TILE] * 4 + [NATURAL],
            "section_step",
        )

    tap_parts = jnp.stack(tap_list).astype(BF16).reshape(SECTIONS, DP, 5, LANES)
    tap_parts = tap_parts.transpose(1, 0, 2, 3)
    pair_parts = pair_grad[0:CLIPS].reshape(CLIPS, DP, MICRO * SHARD).transpose(1, 0, 2)
    pair_parts = jnp.pad(pair_parts.reshape(DP, -1), ((0, 0), (0, 2 * LANES - CLIPS * MICRO * SHARD)))
    pair_parts = jnp.broadcast_to(
        pair_parts.reshape(DP, 1, 2, LANES), (DP, SECTIONS, 2, LANES)
    )
    message = jnp.concatenate([tap_parts, pair_parts], 2).reshape(DP * SECTIONS, 7, LANES)
    message = jnp.pad(message, ((0, 0), (0, 1), (0, 0)))
    message = lax.all_to_all(message, ("dp", "section"), 0, 0)

    own = sums[0]
    shifted = [own]
    for steps in range(1, MP):
        shifted.append(
            lax.ppermute(own, "mp", [(source, (source + steps) % MP) for source in range(MP)])
        )
    sums = jnp.stack(shifted)
    (result_list[0],) = section_call(
        last_kernel,
        hops,
        (sums, up, grad, normed, inv),
        before(0),
        [shape((ROWS, WIDE), BF16)],
        [ROW_TILE] * 2 + [NATURAL],
        "section_end",
    )

    tap_sum = jnp.sum(message[:, 0:5].astype(F32), axis=0).astype(BF16)
    tap_grads = lax.all_to_all(jnp.broadcast_to(tap_sum[None], (DP, 5, LANES)), "dp", 0, 0)
    tap_grads = tap_grads.reshape(16, WIDE)[0:KERNEL].astype(F32)

    columns = message[:, 5:7].reshape(DP, SECTIONS, 2 * LANES)[..., : CLIPS * MICRO * SHARD]
    columns = columns.reshape(DP, SECTIONS, MICRO, OWN, MICRO * SHARD)
    columns = columns.transpose(0, 2, 1, 3, 4).reshape(TEXTS, MICRO * SHARD)
    key_grads = (
        lax.dot_general(
            columns, texts[:, SLICE:], (((0,), (0,)), ((), ())), preferred_element_type=F32
        )
        * SCORE_SCALE
    ).reshape(MICRO, SHARD, SLICE)

    stacked = jnp.stack(result_list)
    results = jnp.zeros(inputs_all.shape, BF16)
    for steps in range(SECTIONS):
        target = (section_now + steps) % SECTIONS
        source = (section_now - steps) % SECTIONS
        block = lax.dynamic_index_in_dim(stacked, target, 0, keepdims=False)
        block = rotate(block, steps) if steps else block
        block = block.reshape(MICRO, OWN, FRAMES, WIDE)
        results = lax.dynamic_update_slice_in_dim(results, block, OWN * source, 1)
    return (results[None], tap_grads[None], key_grads)


def solution(mesh):
    return jax.shard_map(
        per_device,
        mesh=mesh,
        in_specs=(
            P("section", None, "dp", None, "mp"),
            P("section", "mp"),
            P("section", None, "mp"),
            P("mp", None),
            P(None, "dp", "mp"),
            P(None, "dp", "mp"),
            P(None, "dp"),
            P(None, "dp"),
        ),
        out_specs=(
            P("section", None, "dp", None, "mp"),
            P("section", None, "mp"),
            P(None, "dp", "mp"),
        ),
        check_vma=False,
    )
```

time: 625 us -> 215 us (0.34)
  blocking collectives: 392 us -> 22 us
  other arithmetic: 89.6 us -> 5.77 us
  starting transfers between devices: 56.5 us -> 86.5 us
  waiting for transfers between devices: 10.1 us -> 34 us
  Pallas kernels: 0 us -> 22.1 us
  local copies, waits for them, and re-layouts: 60.6 us -> 40.8 us
    psum x7 -> x0, blocking collectives: 207 us -> none  [the longest x1 119 us: per_device(): lax.psum(tap_total.astype(jnp.bfloat16), 'dp').astype(jnp.float32)]
    all_gather x6 -> x0, blocking collectives: 130 us -> none  [the longest x2 88.6 us: pair_loss_grads(): all_keys = lax.all_gather(key_full, 'dp', axis=0, tiled=True)]
    reduce_sum x14 -> x1, other arithmetic: 62 us -> 0.14 us  [per_device(): tap_sum = jnp.sum(message[:, 0:5].astype(F32), axis=0).astype(BF16)]
    unnamed x1 -> x0, blocking collectives: 54.8 us -> none
    unnamed x16 -> x0, starting transfers between devices: 50.9 us -> none
    all_to_all x0 -> x6, starting transfers between devices: none -> 50.6 us  [the longest x1 16.5 us: per_device(): message = lax.all_to_all(message, ('dp', 'section'), 0, 0)]
    ppermute x4 -> x9, starting transfers between devices: 5.56 us -> 35.9 us  [the longest x6 21.3 us: rotate(): return lax.ppermute(value, 'section', pairs)]
    another operation x82 -> x4, local copies, waits for them, and re-layouts: 25.5 us -> 2.92 us  [per_device(): tap_parts = jnp.stack(tap_list).astype(BF16).reshape(SECTIONS, DP, 5, LANES)]
  transfers between devices with their start and end apart: 20 -> 15, of which waited for: 3 -> 7; matrix products, arithmetic and copies ran while one was open for 12% -> 7% of each run, Pallas kernels for 0% -> 2%
where the time goes in v1:
time: 215 us; the launch traced here: 213 us
  starting transfers between devices  86.5 us (40%)
  local copies, waits for them, and re-layouts  40.8 us (19%)
  waiting for transfers between devices  34 us (16%)
  Pallas kernels  22.1 us (10%)
  blocking collectives  22 us (10%)
  other arithmetic  5.77 us (3%)
    unnamed x84, local copies, waits for them, and re-layouts  27.1 us
    all_to_all x2, blocking collectives, per_device(): sums = lax.all_to_all(sums, 'mp', 0, 0)  22 us
    ppermute x6, starting transfers between devices, rotate(): return lax.ppermute(value, 'section', pairs)  21.3 us
    ppermute x6, waiting for transfers between devices, rotate(): return lax.ppermute(value, 'section', pairs)  17.8 us
    all_to_all x1, starting transfers between devices, per_device(): message = lax.all_to_all(message, ('dp', 'section'), 0, 0)  16.5 us
    pallas_call x5, Pallas kernels, section_call(): pl.pallas_call(kernel, out_shape=outs, grid_spec=pltpu.PrefetchScalarGrid...  15 us
    ppermute x3, starting transfers between devices, per_device(): lax.ppermute(own, 'mp', [(source, (source + steps) % MP) for source in ra...  14.6 us
    all_to_all x1, starting transfers between devices, per_device(): texts = lax.all_to_all(pairs, 'dp', 0, 0).reshape(TEXTS, 2 * SLICE)  13.1 us
  transfers between devices with their start and end apart: 15, of which 7 were waited for; matrix products, arithmetic and copies ran while one was open for 7% of the time, Pallas kernels for 2%

profile of v1, /device:TPU:1, one launch (start us, length us, event | category | flops | bytes accessed | tf_op | source)
XLA Modules:
  0.0 212.8 jit_solution(12672821950567556816)
XLA Ops:
  2.5 13.1 %all-to-all-start = ((bf16[32,24,512]{2,1,0:T(8,128)(2,1)}), bf16[32,24,512]{2,1,0:T(8,128)(2,1)S(1)}, u32[]{:S(2)}, u32[]{:S(2)}) async-start(bf16[32,24,512]{2,1,0:T(8,128)(2,1)} %broadcast_in_dim.50), calls=%async_computation | async-start | bytes 1572864 | tf_op jit(solution)/shard_map/all_to_all | solution.py:324
  15.9 3.1 %collective-permute-start = (bf16[112,1280]{1,0:T(8,128)(2,1)S(1)}, bf16[112,1280]{1,0:T(8,128)(2,1)S(1)}, u32[]{:S(2)}, u32[]{:S(2)}) collective-permute-start(bf16[112,1280]{1,0:T(8,128)(2,1)S(1)} %get-tuple-element.74), channel_id=1, source_target_pairs={{0,4},{4,8},{8,12},{12,0},{1,5},{5,9},{9,13},{13,1},{2,6},{6,10},{... | collective-permute-start | bytes 860168 | tf_op jit(solution)/shard_map/ppermute | solution.py:304
  19.0 4.4 %collective-permute-start.1 = (bf16[112,1280]{1,0:T(8,128)(2,1)S(1)}, bf16[112,1280]{1,0:T(8,128)(2,1)S(1)}, u32[]{:S(2)}, u32[]{:S(2)}) collective-permute-start(bf16[112,1280]{1,0:T(8,128)(2,1)S(1)} %get-tuple-element.75), channel_id=1, source_target_pairs={{0,8},{4,12},{8,0},{12,4},{1,9},{5,13},{9,1},{13,5},{2,10},{6,14},... | collective-permute-start | bytes 860168 | tf_op jit(solution)/shard_map/ppermute | solution.py:304
  23.4 3.1 %collective-permute-start.2 = (bf16[112,1280]{1,0:T(8,128)(2,1)S(1)}, bf16[112,1280]{1,0:T(8,128)(2,1)S(1)}, u32[]{:S(2)}, u32[]{:S(2)}) collective-permute-start(bf16[112,1280]{1,0:T(8,128)(2,1)S(1)} %get-tuple-element.73), channel_id=1, source_target_pairs={{0,12},{4,0},{8,4},{12,8},{1,13},{5,1},{9,5},{13,9},{2,14},{6,2},{... | collective-permute-start | bytes 860168 | tf_op jit(solution)/shard_map/ppermute | solution.py:304
  27.8 6.6 %collective-permute-done.1.x2 = bf16[112,1280]{1,0:T(8,128)(2,1)S(1)} collective-permute-done((bf16[112,1280]{1,0:T(8,128)(2,1)S(1)}, bf16[112,1280]{1,0:T(8,128)(2,1)S(1)}, u32[]{:S(2)}, u32[]{:S(2)}) %collective-permute-start.1) | collective-permute-done | bytes 286752 | tf_op jit(solution)/shard_map/ppermute | solution.py:304
  35.5 1.6 all-to-all-done
  37.1 1.5 row_sums_and_scores.1
  38.6 5.9 %all-to-all-start.1 = ((f32[4,8,896]{2,1,0:T(8,128)}), f32[4,8,896]{2,1,0:T(8,128)S(1)}, u32[]{:S(2)}, u32[]{:S(2)}) async-start(f32[4,8,896]{2,1,0:T(8,128)} %row_sums_and_scores.1), calls=%async_computation.1 | async-start | bytes 229376 | tf_op jit(solution)/shard_map/all_to_all | solution.py:348
  44.6 7.5 %all-to-all-done.1.parts = f32[4,8,896]{2,1,0:T(8,128)S(1)} async-done(((f32[4,8,896]{2,1,0:T(8,128)}), f32[4,8,896]{2,1,0:T(8,128)S(1)}, u32[]{:S(2)}, u32[]{:S(2)}) %all-to-all-start.1) | async-done | bytes 114720 | tf_op jit(solution)/shard_map/all_to_all | solution.py:348
  53.3 3.9 %all-to-all-start.2 = ((bf16[4,16,256]{2,1,0:T(8,128)(2,1)}), bf16[4,16,256]{2,1,0:T(8,128)(2,1)}, u32[]{:S(2)}, u32[]{:S(2)}) async-start(bf16[4,16,256]{2,1,0:T(8,128)(2,1)} %get-tuple-element.28), calls=%async_computation.2 | async-start | bytes 65536 | tf_op jit(solution)/shard_map/all_to_all | solution.py:358
  61.0 4.6 %sections_forward.1 = (f32[4,10,16,8,128]{4,3,2,1,0:T(8,128)S(1)}, f32[4,10,16,8,128]{4,3,2,1,0:T(8,128)S(1)}, f32[4,16,8,128]{3,2,1,0:T(8,128)S(1)}, f32[4,16,1280]{2,1,0:T(8,128)S(1)}) custom-call(f32[4,8,896]{2,1,0:T(8,128)S(1)} %all-to-all-done.1.parts, bf16[112,1280]{1,0:T(8,128)(2,1)S(1)} %copy-done.13, bf16[112,1280]{1,0:T(8,128)(2,1)S(1)} %copy-done.23, ...), custom_call_target="tpu_custom_call" | custom-call | flops 1000000000 | bytes 6000000 | tf_op jit(solution)/shard_map/sections_forward/pallas_call | solution.py:360
  68.5 1.7 copy-done.2
  71.2 1.7 copy-done.11
  73.0 4.7 %head_and_section.1 = (f32[10,16,8,128]{3,2,1,0:T(8,128)S(1)}, f32[10,16,8,128]{3,2,1,0:T(8,128)S(1)}, f32[16,1280]{1,0:T(8,128)S(1)}, f32[4,8,128]{2,1,0:T(8,128)S(1)}) custom-call(s32[4]{0:T(128)S(1)} %pad_add_fusion.hops, bf16[4,16,256]{2,1,0:T(8,128)(2,1)} %all-to-all-done.2.query_grad, bf16[1280,1024]{1,0:T(8,128)(2,1)S(1)} %copy-done.11, ...), custom_call_target="tpu_custom_call" | custom-call | tf_op jit(solution)/shard_map/head_and_section/pallas_call | solution.py:287
  77.7 13.0 %all_to_all.40.parts = f32[4,8,128]{2,1,0:T(8,128)S(1)} all-to-all(f32[4,8,128]{2,1,0:T(8,128)S(1)} %get-tuple-element.32), channel_id=1, replica_groups=mesh['dp'=32,'section'=4,'mp'=4] {'mp'}, dimensions={0} | all-to-all | bytes 32768 | tf_op jit(solution)/shard_map/all_to_all | solution.py:401
  90.7 2.8 %section_step.3 = (bf16[96,1280]{1,0:T(8,128)(2,1)S(1)}, f32[10,16,8,128]{3,2,1,0:T(8,128)S(1)}, f32[10,16,8,128]{3,2,1,0:T(8,128)S(1)}, f32[16,1280]{1,0:T(8,128)S(1)}, f32[4,8,128]{2,1,0:T(8,128)S(1)}) custom-call(s32[4]{0:T(128)S(1)} %pad_add_fusion.hops, f32[4,8,128]{2,1,0:T(8,128)S(1)} %all_to_all.40.parts, ...), custom_call_target="tpu_custom_call" | custom-call | tf_op jit(solution)/shard_map/section_step/pallas_call | solution.py:287
  94.2 9.0 %all_to_all.41.parts = f32[4,8,128]{2,1,0:T(8,128)S(1)} all-to-all(f32[4,8,128]{2,1,0:T(8,128)S(1)} %get-tuple-element.36), channel_id=1, replica_groups=mesh['dp'=32,'section'=4,'mp'=4] {'mp'}, dimensions={0} | all-to-all | bytes 32768 | tf_op jit(solution)/shard_map/all_to_all | solution.py:401
  103.2 3.4 %section_step.4 = (bf16[96,1280]{1,0:T(8,128)(2,1)S(1)}, f32[10,16,8,128]{3,2,1,0:T(8,128)S(1)}, f32[10,16,8,128]{3,2,1,0:T(8,128)S(1)}, f32[16,1280]{1,0:T(8,128)S(1)}, f32[4,8,128]{2,1,0:T(8,128)}) custom-call(s32[4]{0:T(128)S(1)} %pad_add_fusion.hops, f32[4,8,128]{2,1,0:T(8,128)S(1)} %all_to_all.41.parts, f32[10,16,8,128]{3,2,1,0:T(8,128)S(1)} %get-tuple-element.37.up, ...), custom_call_target="tpu_custom_call" | custom-call | tf_op jit(solution)/shard_map/section_step/pallas_call | solution.py:287
  109.6 3.3 %all-to-all-start.5 = ((f32[4,8,128]{2,1,0:T(8,128)}), f32[4,8,128]{2,1,0:T(8,128)S(1)}, u32[]{:S(2)}, u32[]{:S(2)}) async-start(f32[4,8,128]{2,1,0:T(8,128)} %get-tuple-element.39), calls=%async_computation.5 | async-start | bytes 32768 | tf_op jit(solution)/shard_map/all_to_all | solution.py:401
  122.8 1.7 copy-done.3
  128.6 2.8 %section_step.5 = (bf16[96,1280]{1,0:T(8,128)(2,1)S(1)}, f32[10,16,8,128]{3,2,1,0:T(8,128)S(1)}, f32[10,16,8,128]{3,2,1,0:T(8,128)S(1)}, f32[16,1280]{1,0:T(8,128)S(1)}, f32[4,8,128]{2,1,0:T(8,128)S(1)}) custom-call(s32[4]{0:T(128)S(1)} %pad_add_fusion.hops, f32[4,8,128]{2,1,0:T(8,128)S(1)} %all-to-all-done.5.parts, f32[10,16,8,128]{3,2,1,0:T(8,128)S(1)} %copy-done.15, ...), custom_call_target="tpu_custom_call" | custom-call | tf_op jit(solution)/shard_map/section_step/pallas_call | solution.py:287
  134.4 4.2 %collective-permute-start.3 = (f32[8,128]{1,0:T(8,128)}, f32[8,128]{1,0:T(8,128)}, u32[]{:S(2)}, u32[]{:S(2)}) collective-permute-start(f32[8,128]{1,0:T(8,128)} %get-tuple-element.78), channel_id=1, source_target_pairs={{0,1},{1,2},{2,3},{3,0},{4,5},{5,6},{6,7},{7,4},{8,9},{9,10},{10,1... | collective-permute-start | bytes 12296 | tf_op jit(solution)/shard_map/ppermute | solution.py:427
  138.6 5.2 %collective-permute-start.4 = (f32[8,128]{1,0:T(8,128)}, f32[8,128]{1,0:T(8,128)}, u32[]{:S(2)}, u32[]{:S(2)}) collective-permute-start(f32[8,128]{1,0:T(8,128)} %get-tuple-element.78), channel_id=1, source_target_pairs={{0,2},{1,3},{2,0},{3,1},{4,6},{5,7},{6,4},{7,5},{8,10},{9,11},{10,... | collective-permute-start | bytes 12296 | tf_op jit(solution)/shard_map/ppermute | solution.py:427
  143.8 5.2 %collective-permute-start.5 = (f32[8,128]{1,0:T(8,128)}, f32[8,128]{1,0:T(8,128)}, u32[]{:S(2)}, u32[]{:S(2)}) collective-permute-start(f32[8,128]{1,0:T(8,128)} %get-tuple-element.78), channel_id=1, source_target_pairs={{0,3},{1,0},{2,1},{3,2},{4,7},{5,4},{6,5},{7,6},{8,11},{9,8},{10,9... | collective-permute-start | bytes 12296 | tf_op jit(solution)/shard_map/ppermute | solution.py:427
  155.5 3.2 %collective-permute-start.6 = (bf16[96,1280]{1,0:T(8,128)(2,1)S(1)}, bf16[96,1280]{1,0:T(8,128)(2,1)S(1)}, u32[]{:S(2)}, u32[]{:S(2)}) collective-permute-start(bf16[96,1280]{1,0:T(8,128)(2,1)S(1)} %get-tuple-element.67), channel_id=1, source_target_pairs={{0,4},{4,8},{8,12},{12,0},{1,5},{5,9},{9,13},{13,1},{2,6},{6,10},{... | collective-permute-start | bytes 737288 | tf_op jit(solution)/shard_map/ppermute | solution.py:304
  160.0 16.5 %all-to-all-start.6 = ((bf16[128,8,128]{2,1,0:T(8,128)(2,1)}), bf16[128,8,128]{2,1,0:T(8,128)(2,1)S(1)}, u32[]{:S(2)}, u32[]{:S(2)}) async-start(bf16[128,8,128]{2,1,0:T(8,128)(2,1)} %pad.24.clone), calls=%async_computation.6 | async-start | bytes 524288 | tf_op jit(solution)/shard_map/all_to_all | solution.py:421
  176.6 4.8 %collective-permute-start.7 = (bf16[96,1280]{1,0:T(8,128)(2,1)S(1)}, bf16[96,1280]{1,0:T(8,128)(2,1)S(1)}, u32[]{:S(2)}, u32[]{:S(2)}) collective-permute-start(bf16[96,1280]{1,0:T(8,128)(2,1)S(1)} %get-tuple-element.66), channel_id=1, source_target_pairs={{0,8},{4,12},{8,0},{12,4},{1,9},{5,13},{9,1},{13,5},{2,10},{6,14},... | collective-permute-start | bytes 737288 | tf_op jit(solution)/shard_map/ppermute | solution.py:304
  181.4 2.8 %collective-permute-start.8 = (bf16[96,1280]{1,0:T(8,128)(2,1)S(1)}, bf16[96,1280]{1,0:T(8,128)(2,1)S(1)}, u32[]{:S(2)}, u32[]{:S(2)}) collective-permute-start(bf16[96,1280]{1,0:T(8,128)(2,1)S(1)} %get-tuple-element.65), channel_id=1, source_target_pairs={{0,12},{4,0},{8,4},{12,8},{1,13},{5,1},{9,5},{13,9},{2,14},{6,2},{... | collective-permute-start | bytes 737288 | tf_op jit(solution)/shard_map/ppermute | solution.py:304
  184.3 5.0 %collective-permute-done.7 = bf16[96,1280]{1,0:T(8,128)(2,1)S(1)} collective-permute-done((bf16[96,1280]{1,0:T(8,128)(2,1)S(1)}, bf16[96,1280]{1,0:T(8,128)(2,1)S(1)}, u32[]{:S(2)}, u32[]{:S(2)}) %collective-permute-start.7) | collective-permute-done | bytes 245792 | tf_op jit(solution)/shard_map/ppermute | solution.py:304
  189.4 5.0 %collective-permute-done.8 = bf16[96,1280]{1,0:T(8,128)(2,1)S(1)} collective-permute-done((bf16[96,1280]{1,0:T(8,128)(2,1)S(1)}, bf16[96,1280]{1,0:T(8,128)(2,1)S(1)}, u32[]{:S(2)}, u32[]{:S(2)}) %collective-permute-start.8) | collective-permute-done | bytes 245792 | tf_op jit(solution)/shard_map/ppermute | solution.py:304
  196.2 8.0 %all-to-all-start.7 = ((bf16[32,5,128]{2,1,0:T(8,128)(2,1)}), bf16[32,5,128]{2,1,0:T(8,128)(2,1)S(1)}, u32[]{:S(2)}, u32[]{:S(2)}) async-start(bf16[32,5,128]{2,1,0:T(8,128)(2,1)} %broadcast_in_dim.59), calls=%async_computation.7 | async-start | bytes 131072 | tf_op jit(solution)/shard_map/all_to_all | solution.py:441
  205.0 7.1 %all-to-all-done.7 = bf16[32,5,128]{2,1,0:T(8,128)(2,1)S(1)} async-done(((bf16[32,5,128]{2,1,0:T(8,128)(2,1)}), bf16[32,5,128]{2,1,0:T(8,128)(2,1)S(1)}, u32[]{:S(2)}, u32[]{:S(2)}) %all-to-all-start.7) | async-done | bytes 40992 | tf_op jit(solution)/shard_map/all_to_all | solution.py:441
  (154 shorter events, 44.9 us)
Async XLA Ops:
  0.6 26.8 %copy-start = (f32[2,12]{1,0:T(2,128)S(1)}, f32[2,12]{1,0:T(2,128)}, u32[]{:S(2)}) copy-start(f32[2,12]{1,0:T(2,128)} %param.15) | copy-start | bytes 292
  0.6 15.0 %copy-start.39 = (f32[1,1280]{1,0:T(1,128)S(1)}, f32[1,1280]{1,0:T(1,128)}, u32[]{:S(2)}) copy-start(f32[1,1280]{1,0:T(1,128)} %param.9) | copy-start | bytes 15364
  0.7 15.1 %copy-start.36 = (bf16[1,2,12,16,1280]{4,3,2,1,0:T(8,128)(2,1)S(1)}, bf16[1,2,12,16,1280]{4,3,2,1,0:T(8,128)(2,1)}, u32[]{:S(2)}) copy-start(bf16[1,2,12,16,1280]{4,3,2,1,0:T(8,128)(2,1)} %param.8) | copy-start | bytes 2949124
  0.7 15.2 %copy-start.38 = (bf16[1,15,1280]{2,1,0:T(8,128)(2,1)S(1)}, bf16[1,15,1280]{2,1,0:T(8,128)(2,1)}, u32[]{:S(2)}) copy-start(bf16[1,15,1280]{2,1,0:T(8,128)(2,1)} %param.10) | copy-start | bytes 115204
  2.5 24.8 %copy-start.40 = (s32[2,12]{1,0:T(2,128)S(1)}, s32[2,12]{1,0:T(2,128)}, u32[]{:S(2)}) copy-start(s32[2,12]{1,0:T(2,128)} %param.14) | copy-start | bytes 292
  2.5 34.6 %all-to-all-start = ((bf16[32,24,512]{2,1,0:T(8,128)(2,1)}), bf16[32,24,512]{2,1,0:T(8,128)(2,1)S(1)}, u32[]{:S(2)}, u32[]{:S(2)}) async-start(bf16[32,24,512]{2,1,0:T(8,128)(2,1)} %broadcast_in_dim.50), calls=%async_computation | async-start | bytes 1572864 | tf_op jit(solution)/shard_map/all_to_all | solution.py:324
  15.9 37.3 %copy-start.12 = (bf16[112,1280]{1,0:T(8,128)(2,1)}, bf16[112,1280]{1,0:T(8,128)(2,1)S(1)}, u32[]{:S(2)}) copy-start(bf16[112,1280]{1,0:T(8,128)(2,1)S(1)} %get-tuple-element.76.x0) | copy-start | bytes 860164
  15.9 11.8 %collective-permute-start = (bf16[112,1280]{1,0:T(8,128)(2,1)S(1)}, bf16[112,1280]{1,0:T(8,128)(2,1)S(1)}, u32[]{:S(2)}, u32[]{:S(2)}) collective-permute-start(bf16[112,1280]{1,0:T(8,128)(2,1)S(1)} %get-tuple-element.74), channel_id=1, source_target_pairs={{0,4},{4,8},{8,12},{12,0},{1,5},{5,9},{9,13},{13,1},{2,6},{6,10},{... | collective-permute-start | bytes 860168 | tf_op jit(solution)/shard_map/ppermute | solution.py:304
  19.0 15.3 %collective-permute-start.1 = (bf16[112,1280]{1,0:T(8,128)(2,1)S(1)}, bf16[112,1280]{1,0:T(8,128)(2,1)S(1)}, u32[]{:S(2)}, u32[]{:S(2)}) collective-permute-start(bf16[112,1280]{1,0:T(8,128)(2,1)S(1)} %get-tuple-element.75), channel_id=1, source_target_pairs={{0,8},{4,12},{8,0},{12,4},{1,9},{5,13},{9,1},{13,5},{2,10},{6,14},... | collective-permute-start | bytes 860168 | tf_op jit(solution)/shard_map/ppermute | solution.py:304
  23.4 12.1 %collective-permute-start.2 = (bf16[112,1280]{1,0:T(8,128)(2,1)S(1)}, bf16[112,1280]{1,0:T(8,128)(2,1)S(1)}, u32[]{:S(2)}, u32[]{:S(2)}) collective-permute-start(bf16[112,1280]{1,0:T(8,128)(2,1)S(1)} %get-tuple-element.73), channel_id=1, source_target_pairs={{0,12},{4,0},{8,4},{12,8},{1,13},{5,1},{9,5},{13,9},{2,14},{6,2},{... | collective-permute-start | bytes 860168 | tf_op jit(solution)/shard_map/ppermute | solution.py:304
  27.8 25.5 %copy-start.22 = (bf16[112,1280]{1,0:T(8,128)(2,1)}, bf16[112,1280]{1,0:T(8,128)(2,1)S(1)}, u32[]{:S(2)}) copy-start(bf16[112,1280]{1,0:T(8,128)(2,1)S(1)} %collective-permute-done.x1) | copy-start | bytes 860164
  34.4 18.9 %copy-start.24 = (bf16[112,1280]{1,0:T(8,128)(2,1)}, bf16[112,1280]{1,0:T(8,128)(2,1)S(1)}, u32[]{:S(2)}) copy-start(bf16[112,1280]{1,0:T(8,128)(2,1)S(1)} %collective-permute-done.1.x2) | copy-start | bytes 860164
  35.5 17.7 %copy-start.26 = (bf16[112,1280]{1,0:T(8,128)(2,1)}, bf16[112,1280]{1,0:T(8,128)(2,1)S(1)}, u32[]{:S(2)}) copy-start(bf16[112,1280]{1,0:T(8,128)(2,1)S(1)} %collective-permute-done.2.x3) | copy-start | bytes 860164
  38.6 13.5 %all-to-all-start.1 = ((f32[4,8,896]{2,1,0:T(8,128)}), f32[4,8,896]{2,1,0:T(8,128)S(1)}, u32[]{:S(2)}, u32[]{:S(2)}) async-start(f32[4,8,896]{2,1,0:T(8,128)} %row_sums_and_scores.1), calls=%async_computation.1 | async-start | bytes 229376 | tf_op jit(solution)/shard_map/all_to_all | solution.py:348
  53.3 15.2 %all-to-all-start.2 = ((bf16[4,16,256]{2,1,0:T(8,128)(2,1)}), bf16[4,16,256]{2,1,0:T(8,128)(2,1)}, u32[]{:S(2)}, u32[]{:S(2)}) async-start(bf16[4,16,256]{2,1,0:T(8,128)(2,1)} %get-tuple-element.28), calls=%async_computation.2 | async-start | bytes 65536 | tf_op jit(solution)/shard_map/all_to_all | solution.py:358
  68.5 1.7 copy-start.2
  71.2 1.7 copy-start.11
  73.0 17.8 %copy-start.8 = (f32[4,16,8,128]{3,2,1,0:T(8,128)S(1)}, f32[4,16,8,128]{3,2,1,0:T(8,128)}, u32[]{:S(2)}) copy-start(f32[4,16,8,128]{3,2,1,0:T(8,128)} %copy-done.7) | copy-start | bytes 786436
  94.2 12.4 %copy-start.28 = (bf16[96,1280]{1,0:T(8,128)(2,1)}, bf16[96,1280]{1,0:T(8,128)(2,1)S(1)}, u32[]{:S(2)}) copy-start(bf16[96,1280]{1,0:T(8,128)(2,1)S(1)} %get-tuple-element.47) | copy-start | bytes 737284
  109.6 13.2 %all-to-all-start.5 = ((f32[4,8,128]{2,1,0:T(8,128)}), f32[4,8,128]{2,1,0:T(8,128)S(1)}, u32[]{:S(2)}, u32[]{:S(2)}) async-start(f32[4,8,128]{2,1,0:T(8,128)} %get-tuple-element.39), calls=%async_computation.5 | async-start | bytes 32768 | tf_op jit(solution)/shard_map/all_to_all | solution.py:401
  122.8 1.7 copy-start.3
  134.4 15.7 %collective-permute-start.3 = (f32[8,128]{1,0:T(8,128)}, f32[8,128]{1,0:T(8,128)}, u32[]{:S(2)}, u32[]{:S(2)}) collective-permute-start(f32[8,128]{1,0:T(8,128)} %get-tuple-element.78), channel_id=1, source_target_pairs={{0,1},{1,2},{2,3},{3,0},{4,5},{5,6},{6,7},{7,4},{8,9},{9,10},{10,1... | collective-permute-start | bytes 12296 | tf_op jit(solution)/shard_map/ppermute | solution.py:427
  138.6 11.6 %collective-permute-start.4 = (f32[8,128]{1,0:T(8,128)}, f32[8,128]{1,0:T(8,128)}, u32[]{:S(2)}, u32[]{:S(2)}) collective-permute-start(f32[8,128]{1,0:T(8,128)} %get-tuple-element.78), channel_id=1, source_target_pairs={{0,2},{1,3},{2,0},{3,1},{4,6},{5,7},{6,4},{7,5},{8,10},{9,11},{10,... | collective-permute-start | bytes 12296 | tf_op jit(solution)/shard_map/ppermute | solution.py:427
  143.8 6.4 %collective-permute-start.5 = (f32[8,128]{1,0:T(8,128)}, f32[8,128]{1,0:T(8,128)}, u32[]{:S(2)}, u32[]{:S(2)}) collective-permute-start(f32[8,128]{1,0:T(8,128)} %get-tuple-element.78), channel_id=1, source_target_pairs={{0,3},{1,0},{2,1},{3,2},{4,7},{5,4},{6,5},{7,6},{8,11},{9,8},{10,9... | collective-permute-start | bytes 12296 | tf_op jit(solution)/shard_map/ppermute | solution.py:427
  149.1 6.2 %copy-start.29 = (bf16[96,1280]{1,0:T(8,128)(2,1)S(1)}, bf16[96,1280]{1,0:T(8,128)(2,1)}, u32[]{:S(2)}) copy-start(bf16[96,1280]{1,0:T(8,128)(2,1)} %copy-done.28) | copy-start | bytes 737284
  149.1 6.2 %copy-start.31 = (bf16[96,1280]{1,0:T(8,128)(2,1)S(1)}, bf16[96,1280]{1,0:T(8,128)(2,1)}, u32[]{:S(2)}) copy-start(bf16[96,1280]{1,0:T(8,128)(2,1)} %copy-done.30) | copy-start | bytes 737284
  155.5 28.7 %collective-permute-start.6 = (bf16[96,1280]{1,0:T(8,128)(2,1)S(1)}, bf16[96,1280]{1,0:T(8,128)(2,1)S(1)}, u32[]{:S(2)}, u32[]{:S(2)}) collective-permute-start(bf16[96,1280]{1,0:T(8,128)(2,1)S(1)} %get-tuple-element.67), channel_id=1, source_target_pairs={{0,4},{4,8},{8,12},{12,0},{1,5},{5,9},{9,13},{13,1},{2,6},{6,10},{... | collective-permute-start | bytes 737288 | tf_op jit(solution)/shard_map/ppermute | solution.py:304
  160.0 34.4 %all-to-all-start.6 = ((bf16[128,8,128]{2,1,0:T(8,128)(2,1)}), bf16[128,8,128]{2,1,0:T(8,128)(2,1)S(1)}, u32[]{:S(2)}, u32[]{:S(2)}) async-start(bf16[128,8,128]{2,1,0:T(8,128)(2,1)} %pad.24.clone), calls=%async_computation.6 | async-start | bytes 524288 | tf_op jit(solution)/shard_map/all_to_all | solution.py:421
  176.6 12.8 %collective-permute-start.7 = (bf16[96,1280]{1,0:T(8,128)(2,1)S(1)}, bf16[96,1280]{1,0:T(8,128)(2,1)S(1)}, u32[]{:S(2)}, u32[]{:S(2)}) collective-permute-start(bf16[96,1280]{1,0:T(8,128)(2,1)S(1)} %get-tuple-element.66), channel_id=1, source_target_pairs={{0,8},{4,12},{8,0},{12,4},{1,9},{5,13},{9,1},{13,5},{2,10},{6,14},... | collective-permute-start | bytes 737288 | tf_op jit(solution)/shard_map/ppermute | solution.py:304
  181.4 13.0 %collective-permute-start.8 = (bf16[96,1280]{1,0:T(8,128)(2,1)S(1)}, bf16[96,1280]{1,0:T(8,128)(2,1)S(1)}, u32[]{:S(2)}, u32[]{:S(2)}) collective-permute-start(bf16[96,1280]{1,0:T(8,128)(2,1)S(1)} %get-tuple-element.65), channel_id=1, source_target_pairs={{0,12},{4,0},{8,4},{12,8},{1,13},{5,1},{9,5},{13,9},{2,14},{6,2},{... | collective-permute-start | bytes 737288 | tf_op jit(solution)/shard_map/ppermute | solution.py:304
  194.4 18.4 %copy-start.37 = (bf16[1,2,12,16,1280]{4,3,2,1,0:T(8,128)(2,1)}, bf16[1,2,12,16,1280]{4,3,2,1,0:T(8,128)(2,1)S(1)}, u32[]{:S(2)}) copy-start(bf16[1,2,12,16,1280]{4,3,2,1,0:T(8,128)(2,1)S(1)} %constant_dynamic-update-slice_fusion) | copy-start | bytes 2949124
  196.2 15.9 %all-to-all-start.7 = ((bf16[32,5,128]{2,1,0:T(8,128)(2,1)}), bf16[32,5,128]{2,1,0:T(8,128)(2,1)S(1)}, u32[]{:S(2)}, u32[]{:S(2)}) async-start(bf16[32,5,128]{2,1,0:T(8,128)(2,1)} %broadcast_in_dim.59), calls=%async_computation.7 | async-start | bytes 131072 | tf_op jit(solution)/shard_map/all_to_all | solution.py:441
  (24 other events, 22.3 us)

commit v2 on v1

--- a/solution.py
+++ b/solution.py
@@ -1,5 +1,3 @@
-import functools
-
 import jax
 import jax.numpy as jnp
 from jax import lax
@@ -33,7 +31,7 @@
 
 NT = (((1,), (1,)), ((), ()))
 VMEM = pl.BlockSpec(memory_space=pltpu.VMEM)
-PARAMS = pltpu.CompilerParams(vmem_limit_bytes=40 * 1024 * 1024)
+PARAMS = pltpu.CompilerParams(vmem_limit_bytes=24 * 1024 * 1024)
 
 
 def lane_sums(partial):
@@ -91,8 +89,16 @@
         query_grad[peer] = result
 
 
+def spread(row, rows_out, natural):
+    natural[...] = wide_rows(row)
+    for f in range(FRAMES):
+        rows_out[f] = natural[pl.ds(f, PAD, stride=FRAMES), :]
+
+
 def forward_kernel(
-    parts, x0, x1, x2, x3, normed_out, gate_out, inv_out, taps_out, natural, mean_rows, inv_rows
+    parts, x0, x1, x2, x3,
+    normed_out, gate_out, inv_out, inv_row_out, taps_out,
+    natural, mean_rows, inv_rows,
 ):
     stats = parts[0, :, TEXTS:]
     for peer in range(1, MP):
@@ -101,8 +107,10 @@
     for hop, x in enumerate((x0, x1, x2, x3)):
         mean = stats[2 * hop : 2 * hop + 1] / D
         variance = stats[2 * hop + 1 : 2 * hop + 2] / D - mean * mean
+        inv = lax.rsqrt(variance + EPSILON)
+        inv_row_out[hop : hop + 1, :] = inv
         mean_rows[...] = wide_rows(mean)
-        inv_rows[...] = wide_rows(lax.rsqrt(variance + EPSILON))
+        inv_rows[...] = wide_rows(inv)
         for f in range(FRAMES):
             inv_out[hop, f] = inv_rows[pl.ds(f, PAD, stride=FRAMES), :]
 
@@ -133,49 +141,149 @@
         lax.fori_loop(0, BLOCKS, block_step, 0)
 
 
-def back_block(upstream, block, normed, gate, taps_in, grad_out, tap_out, first, second):
-    lanes = lanes_of(block)
-    weights = taps_in[0, :, lanes]
-    taps = [jnp.broadcast_to(weights[k : k + 1], (PAD, LANES)) for k in range(KERNEL + 1)]
-    gain = taps[KERNEL]
-    grad_conv = [upstream[f] * gate[0, block, f] for f in range(FRAMES)]
+def pair_kernel(
+    hops, normed, gate, taps_in, out, normed_rows, gate_rows, both_rows, left, right, plain
+):
+    frame = lax.broadcasted_iota(jnp.int32, (FRAMES, 2 * LANES), 0)
+    lane = lax.broadcasted_iota(jnp.int32, (FRAMES, 2 * LANES), 1)
+    lane_frame = lane & (FRAMES - 1)
+    lane_clip = (lane & (LANES - 1)) >> 4
+    for pair, section in enumerate((2, 0)):
+        here = hops[section]
+        above = hops[section + 1]
+
+        def block_step(block, carry, here=here, above=above):
+            lanes = lanes_of(block)
+            weights = taps_in[here, :, lanes]
+            weights = weights * weights[KERNEL : KERNEL + 1]
+            plain[:, lanes] = weights.astype(BF16)
+            for f in range(FRAMES):
+                rows = pl.ds(f, PAD, stride=FRAMES)
+                value = gate[here, block, f]
+                normed_rows[rows, :] = normed[here, block, f]
+                gate_rows[rows, :] = value
+                both_rows[rows, :] = value * normed[above, block, f]
+            right[0:LANES, lanes] = gate_rows[...].astype(BF16)
+            right[LANES : 2 * LANES, lanes] = both_rows[...].astype(BF16)
+            for c in range(CLIPS):
+                value = normed_rows[c * FRAMES : (c + 1) * FRAMES, :]
+                for k in range(KERNEL):
+                    start = (c * KERNEL + k) * FRAMES
+                    left[start : start + FRAMES, lanes] = (value * weights[k : k + 1]).astype(
+                        BF16
+                    )
+            return carry
+
+        lax.fori_loop(0, BLOCKS, block_step, 0)
+        columns = right[...]
+        sums = lax.dot_general(plain[...], columns, NT, preferred_element_type=F32)
+        first = jnp.zeros((FRAMES, 2 * LANES), F32)
+        second = jnp.zeros((FRAMES, 2 * LANES), F32)
+        for k in range(KERNEL):
+            first = first + jnp.where(lane_frame == frame - k + HALF, sums[k : k + 1], 0.0)
+        for c in range(CLIPS):
+            start = c * KERNEL * FRAMES
+            sums = lax.dot_general(
+                left[start : start + KERNEL * FRAMES, :], columns, NT, preferred_element_type=F32
+            )
+            total = jnp.zeros((FRAMES, 2 * LANES), F32)
+            for k in range(KERNEL):
+                total = total + jnp.where(
+                    lane_frame == frame - k + HALF, sums[k * FRAMES : (k + 1) * FRAMES], 0.0
+                )
+            second = second + jnp.where(lane_clip == c, total, 0.0)
+        out[pair, 0:16, :] = first[:, 0:LANES]
+        out[pair, 16:32, :] = second[:, 0:LANES]
+        out[pair, 32:48, :] = first[:, LANES:]
+        out[pair, 48:64, :] = second[:, LANES:]
+
+
+def tap_rows(taps_in, hop, block):
+    weights = taps_in[hop, :, lanes_of(block)]
+    return [jnp.broadcast_to(weights[k : k + 1], (PAD, LANES)) for k in range(KERNEL + 1)]
+
+
+def conv_back(grad_conv, taps):
+    out = []
     for f in range(FRAMES):
         conv = None
         for k in range(KERNEL):
             if 0 <= f - k + HALF < FRAMES:
                 term = taps[k] * grad_conv[f - k + HALF]
                 conv = term if conv is None else conv + term
-        conv = conv * gain
-        grad_out[block, f] = conv
-        first[f] += conv
-        second[f] += conv * normed[0, block, f]
-    hidden = [normed[0, block, f] * gain for f in range(FRAMES)]
+        out.append(conv * taps[KERNEL])
+    return out
+
+
+def add_taps(grad_conv, normed, hop, block, taps, tap_out):
+    hidden = [normed[hop, block, f] * taps[KERNEL] for f in range(FRAMES)]
     for k in range(KERNEL):
         total = None
         for f in range(FRAMES):
             if 0 <= f + k - HALF < FRAMES:
                 term = grad_conv[f] * hidden[f + k - HALF]
                 total = term if total is None else total + term
-        tap_out[k : k + 1, lanes] = jnp.sum(total, axis=0, keepdims=True)
-    tap_out[KERNEL : KERNEL + 1, lanes] = jnp.zeros((1, LANES), F32)
-
-
-def write_sums(first, second, sums_out):
+        tap_out[k : k + 1, lanes_of(block)] = jnp.sum(total, axis=0, keepdims=True)
+
+
+def add_sums(grads, normed, hop, block, first, second):
+    for f in range(FRAMES):
+        first[f] += grads[f]
+        second[f] += grads[f] * normed[hop, block, f]
+
+
+def write_sums(sums, matrices, out, natural):
     row = lax.broadcasted_iota(jnp.int32, (PAD, LANES), 0)
-    sums = jnp.where(
-        row == 0,
-        lane_sums(first[...].reshape(LANES, LANES)),
-        lane_sums(second[...].reshape(LANES, LANES)),
-    )
+    packed = jnp.zeros((PAD, LANES), F32)
+    for index, total in enumerate(sums):
+        for f in range(FRAMES):
+            natural[pl.ds(f, PAD, stride=FRAMES), :] = total[f]
+        packed = jnp.where(row == index, lane_sums(natural[...]), packed)
     for peer in range(MP):
-        sums_out[peer] = sums
+        out[peer, 0:PAD, :] = packed
+        out[peer, PAD:, :] = matrices
+
+
+def read_sums(parts, inv_row, above, here, natural, above_first, above_second, here_first, here_second):
+    total = parts[0]
+    for peer in range(1, MP):
+        total = total + parts[peer]
+    scale = inv_row[pl.ds(above, 1), :] / D
+    first = total[0:1] * scale
+    second = total[1:2] * scale
+    matrix = total[PAD:]
+    products = matrix[0:32] * first + matrix[32:64] * second
+    row = lax.broadcasted_iota(jnp.int32, (LANES, LANES), 0)
+    column = lax.broadcasted_iota(jnp.int32, (LANES, LANES), 1)
+    same = jnp.where((row >> 4) == (column >> 4), 1.0, 0.0)
+    products = jnp.dot(
+        products, same, preferred_element_type=F32, precision=lax.Precision.HIGHEST
+    )
+    keep = (row & (FRAMES - 1)) == (column & (FRAMES - 1))
+    keep = keep[0:FRAMES]
+    change_first = jnp.sum(jnp.where(keep, products[0:16], 0.0), axis=0, keepdims=True)
+    change_second = jnp.sum(jnp.where(keep, products[16:32], 0.0), axis=0, keepdims=True)
+    spread(first, above_first, natural)
+    spread(second, above_second, natural)
+    scale = inv_row[pl.ds(here, 1), :] / D
+    spread((total[2:3] - change_first) * scale, here_first, natural)
+    spread((total[3:4] - change_second) * scale, here_second, natural)
+
+
+def write_result(values, natural, result, index, block):
+    for f in range(FRAMES):
+        natural[pl.ds(f, PAD, stride=FRAMES), :] = values[f]
+    result[index, :, lanes_of(block)] = natural[0:ROWS, :].astype(BF16)
 
 
 def head_kernel(
-    hops, query_grad, weight, normed, gate, taps_in, up_out, grad_out, tap_out, sums_out, first, second
+    hops, query_grad, weight, normed, gate, inv, taps_in, matrices,
+    up_out, tap_out, sums_out,
+    s0, s1, s2, s3, natural,
 ):
-    first[...] = jnp.zeros_like(first)
-    second[...] = jnp.zeros_like(second)
+    for total in (s0, s1, s2, s3):
+        total[...] = jnp.zeros_like(total)
+    three, two = hops[3], hops[2]
 
     def block_step(block, carry):
         rows = weight[pl.ds(pl.multiple_of(block * LANES, LANES), LANES), :]
@@ -189,80 +297,115 @@
             )
             pooled = term if pooled is None else pooled + term
         head = (pooled[0:PAD] / FRAMES).astype(BF16).astype(F32)
+        taps = tap_rows(taps_in, three, block)
+        grad_conv = [head * gate[three, block, f] for f in range(FRAMES)]
+        grads = conv_back(grad_conv, taps)
+        add_taps(grad_conv, normed, three, block, taps, tap_out)
+        add_sums(grads, normed, three, block, s0, s1)
+        ups = [head + inv[three, f] * grads[f] for f in range(FRAMES)]
         for f in range(FRAMES):
-            up_out[block, f] = head
-        back_block(
-            [head] * FRAMES, block, normed, gate, taps_in, grad_out, tap_out, first, second
+            up_out[block, f] = ups[f]
+        grads = conv_back(
+            [ups[f] * gate[two, block, f] for f in range(FRAMES)], tap_rows(taps_in, two, block)
         )
+        add_sums(grads, normed, two, block, s2, s3)
         return carry
 
     lax.fori_loop(0, BLOCKS, block_step, 0)
-    write_sums(first, second, sums_out)
-
-
-def read_sums(parts, inv, first_rows, second_rows):
-    sums = parts[0]
-    for peer in range(1, MP):
-        sums = sums + parts[peer]
-    sums = sums / D
-    first_rows[...] = inv[0] * wide_rows(sums[0:1]).reshape(FRAMES, PAD, LANES)
-    second_rows[...] = inv[0] * wide_rows(sums[1:2]).reshape(FRAMES, PAD, LANES)
-
-
-def corrected(block, up, grad, normed, inv, first_rows, second_rows, natural, result):
-    values = []
-    for f in range(FRAMES):
-        value = (
-            up[block, f]
-            + inv[0, f] * grad[block, f]
-            - first_rows[f]
-            - normed[0, block, f] * second_rows[f]
+    write_sums((s0, s1, s2, s3), matrices[0], sums_out, natural)
+
+
+def corrected(up, normed, hop, block, first_rows, second_rows):
+    return [
+        up[f] - first_rows[f] - normed[hop, block, f] * second_rows[f] for f in range(FRAMES)
+    ]
+
+
+def middle_kernel(
+    hops, parts, up, normed, gate, inv, inv_row, taps_in, matrices,
+    result, up_out, tap_two, tap_one, sums_out,
+    s0, s1, s2, s3, a0, a1, b0, b1, natural,
+):
+    for total in (s0, s1, s2, s3):
+        total[...] = jnp.zeros_like(total)
+    three, two, one, zero = hops[3], hops[2], hops[1], hops[0]
+    read_sums(parts, inv_row, three, two, natural, a0, a1, b0, b1)
+
+    def block_step(block, carry):
+        ups = corrected([up[block, f] for f in range(FRAMES)], normed, three, block, a0, a1)
+        write_result(ups, natural, result, 0, block)
+        taps = tap_rows(taps_in, two, block)
+        grad_conv = [ups[f] * gate[two, block, f] for f in range(FRAMES)]
+        grads = conv_back(grad_conv, taps)
+        add_taps(grad_conv, normed, two, block, taps, tap_two)
+        ups = [ups[f] + inv[two, f] * grads[f] for f in range(FRAMES)]
+        ups = corrected(ups, normed, two, block, b0, b1)
+        write_result(ups, natural, result, 1, block)
+        taps = tap_rows(taps_in, one, block)
+        grad_conv = [ups[f] * gate[one, block, f] for f in range(FRAMES)]
+        grads = conv_back(grad_conv, taps)
+        add_taps(grad_conv, normed, one, block, taps, tap_one)
+        add_sums(grads, normed, one, block, s0, s1)
+        ups = [ups[f] + inv[one, f] * grads[f] for f in range(FRAMES)]
+        for f in range(FRAMES):
+            up_out[block, f] = ups[f]
+        grads = conv_back(
+            [ups[f] * gate[zero, block, f] for f in range(FRAMES)],
+            tap_rows(taps_in, zero, block),
         )
-        natural[pl.ds(f, PAD, stride=FRAMES), :] = value
-        values.append(value)
-    result[:, lanes_of(block)] = natural[0:ROWS, :].astype(BF16)
-    return values
-
-
-def step_kernel(
-    hops, parts, up, grad, normed_before, inv_before, normed, gate, taps_in,
-    result, up_out, grad_out, tap_out, sums_out,
-    first, second, first_rows, second_rows, natural,
+        add_sums(grads, normed, zero, block, s2, s3)
+        return carry
+
+    lax.fori_loop(0, BLOCKS, block_step, 0)
+    write_sums((s0, s1, s2, s3), matrices[1], sums_out, natural)
+
+
+def end_kernel(
+    hops, parts, up, normed, gate, inv, inv_row, taps_in,
+    before, tap_three, tap_two, tap_one, pair_parts,
+    result, message,
+    a0, a1, b0, b1, natural, tap_zero, wide,
 ):
-    first[...] = jnp.zeros_like(first)
-    second[...] = jnp.zeros_like(second)
-    read_sums(parts, inv_before, first_rows, second_rows)
+    three, two, one, zero = hops[3], hops[2], hops[1], hops[0]
+    slots = [(SECTIONS - hop) & (SECTIONS - 1) for hop in (zero, one, two, three)]
+    read_sums(parts, inv_row, one, zero, natural, a0, a1, b0, b1)
+    result[slots[3]] = before[0]
+    result[slots[2]] = before[1]
 
     def block_step(block, carry):
-        values = corrected(
-            block, up, grad, normed_before, inv_before, first_rows, second_rows, natural, result
-        )
-        for f in range(FRAMES):
-            up_out[block, f] = values[f]
-        back_block(values, block, normed, gate, taps_in, grad_out, tap_out, first, second)
+        ups = corrected([up[block, f] for f in range(FRAMES)], normed, one, block, a0, a1)
+        write_result(ups, natural, result, slots[1], block)
+        taps = tap_rows(taps_in, zero, block)
+        grad_conv = [ups[f] * gate[zero, block, f] for f in range(FRAMES)]
+        grads = conv_back(grad_conv, taps)
+        add_taps(grad_conv, normed, zero, block, taps, tap_zero)
+        ups = [ups[f] + inv[zero, f] * grads[f] for f in range(FRAMES)]
+        ups = corrected(ups, normed, zero, block, b0, b1)
+        write_result(ups, natural, result, slots[0], block)
         return carry
 
     lax.fori_loop(0, BLOCKS, block_step, 0)
-    write_sums(first, second, sums_out)
-
-
-def last_kernel(
-    hops, parts, up, grad, normed_before, inv_before, result, first_rows, second_rows, natural
-):
-    read_sums(parts, inv_before, first_rows, second_rows)
-
-    def block_step(block, carry):
-        corrected(
-            block, up, grad, normed_before, inv_before, first_rows, second_rows, natural, result
-        )
-        return carry
-
-    lax.fori_loop(0, BLOCKS, block_step, 0)
+
+    wide[...] = jnp.zeros_like(wide)
+    for target in range(DP):
+        for section, source in enumerate((tap_zero, tap_one, tap_two, tap_three)):
+            row = target // 2
+            if row < KERNEL:
+                for piece in range(5):
+                    start = ((target % 2) * 5 + piece) * LANES
+                    wide[target * SECTIONS + section, piece : piece + 1, :] = source[
+                        row : row + 1, start : start + LANES
+                    ]
+            wide[target * SECTIONS + section, 5:7, :] = pair_parts[target]
+    half = DP * SECTIONS // 2
+    message[...] = wide[...].reshape(2 * half * PAD, LANES).astype(BF16)
 
 
 FRAME_MAJOR = (BLOCKS, FRAMES, PAD, LANES)
 ROW_TILE = pltpu.VMEM((FRAMES, PAD, LANES), F32)
 NATURAL = pltpu.VMEM((LANES, LANES), F32)
+MATRIX_ROWS = 64
+SMEM = pl.BlockSpec(memory_space=pltpu.SMEM)
 
 
 def shape(dims, dtype=F32):
@@ -273,28 +416,15 @@
     return pl.CostEstimate(flops=flops, bytes_accessed=moved, transcendentals=0)
 
 
-def whole(*dims):
-    return pl.BlockSpec(dims, lambda i, hops: (0,) * len(dims))
-
-
-def at_hop(section, *dims):
-    return pl.BlockSpec(
-        (1,) + dims, lambda i, hops: (hops[section],) + (0,) * len(dims)
-    )
-
-
-def section_call(kernel, hops, operands, in_specs, outs, scratch, name):
+def local_call(kernel, hops, operands, outs, scratch, name, estimate=None):
     return pl.pallas_call(
         kernel,
         out_shape=outs,
-        grid_spec=pltpu.PrefetchScalarGridSpec(
-            num_scalar_prefetch=1,
-            grid=(1,),
-            in_specs=in_specs,
-            out_specs=[whole(*out.shape) for out in outs],
-            scratch_shapes=scratch,
-        ),
+        in_specs=[SMEM] + [VMEM] * len(operands),
+        out_specs=[VMEM] * len(outs),
+        scratch_shapes=scratch,
         compiler_params=PARAMS,
+        cost_estimate=estimate,
         name=name,
     )(hops, *operands)
 
@@ -357,84 +487,73 @@
     )(parts, texts, valid, column, own_weights)
     query_grad = lax.all_to_all(query_grad, "mp", 0, 0)
 
-    normed, gate, inv, taps = pl.pallas_call(
+    normed, gate, inv, inv_row, taps = pl.pallas_call(
         forward_kernel,
         out_shape=(
             shape((SECTIONS,) + FRAME_MAJOR),
             shape((SECTIONS,) + FRAME_MAJOR),
             shape((SECTIONS, FRAMES, PAD, LANES)),
+            shape((PAD, LANES)),
             shape((SECTIONS, 16, WIDE)),
         ),
         in_specs=[VMEM] * 5,
-        out_specs=(VMEM,) * 4,
+        out_specs=(VMEM,) * 5,
         scratch_shapes=[NATURAL] * 3,
         compiler_params=PARAMS,
         cost_estimate=cost(10**9, 6 * 10**6),
         name="sections_forward",
     )(parts, *sections)
-
-    outs = [shape(FRAME_MAJOR), shape(FRAME_MAJOR), shape((16, WIDE)), shape((MP, PAD, LANES))]
-    now = lambda t: [
-        at_hop(t, *FRAME_MAJOR),
-        at_hop(t, *FRAME_MAJOR),
-        at_hop(t, 16, WIDE),
-    ]
-    before = lambda t: [
-        whole(MP, PAD, LANES),
-        whole(*FRAME_MAJOR),
-        whole(*FRAME_MAJOR),
-        at_hop(t, *FRAME_MAJOR),
-        at_hop(t, FRAMES, PAD, LANES),
-    ]
-    tap_list = [None] * SECTIONS
-    result_list = [None] * SECTIONS
-    up, grad, tap_list[3], sums = section_call(
+    (matrices,) = local_call(
+        pair_kernel,
+        hops,
+        (normed, gate, taps),
+        [shape((2, MATRIX_ROWS, LANES))],
+        [NATURAL] * 3
+        + [
+            pltpu.VMEM((CLIPS * KERNEL * FRAMES, WIDE), BF16),
+            pltpu.VMEM((2 * LANES, WIDE), BF16),
+            pltpu.VMEM((16, WIDE), BF16),
+        ],
+        "pair_matrices",
+        cost(3 * 10**9, 6 * 10**6),
+    )
+
+    sums_shape = shape((MP, PAD + MATRIX_ROWS, LANES))
+    tap_shape = shape((16, WIDE))
+    up, tap_three, sums = local_call(
         head_kernel,
         hops,
-        (query_grad, head_weight, normed, gate, taps),
-        [whole(MP, 16, SLICE), whole(WIDE, EMB)] + now(3),
-        outs,
-        [ROW_TILE] * 2,
-        "head_and_section",
-    )
-    for t in (2, 1, 0):
-        sums = lax.all_to_all(sums, "mp", 0, 0)
-        result_list[t + 1], up, grad, tap_list[t], sums = section_call(
-            step_kernel,
-            hops,
-            (sums, up, grad, normed, inv, normed, gate, taps),
-            before(t + 1) + now(t),
-            [shape((ROWS, WIDE), BF16)] + outs,
-            [ROW_TILE] * 4 + [NATURAL],
-            "section_step",
-        )
-
-    tap_parts = jnp.stack(tap_list).astype(BF16).reshape(SECTIONS, DP, 5, LANES)
-    tap_parts = tap_parts.transpose(1, 0, 2, 3)
-    pair_parts = pair_grad[0:CLIPS].reshape(CLIPS, DP, MICRO * SHARD).transpose(1, 0, 2)
-    pair_parts = jnp.pad(pair_parts.reshape(DP, -1), ((0, 0), (0, 2 * LANES - CLIPS * MICRO * SHARD)))
-    pair_parts = jnp.broadcast_to(
-        pair_parts.reshape(DP, 1, 2, LANES), (DP, SECTIONS, 2, LANES)
-    )
-    message = jnp.concatenate([tap_parts, pair_parts], 2).reshape(DP * SECTIONS, 7, LANES)
-    message = jnp.pad(message, ((0, 0), (0, 1), (0, 0)))
-    message = lax.all_to_all(message, ("dp", "section"), 0, 0)
-
-    own = sums[0]
-    shifted = [own]
-    for steps in range(1, MP):
-        shifted.append(
-            lax.ppermute(own, "mp", [(source, (source + steps) % MP) for source in range(MP)])
-        )
-    sums = jnp.stack(shifted)
-    (result_list[0],) = section_call(
-        last_kernel,
+        (query_grad, head_weight, normed, gate, inv, taps, matrices),
+        [shape(FRAME_MAJOR), tap_shape, sums_shape],
+        [ROW_TILE] * 4 + [NATURAL],
+        "head_and_sections",
+    )
+    sums = lax.all_to_all(sums, "mp", 0, 0)
+    before, up, tap_two, tap_one, sums = local_call(
+        middle_kernel,
         hops,
-        (sums, up, grad, normed, inv),
-        before(0),
-        [shape((ROWS, WIDE), BF16)],
-        [ROW_TILE] * 2 + [NATURAL],
-        "section_end",
+        (sums, up, normed, gate, inv, inv_row, taps, matrices),
+        [shape((2, ROWS, WIDE), BF16), shape(FRAME_MAJOR), tap_shape, tap_shape, sums_shape],
+        [ROW_TILE] * 8 + [NATURAL],
+        "middle_sections",
+    )
+    sums = lax.all_to_all(sums, "mp", 0, 0)
+
+    pair_parts = pair_grad[0:CLIPS].astype(F32).reshape(CLIPS, DP, MICRO * SHARD)
+    pair_parts = pair_parts.transpose(1, 0, 2).reshape(DP, -1)
+    pair_parts = jnp.pad(pair_parts, ((0, 0), (0, 2 * LANES - CLIPS * MICRO * SHARD)))
+    pair_parts = pair_parts.reshape(DP, 2, LANES)
+    results_out, message = local_call(
+        end_kernel,
+        hops,
+        (sums, up, normed, gate, inv, inv_row, taps, before, tap_three, tap_two, tap_one, pair_parts),
+        [shape((SECTIONS, ROWS, WIDE), BF16), shape((DP * SECTIONS * PAD, LANES), BF16)],
+        [ROW_TILE] * 4
+        + [NATURAL, pltpu.VMEM((16, WIDE), F32), pltpu.VMEM((DP * SECTIONS, PAD, LANES), F32)],
+        "end_sections",
+    )
+    message = lax.all_to_all(
+        message.reshape(DP * SECTIONS, PAD, LANES), ("dp", "section"), 0, 0
     )
 
     tap_sum = jnp.sum(message[:, 0:5].astype(F32), axis=0).astype(BF16)
@@ -451,12 +570,10 @@
         * SCORE_SCALE
     ).reshape(MICRO, SHARD, SLICE)
 
-    stacked = jnp.stack(result_list)
     results = jnp.zeros(inputs_all.shape, BF16)
     for steps in range(SECTIONS):
-        target = (section_now + steps) % SECTIONS
         source = (section_now - steps) % SECTIONS
-        block = lax.dynamic_index_in_dim(stacked, target, 0, keepdims=False)
+        block = results_out[steps]
         block = rotate(block, steps) if steps else block
         block = block.reshape(MICRO, OWN, FRAMES, WIDE)
         results = lax.dynamic_update_slice_in_dim(results, block, OWN * source, 1)

time: 215 us -> 187 us (0.87)
  starting transfers between devices: 86.5 us -> 67.5 us
  local copies, waits for them, and re-layouts: 40.8 us -> 31.1 us
  waiting for transfers between devices: 34 us -> 43.3 us
  blocking collectives: 22 us -> 13.7 us
  Pallas kernels: 22.1 us -> 27.4 us
  other arithmetic: 5.77 us -> 1.36 us
    ppermute x3 -> x0, starting transfers between devices: 14.6 us -> none  [per_device(): lax.ppermute(own, 'mp', [(source, (source + steps) % MP) for source in ra...]
    all_to_all x1, waiting for transfers between devices: 0.01 us -> 12.3 us  [per_device(): lax.all_to_all(message.reshape(DP * SECTIONS, PAD, LANES), ('dp', 'sectio...]
    ppermute x6, waiting for transfers between devices: 17.8 us -> 7.81 us  [rotate(): return lax.ppermute(value, 'section', pairs)]
    all_to_all x2 -> x1, blocking collectives: 22 us -> 13.7 us  [per_device(): sums = lax.all_to_all(sums, 'mp', 0, 0)]
    all_to_all x1, waiting for transfers between devices: 0.01 us -> 7.01 us  [per_device(): sums = lax.all_to_all(sums, 'mp', 0, 0)]
    pallas_call x5 -> x4, Pallas kernels: 15 us -> 20.3 us  [local_call(): pl.pallas_call(kernel, out_shape=outs, in_specs=[SMEM] + [VMEM] * len(ope...]
    another operation x6 -> x0, other arithmetic: 3.25 us -> none
    all_to_all x1, starting transfers between devices: 7.95 us -> 4.81 us  [per_device(): lax.all_to_all(jnp.broadcast_to(tap_sum[None], (DP, 5, LANES)), 'dp', 0, 0)]
  transfers between devices with their start and end apart: 15 -> 12, of which waited for: 7 -> 7; matrix products, arithmetic and copies ran while one was open for 7% -> 1% of each run, Pallas kernels for 2% -> 6%
where the time goes in v2:
time: 187 us; the launch traced here: 186 us
  starting transfers between devices  67.5 us (36%)
  waiting for transfers between devices  43.3 us (23%)
  local copies, waits for them, and re-layouts  31.1 us (17%)
  Pallas kernels  27.4 us (15%)
  blocking collectives  13.7 us (7%)
    unnamed x79, local copies, waits for them, and re-layouts  25.4 us
    ppermute x6, starting transfers between devices, rotate(): return lax.ppermute(value, 'section', pairs)  21 us
    pallas_call x4, Pallas kernels, local_call(): pl.pallas_call(kernel, out_shape=outs, in_specs=[SMEM] + [VMEM] * len(ope...  20.3 us
    all_to_all x1, starting transfers between devices, per_device(): lax.all_to_all(message.reshape(DP * SECTIONS, PAD, LANES), ('dp', 'sectio...  14.8 us
    all_to_all x1, blocking collectives, per_device(): sums = lax.all_to_all(sums, 'mp', 0, 0)  13.7 us
    all_to_all x1, starting transfers between devices, per_device(): texts = lax.all_to_all(pairs, 'dp', 0, 0).reshape(TEXTS, 2 * SLICE)  13.1 us
    all_to_all x1, waiting for transfers between devices, per_device(): lax.all_to_all(message.reshape(DP * SECTIONS, PAD, LANES), ('dp', 'sectio...  12.3 us
    ppermute x6, waiting for transfers between devices, rotate(): return lax.ppermute(value, 'section', pairs)  7.81 us
  transfers between devices with their start and end apart: 12, of which 7 were waited for; matrix products, arithmetic and copies ran while one was open for 1% of the time, Pallas kernels for 6%

profile of v2, /device:TPU:1, one launch (start us, length us, event | category | flops | bytes accessed | tf_op | source)
XLA Modules:
  0.0 185.9 jit_solution(7202180982067795988)
XLA Ops:
  2.5 13.1 %all-to-all-start = ((bf16[32,24,512]{2,1,0:T(8,128)(2,1)}), bf16[32,24,512]{2,1,0:T(8,128)(2,1)S(1)}, u32[]{:S(2)}, u32[]{:S(2)}) async-start(bf16[32,24,512]{2,1,0:T(8,128)(2,1)} %broadcast_in_dim.43), calls=%async_computation | async-start | bytes 1572864 | tf_op jit(solution)/shard_map/all_to_all | solution.py:454
  15.9 3.1 %collective-permute-start = (bf16[112,1280]{1,0:T(8,128)(2,1)S(1)}, bf16[112,1280]{1,0:T(8,128)(2,1)S(1)}, u32[]{:S(2)}, u32[]{:S(2)}) collective-permute-start(bf16[112,1280]{1,0:T(8,128)(2,1)S(1)} %get-tuple-element.58), channel_id=1, source_target_pairs={{0,4},{4,8},{8,12},{12,0},{1,5},{5,9},{9,13},{13,1},{2,6},{6,10},{... | collective-permute-start | bytes 860168 | tf_op jit(solution)/shard_map/ppermute | solution.py:434
  19.0 4.4 %collective-permute-start.1 = (bf16[112,1280]{1,0:T(8,128)(2,1)S(1)}, bf16[112,1280]{1,0:T(8,128)(2,1)S(1)}, u32[]{:S(2)}, u32[]{:S(2)}) collective-permute-start(bf16[112,1280]{1,0:T(8,128)(2,1)S(1)} %get-tuple-element.59), channel_id=1, source_target_pairs={{0,8},{4,12},{8,0},{12,4},{1,9},{5,13},{9,1},{13,5},{2,10},{6,14},... | collective-permute-start | bytes 860168 | tf_op jit(solution)/shard_map/ppermute | solution.py:434
  23.4 3.1 %collective-permute-start.2 = (bf16[112,1280]{1,0:T(8,128)(2,1)S(1)}, bf16[112,1280]{1,0:T(8,128)(2,1)S(1)}, u32[]{:S(2)}, u32[]{:S(2)}) collective-permute-start(bf16[112,1280]{1,0:T(8,128)(2,1)S(1)} %get-tuple-element.57), channel_id=1, source_target_pairs={{0,12},{4,0},{8,4},{12,8},{1,13},{5,1},{9,5},{13,9},{2,14},{6,2},{... | collective-permute-start | bytes 860168 | tf_op jit(solution)/shard_map/ppermute | solution.py:434
  27.7 6.6 %collective-permute-done.1.x2 = bf16[112,1280]{1,0:T(8,128)(2,1)S(1)} collective-permute-done((bf16[112,1280]{1,0:T(8,128)(2,1)S(1)}, bf16[112,1280]{1,0:T(8,128)(2,1)S(1)}, u32[]{:S(2)}, u32[]{:S(2)}) %collective-permute-start.1) | collective-permute-done | bytes 286752 | tf_op jit(solution)/shard_map/ppermute | solution.py:434
  34.4 1.2 collective-permute-done.2.x3
  35.5 1.6 all-to-all-done
  37.1 1.5 row_sums_and_scores.1
  38.6 5.9 %all-to-all-start.1 = ((f32[4,8,896]{2,1,0:T(8,128)}), f32[4,8,896]{2,1,0:T(8,128)S(1)}, u32[]{:S(2)}, u32[]{:S(2)}) async-start(f32[4,8,896]{2,1,0:T(8,128)} %row_sums_and_scores.1), calls=%async_computation.1 | async-start | bytes 229376 | tf_op jit(solution)/shard_map/all_to_all | solution.py:478
  44.6 7.6 %all-to-all-done.1.parts = f32[4,8,896]{2,1,0:T(8,128)S(1)} async-done(((f32[4,8,896]{2,1,0:T(8,128)}), f32[4,8,896]{2,1,0:T(8,128)S(1)}, u32[]{:S(2)}, u32[]{:S(2)}) %all-to-all-start.1) | async-done | bytes 114720 | tf_op jit(solution)/shard_map/all_to_all | solution.py:478
  53.9 3.9 %all-to-all-start.2 = ((bf16[4,16,256]{2,1,0:T(8,128)(2,1)}), bf16[4,16,256]{2,1,0:T(8,128)(2,1)}, u32[]{:S(2)}, u32[]{:S(2)}) async-start(bf16[4,16,256]{2,1,0:T(8,128)(2,1)} %get-tuple-element.20), calls=%async_computation.2 | async-start | bytes 65536 | tf_op jit(solution)/shard_map/all_to_all | solution.py:488
  61.6 4.6 %sections_forward.1 = (f32[4,10,16,8,128]{4,3,2,1,0:T(8,128)S(1)}, f32[4,10,16,8,128]{4,3,2,1,0:T(8,128)S(1)}, f32[4,16,8,128]{3,2,1,0:T(8,128)S(1)}, f32[8,128]{1,0:T(8,128)S(1)}, f32[4,16,1280]{2,1,0:T(8,128)S(1)}) custom-call(f32[4,8,896]{2,1,0:T(8,128)S(1)} %all-to-all-done.1.parts, bf16[112,1280]{1,0:T(8,128)(2,1)S(1)} %copy-done.13, ...), custom_call_target="tpu_custom_call" | custom-call | flops 1000000000 | bytes 6000000 | tf_op jit(solution)/shard_map/sections_forward/pallas_call | solution.py:490
  66.9 6.2 %pair_matrices.1.matrices = f32[2,64,128]{2,1,0:T(8,128)S(1)} custom-call(s32[4]{0:T(128)S(1)} %pad_add_fusion.hops, f32[4,10,16,8,128]{4,3,2,1,0:T(8,128)S(1)} %get-tuple-element.21.normed, f32[4,10,16,8,128]{4,3,2,1,0:T(8,128)S(1)} %get-tuple-element.22.gate, f32[4,16,1280]{2,1,0:T(8,128)S(1)} %get-tuple-element.24.taps_in), custom_call_target="tpu_custom_call" | custom-call | flops 3000000000 | bytes 6000000 | tf_op jit(solution)/shard_map/pair_matrices/pallas_call | solution.py:420
  73.1 1.5 copy-done.1
  75.3 1.7 copy-done.2
  78.0 1.7 copy-done.8
  80.7 5.2 %head_and_sections.1 = (f32[10,16,8,128]{3,2,1,0:T(8,128)S(1)}, f32[16,1280]{1,0:T(8,128)S(1)}, f32[4,72,128]{2,1,0:T(8,128)S(1)}) custom-call(s32[4]{0:T(128)S(1)} %pad_add_fusion.hops, bf16[4,16,256]{2,1,0:T(8,128)(2,1)} %all-to-all-done.2.query_grad, bf16[1280,1024]{1,0:T(8,128)(2,1)S(1)} %copy-done.8, ...), custom_call_target="tpu_custom_call" | custom-call | tf_op jit(solution)/shard_map/head_and_sections/pallas_call | solution.py:420
  85.9 13.7 %all_to_all.35.parts = f32[4,72,128]{2,1,0:T(8,128)S(1)} all-to-all(f32[4,72,128]{2,1,0:T(8,128)S(1)} %get-tuple-element.25), channel_id=1, replica_groups=mesh['dp'=32,'section'=4,'mp'=4] {'mp'}, dimensions={0} | all-to-all | bytes 294912 | tf_op jit(solution)/shard_map/all_to_all | solution.py:531
  99.6 5.4 %middle_sections.1 = (bf16[2,96,1280]{2,1,0:T(8,128)(2,1)S(1)}, f32[10,16,8,128]{3,2,1,0:T(8,128)S(1)}, f32[16,1280]{1,0:T(8,128)S(1)}, f32[16,1280]{1,0:T(8,128)S(1)}, f32[4,72,128]{2,1,0:T(8,128)S(1)}) custom-call(s32[4]{0:T(128)S(1)} %pad_add_fusion.hops, f32[4,72,128]{2,1,0:T(8,128)S(1)} %all_to_all.35.parts, ...), custom_call_target="tpu_custom_call" | custom-call | tf_op jit(solution)/shard_map/middle_sections/pallas_call | solution.py:420
  108.6 4.0 %all-to-all-start.4 = ((f32[4,72,128]{2,1,0:T(8,128)}), f32[4,72,128]{2,1,0:T(8,128)}, u32[]{:S(2)}, u32[]{:S(2)}) async-start(f32[4,72,128]{2,1,0:T(8,128)} %copy-done.25), calls=%async_computation.4 | async-start | bytes 294912 | tf_op jit(solution)/shard_map/all_to_all | solution.py:540
  113.0 7.0 %all-to-all-done.4.parts = f32[4,72,128]{2,1,0:T(8,128)} async-done(((f32[4,72,128]{2,1,0:T(8,128)}), f32[4,72,128]{2,1,0:T(8,128)}, u32[]{:S(2)}, u32[]{:S(2)}) %all-to-all-start.4) | async-done | bytes 147488 | tf_op jit(solution)/shard_map/all_to_all | solution.py:540
  120.0 1.7 copy-done.3
  123.7 1.1 copy-done.15
  124.7 1.0 copy-done.17
  128.4 3.6 %end_sections.1 = (bf16[4,96,1280]{2,1,0:T(8,128)(2,1)S(1)}, bf16[1024,128]{1,0:T(8,128)(2,1)S(1)}) custom-call(s32[4]{0:T(128)S(1)} %pad_add_fusion.hops, f32[4,72,128]{2,1,0:T(8,128)} %all-to-all-done.4.parts, f32[10,16,8,128]{3,2,1,0:T(8,128)S(1)} %copy-done.15, f32[4,10,16,8,128]{4,3,2,1,0:T(8,128)S(1)} %get-tuple-element.21.normed, ...), custom_call_target="tpu_custom_call" | custom-call | tf_op jit(solution)/shard_map/end_sections/pallas_call | solution.py:420
  132.8 3.8 %collective-permute-start.3 = (bf16[96,1280]{1,0:T(8,128)(2,1)}, bf16[96,1280]{1,0:T(8,128)(2,1)S(1)}, u32[]{:S(2)}, u32[]{:S(2)}) collective-permute-start(bf16[96,1280]{1,0:T(8,128)(2,1)} %get-tuple-element.51), channel_id=1, source_target_pairs={{0,4},{4,8},{8,12},{12,0},{1,5},{5,9},{9,13},{13,1},{2,6},{6,10},{... | collective-permute-start | bytes 737288 | tf_op jit(solution)/shard_map/ppermute | solution.py:434
  136.7 4.1 %collective-permute-start.4 = (bf16[96,1280]{1,0:T(8,128)(2,1)S(1)}, bf16[96,1280]{1,0:T(8,128)(2,1)S(1)}, u32[]{:S(2)}, u32[]{:S(2)}) collective-permute-start(bf16[96,1280]{1,0:T(8,128)(2,1)S(1)} %get-tuple-element.50), channel_id=1, source_target_pairs={{0,8},{4,12},{8,0},{12,4},{1,9},{5,13},{9,1},{13,5},{2,10},{6,14},... | collective-permute-start | bytes 737288 | tf_op jit(solution)/shard_map/ppermute | solution.py:434
  140.8 2.6 %collective-permute-start.5 = (bf16[96,1280]{1,0:T(8,128)(2,1)S(1)}, bf16[96,1280]{1,0:T(8,128)(2,1)S(1)}, u32[]{:S(2)}, u32[]{:S(2)}) collective-permute-start(bf16[96,1280]{1,0:T(8,128)(2,1)S(1)} %get-tuple-element.49), channel_id=1, source_target_pairs={{0,12},{4,0},{8,4},{12,8},{1,13},{5,1},{9,5},{13,9},{2,14},{6,2},{... | collective-permute-start | bytes 737288 | tf_op jit(solution)/shard_map/ppermute | solution.py:434
  143.3 14.8 %all-to-all-start.5 = ((bf16[128,8,128]{2,1,0:T(8,128)(2,1)}), bf16[128,8,128]{2,1,0:T(8,128)(2,1)S(1)}, u32[]{:S(2)}, u32[]{:S(2)}) async-start(bf16[128,8,128]{2,1,0:T(8,128)(2,1)} %bitcast.31), calls=%async_computation.5 | async-start | bytes 524288 | tf_op jit(solution)/shard_map/all_to_all | solution.py:555
  158.4 12.3 %all-to-all-done.5 = bf16[128,8,128]{2,1,0:T(8,128)(2,1)S(1)} async-done(((bf16[128,8,128]{2,1,0:T(8,128)(2,1)}), bf16[128,8,128]{2,1,0:T(8,128)(2,1)S(1)}, u32[]{:S(2)}, u32[]{:S(2)}) %all-to-all-start.5) | async-done | bytes 262176 | tf_op jit(solution)/shard_map/all_to_all | solution.py:555
  172.4 4.8 %all-to-all-start.6 = ((bf16[32,5,128]{2,1,0:T(8,128)(2,1)}), bf16[32,5,128]{2,1,0:T(8,128)(2,1)S(1)}, u32[]{:S(2)}, u32[]{:S(2)}) async-start(bf16[32,5,128]{2,1,0:T(8,128)(2,1)} %broadcast_in_dim.50), calls=%async_computation.6 | async-start | bytes 131072 | tf_op jit(solution)/shard_map/all_to_all | solution.py:560
  178.1 7.1 %all-to-all-done.6 = bf16[32,5,128]{2,1,0:T(8,128)(2,1)S(1)} async-done(((bf16[32,5,128]{2,1,0:T(8,128)(2,1)}), bf16[32,5,128]{2,1,0:T(8,128)(2,1)S(1)}, u32[]{:S(2)}, u32[]{:S(2)}) %all-to-all-start.6) | async-done | bytes 40992 | tf_op jit(solution)/shard_map/all_to_all | solution.py:560
  (126 shorter events, 24.8 us)
Async XLA Ops:
  0.6 26.8 %copy-start = (f32[2,12]{1,0:T(2,128)S(1)}, f32[2,12]{1,0:T(2,128)}, u32[]{:S(2)}) copy-start(f32[2,12]{1,0:T(2,128)} %param.15) | copy-start | bytes 292
  0.6 15.0 %copy-start.37 = (f32[1,1280]{1,0:T(1,128)S(1)}, f32[1,1280]{1,0:T(1,128)}, u32[]{:S(2)}) copy-start(f32[1,1280]{1,0:T(1,128)} %param.9) | copy-start | bytes 15364
  0.7 15.1 %copy-start.34 = (bf16[1,2,12,16,1280]{4,3,2,1,0:T(8,128)(2,1)S(1)}, bf16[1,2,12,16,1280]{4,3,2,1,0:T(8,128)(2,1)}, u32[]{:S(2)}) copy-start(bf16[1,2,12,16,1280]{4,3,2,1,0:T(8,128)(2,1)} %param.8) | copy-start | bytes 2949124
  0.7 15.1 %copy-start.36 = (bf16[1,15,1280]{2,1,0:T(8,128)(2,1)S(1)}, bf16[1,15,1280]{2,1,0:T(8,128)(2,1)}, u32[]{:S(2)}) copy-start(bf16[1,15,1280]{2,1,0:T(8,128)(2,1)} %param.10) | copy-start | bytes 115204
  2.5 24.8 %copy-start.38 = (s32[2,12]{1,0:T(2,128)S(1)}, s32[2,12]{1,0:T(2,128)}, u32[]{:S(2)}) copy-start(s32[2,12]{1,0:T(2,128)} %param.14) | copy-start | bytes 292
  2.5 34.6 %all-to-all-start = ((bf16[32,24,512]{2,1,0:T(8,128)(2,1)}), bf16[32,24,512]{2,1,0:T(8,128)(2,1)S(1)}, u32[]{:S(2)}, u32[]{:S(2)}) async-start(bf16[32,24,512]{2,1,0:T(8,128)(2,1)} %broadcast_in_dim.43), calls=%async_computation | async-start | bytes 1572864 | tf_op jit(solution)/shard_map/all_to_all | solution.py:454
  15.9 37.4 %copy-start.12 = (bf16[112,1280]{1,0:T(8,128)(2,1)}, bf16[112,1280]{1,0:T(8,128)(2,1)S(1)}, u32[]{:S(2)}) copy-start(bf16[112,1280]{1,0:T(8,128)(2,1)S(1)} %get-tuple-element.60.x0) | copy-start | bytes 860164
  15.9 11.8 %collective-permute-start = (bf16[112,1280]{1,0:T(8,128)(2,1)S(1)}, bf16[112,1280]{1,0:T(8,128)(2,1)S(1)}, u32[]{:S(2)}, u32[]{:S(2)}) collective-permute-start(bf16[112,1280]{1,0:T(8,128)(2,1)S(1)} %get-tuple-element.58), channel_id=1, source_target_pairs={{0,4},{4,8},{8,12},{12,0},{1,5},{5,9},{9,13},{13,1},{2,6},{6,10},{... | collective-permute-start | bytes 860168 | tf_op jit(solution)/shard_map/ppermute | solution.py:434
  19.0 15.3 %collective-permute-start.1 = (bf16[112,1280]{1,0:T(8,128)(2,1)S(1)}, bf16[112,1280]{1,0:T(8,128)(2,1)S(1)}, u32[]{:S(2)}, u32[]{:S(2)}) collective-permute-start(bf16[112,1280]{1,0:T(8,128)(2,1)S(1)} %get-tuple-element.59), channel_id=1, source_target_pairs={{0,8},{4,12},{8,0},{12,4},{1,9},{5,13},{9,1},{13,5},{2,10},{6,14},... | collective-permute-start | bytes 860168 | tf_op jit(solution)/shard_map/ppermute | solution.py:434
  23.4 12.1 %collective-permute-start.2 = (bf16[112,1280]{1,0:T(8,128)(2,1)S(1)}, bf16[112,1280]{1,0:T(8,128)(2,1)S(1)}, u32[]{:S(2)}, u32[]{:S(2)}) collective-permute-start(bf16[112,1280]{1,0:T(8,128)(2,1)S(1)} %get-tuple-element.57), channel_id=1, source_target_pairs={{0,12},{4,0},{8,4},{12,8},{1,13},{5,1},{9,5},{13,9},{2,14},{6,2},{... | collective-permute-start | bytes 860168 | tf_op jit(solution)/shard_map/ppermute | solution.py:434
  27.7 25.5 %copy-start.18 = (bf16[112,1280]{1,0:T(8,128)(2,1)}, bf16[112,1280]{1,0:T(8,128)(2,1)S(1)}, u32[]{:S(2)}) copy-start(bf16[112,1280]{1,0:T(8,128)(2,1)S(1)} %collective-permute-done.x1) | copy-start | bytes 860164
  34.4 18.9 %copy-start.20 = (bf16[112,1280]{1,0:T(8,128)(2,1)}, bf16[112,1280]{1,0:T(8,128)(2,1)S(1)}, u32[]{:S(2)}) copy-start(bf16[112,1280]{1,0:T(8,128)(2,1)S(1)} %collective-permute-done.1.x2) | copy-start | bytes 860164
  35.5 17.7 %copy-start.22 = (bf16[112,1280]{1,0:T(8,128)(2,1)}, bf16[112,1280]{1,0:T(8,128)(2,1)S(1)}, u32[]{:S(2)}) copy-start(bf16[112,1280]{1,0:T(8,128)(2,1)S(1)} %collective-permute-done.2.x3) | copy-start | bytes 860164
  38.6 13.5 %all-to-all-start.1 = ((f32[4,8,896]{2,1,0:T(8,128)}), f32[4,8,896]{2,1,0:T(8,128)S(1)}, u32[]{:S(2)}, u32[]{:S(2)}) async-start(f32[4,8,896]{2,1,0:T(8,128)} %row_sums_and_scores.1), calls=%async_computation.1 | async-start | bytes 229376 | tf_op jit(solution)/shard_map/all_to_all | solution.py:478
  53.9 21.4 %all-to-all-start.2 = ((bf16[4,16,256]{2,1,0:T(8,128)(2,1)}), bf16[4,16,256]{2,1,0:T(8,128)(2,1)}, u32[]{:S(2)}, u32[]{:S(2)}) async-start(bf16[4,16,256]{2,1,0:T(8,128)(2,1)} %get-tuple-element.20), calls=%async_computation.2 | async-start | bytes 65536 | tf_op jit(solution)/shard_map/all_to_all | solution.py:488
  73.1 1.5 copy-start.1
  75.3 1.7 copy-start.2
  78.0 1.7 copy-start.8
  80.7 18.9 %copy-start.6 = (f32[4,16,1280]{2,1,0:T(8,128)S(1)}, f32[4,16,1280]{2,1,0:T(8,128)}, u32[]{:S(2)}) copy-start(f32[4,16,1280]{2,1,0:T(8,128)} %copy-done.4) | copy-start | bytes 983044
  85.9 19.2 %copy-start.26 = (f32[16,1280]{1,0:T(8,128)}, f32[16,1280]{1,0:T(8,128)S(1)}, u32[]{:S(2)}) copy-start(f32[16,1280]{1,0:T(8,128)S(1)} %get-tuple-element.31.tap_three) | copy-start | bytes 245764
  99.6 13.0 %copy-start.33 = (bf16[16,768]{1,0:T(8,128)(2,1)S(1)}, bf16[16,768]{1,0:T(8,128)(2,1)}, u32[]{:S(2)}) copy-start(bf16[16,768]{1,0:T(8,128)(2,1)} %copy-done.32) | copy-start | bytes 73732
  108.6 11.3 %all-to-all-start.4 = ((f32[4,72,128]{2,1,0:T(8,128)}), f32[4,72,128]{2,1,0:T(8,128)}, u32[]{:S(2)}, u32[]{:S(2)}) async-start(f32[4,72,128]{2,1,0:T(8,128)} %copy-done.25), calls=%async_computation.4 | async-start | bytes 294912 | tf_op jit(solution)/shard_map/all_to_all | solution.py:540
  120.0 1.7 copy-start.3
  121.7 1.0 copy-start.7
  123.7 1.1 copy-start.15
  124.7 1.0 copy-start.17
  132.8 25.4 %collective-permute-start.3 = (bf16[96,1280]{1,0:T(8,128)(2,1)}, bf16[96,1280]{1,0:T(8,128)(2,1)S(1)}, u32[]{:S(2)}, u32[]{:S(2)}) collective-permute-start(bf16[96,1280]{1,0:T(8,128)(2,1)} %get-tuple-element.51), channel_id=1, source_target_pairs={{0,4},{4,8},{8,12},{12,0},{1,5},{5,9},{9,13},{13,1},{2,6},{6,10},{... | collective-permute-start | bytes 737288 | tf_op jit(solution)/shard_map/ppermute | solution.py:434
  136.7 21.6 %collective-permute-start.4 = (bf16[96,1280]{1,0:T(8,128)(2,1)S(1)}, bf16[96,1280]{1,0:T(8,128)(2,1)S(1)}, u32[]{:S(2)}, u32[]{:S(2)}) collective-permute-start(bf16[96,1280]{1,0:T(8,128)(2,1)S(1)} %get-tuple-element.50), channel_id=1, source_target_pairs={{0,8},{4,12},{8,0},{12,4},{1,9},{5,13},{9,1},{13,5},{2,10},{6,14},... | collective-permute-start | bytes 737288 | tf_op jit(solution)/shard_map/ppermute | solution.py:434
  140.8 17.5 %collective-permute-start.5 = (bf16[96,1280]{1,0:T(8,128)(2,1)S(1)}, bf16[96,1280]{1,0:T(8,128)(2,1)S(1)}, u32[]{:S(2)}, u32[]{:S(2)}) collective-permute-start(bf16[96,1280]{1,0:T(8,128)(2,1)S(1)} %get-tuple-element.49), channel_id=1, source_target_pairs={{0,12},{4,0},{8,4},{12,8},{1,13},{5,1},{9,5},{13,9},{2,14},{6,2},{... | collective-permute-start | bytes 737288 | tf_op jit(solution)/shard_map/ppermute | solution.py:434
  143.3 27.3 %all-to-all-start.5 = ((bf16[128,8,128]{2,1,0:T(8,128)(2,1)}), bf16[128,8,128]{2,1,0:T(8,128)(2,1)S(1)}, u32[]{:S(2)}, u32[]{:S(2)}) async-start(bf16[128,8,128]{2,1,0:T(8,128)(2,1)} %bitcast.31), calls=%async_computation.5 | async-start | bytes 524288 | tf_op jit(solution)/shard_map/all_to_all | solution.py:555
  158.3 27.5 %copy-start.35 = (bf16[1,2,12,16,1280]{4,3,2,1,0:T(8,128)(2,1)}, bf16[1,2,12,16,1280]{4,3,2,1,0:T(8,128)(2,1)S(1)}, u32[]{:S(2)}) copy-start(bf16[1,2,12,16,1280]{4,3,2,1,0:T(8,128)(2,1)S(1)} %constant_dynamic-update-slice_fusion) | copy-start | bytes 2949124
  172.4 12.8 %all-to-all-start.6 = ((bf16[32,5,128]{2,1,0:T(8,128)(2,1)}), bf16[32,5,128]{2,1,0:T(8,128)(2,1)S(1)}, u32[]{:S(2)}, u32[]{:S(2)}) async-start(bf16[32,5,128]{2,1,0:T(8,128)(2,1)} %broadcast_in_dim.50), calls=%async_computation.6 | async-start | bytes 131072 | tf_op jit(solution)/shard_map/all_to_all | solution.py:560
  (19 other events, 15.8 us)

commit v3 on v2

--- a/solution.py
+++ b/solution.py
@@ -50,7 +50,7 @@
     return jnp.broadcast_to(turned[:, 0:1], (LANES, LANES))
 
 
-def sums_kernel(x0, x1, x2, x3, texts, query, out):
+def sums_kernel(hops, positives, weights, x0, x1, x2, x3, texts, query, out):
     rows = []
     for x in (x0, x1, x2, x3):
         total = jnp.zeros((ROWS, LANES), F32)
@@ -71,22 +71,48 @@
         out[peer, :, TEXTS:] = stats
 
 
-def softmax_kernel(parts, texts, valid, positive, weight, query_grad, pair_grad):
+def softmax_kernel(
+    hops, positives, weights, parts, texts, query_grad, pair_parts
+):
     scores = parts[0, :, 0:TEXTS]
     for peer in range(1, MP):
         scores = scores + parts[peer, :, 0:TEXTS]
-    scores = jnp.where(valid[...] > 0.0, scores * SCORE_SCALE, -1e30)
+    row = lax.broadcasted_iota(jnp.int32, (PAD, TEXTS), 0)
+    column = lax.broadcasted_iota(jnp.int32, (PAD, TEXTS), 1)
+    text_micro = ((column * 10923) >> 17) & 1
+    clip_micro = jnp.where(row >= OWN, 1, 0)
+    scores = jnp.where(text_micro == clip_micro, scores * SCORE_SCALE, -1e30)
     exp_scores = jnp.exp(scores - jnp.max(scores, axis=1, keepdims=True))
     probs = exp_scores / jnp.sum(exp_scores, axis=1, keepdims=True)
-    column = lax.broadcasted_iota(jnp.int32, (PAD, TEXTS), 1)
-    hot = jnp.where(column == positive[:, 0:1], 1.0, 0.0)
-    grad = weight[:, 0:1] * (probs - hot)
+    base = hops[SECTIONS] * OWN
+    positive = jnp.full((PAD, TEXTS), -1, jnp.int32)
+    weight = jnp.zeros((PAD, TEXTS), F32)
+    for micro in range(MICRO):
+        for own in range(OWN):
+            index = positives[micro, base + own]
+            owner = (index * 10923) >> 17
+            index = owner * (MICRO * SHARD) + micro * SHARD + (index - owner * SHARD)
+            here = row == micro * OWN + own
+            positive = jnp.where(here, index, positive)
+            weight = jnp.where(here, weights[micro, base + own], weight)
+    hot = jnp.where(column == positive, 1.0, 0.0)
+    grad = weight * (probs - hot)
     grad = jnp.concatenate([grad, jnp.zeros((PAD, TEXTS), F32)], 0).astype(BF16)
-    pair_grad[...] = grad
     result = jnp.dot(grad, texts[:, 0:SLICE], preferred_element_type=F32) * SCORE_SCALE
     result = result.astype(BF16)
     for peer in range(MP):
         query_grad[peer] = result
+    grad = grad.astype(F32)
+    gap = jnp.zeros((1, 32 - MICRO * SHARD), F32)
+    tail = jnp.zeros((1, LANES - OWN * 32), F32)
+    for target in range(DP):
+        start = target * MICRO * SHARD
+        for micro in range(MICRO):
+            pieces = []
+            for own in range(OWN):
+                clip = micro * OWN + own
+                pieces += [grad[clip : clip + 1, start : start + MICRO * SHARD], gap]
+            pair_parts[target, micro : micro + 1, :] = jnp.concatenate(pieces + [tail], 1)
 
 
 def spread(row, rows_out, natural):
@@ -96,7 +122,7 @@
 
 
 def forward_kernel(
-    parts, x0, x1, x2, x3,
+    query_grad, parts, x0, x1, x2, x3,
     normed_out, gate_out, inv_out, inv_row_out, taps_out,
     natural, mean_rows, inv_rows,
 ):
@@ -438,7 +464,8 @@
     saved_inputs, norm_gains, conv_taps, head_weight, queries, key_embeds, positives, pair_weights
 ):
     section_now = lax.axis_index("section")
-    hops = jnp.stack([(section_now - t) % SECTIONS for t in range(SECTIONS)]).astype(jnp.int32)
+    hops = [(section_now - t) % SECTIONS for t in range(SECTIONS)] + [section_now]
+    hops = jnp.stack(hops).astype(jnp.int32)
     inputs_all = saved_inputs[0]
 
     small = jnp.concatenate([conv_taps[0], norm_gains.astype(BF16)], 0)
@@ -455,36 +482,25 @@
 
     own_queries = lax.dynamic_slice_in_dim(queries, OWN * section_now, OWN, 1)
     own_queries = jnp.pad(own_queries.reshape(CLIPS, SLICE), ((0, 16 - CLIPS), (0, 0)))
-    own_positives = lax.dynamic_slice_in_dim(positives, OWN * section_now, OWN, 1)
-    own_weights = lax.dynamic_slice_in_dim(pair_weights, OWN * section_now, OWN, 1)
-    micro = jnp.arange(MICRO, dtype=jnp.int32)[:, None]
-    column = (own_positives // SHARD) * (MICRO * SHARD) + micro * SHARD + own_positives % SHARD
-    column = jnp.pad(column.reshape(CLIPS), (0, PAD - CLIPS), constant_values=-1)
-    column = jnp.broadcast_to(column[:, None], (PAD, LANES))
-    own_weights = jnp.pad(own_weights.reshape(CLIPS), (0, PAD - CLIPS))
-    own_weights = jnp.broadcast_to(own_weights[:, None], (PAD, LANES))
-    text_micro = (jnp.arange(TEXTS) // SHARD) % MICRO
-    clip_micro = jnp.minimum(jnp.arange(PAD) // OWN, MICRO - 1)
-    valid = (clip_micro[:, None] == text_micro[None, :]).astype(F32)
 
     parts = pl.pallas_call(
         sums_kernel,
         out_shape=shape((MP, PAD, TEXTS + LANES)),
-        in_specs=[VMEM] * 6,
+        in_specs=[SMEM] * 3 + [VMEM] * 6,
         out_specs=VMEM,
         compiler_params=PARAMS,
         name="row_sums_and_scores",
-    )(*sections, texts, own_queries)
+    )(hops, positives, pair_weights, *sections, texts, own_queries)
     parts = lax.all_to_all(parts, "mp", 0, 0)
 
-    query_grad, pair_grad = pl.pallas_call(
+    query_grad, pair_parts = pl.pallas_call(
         softmax_kernel,
-        out_shape=(shape((MP, 16, SLICE), BF16), shape((16, TEXTS), BF16)),
-        in_specs=[VMEM] * 5,
+        out_shape=(shape((MP, 16, SLICE), BF16), shape((DP, MICRO, LANES))),
+        in_specs=[SMEM] * 3 + [VMEM] * 2,
         out_specs=(VMEM, VMEM),
         compiler_params=PARAMS,
         name="softmax_grads",
-    )(parts, texts, valid, column, own_weights)
+    )(hops, positives, pair_weights, parts, texts)
     query_grad = lax.all_to_all(query_grad, "mp", 0, 0)
 
     normed, gate, inv, inv_row, taps = pl.pallas_call(
@@ -496,13 +512,13 @@
             shape((PAD, LANES)),
             shape((SECTIONS, 16, WIDE)),
         ),
-        in_specs=[VMEM] * 5,
+        in_specs=[VMEM] * 6,
         out_specs=(VMEM,) * 5,
         scratch_shapes=[NATURAL] * 3,
         compiler_params=PARAMS,
         cost_estimate=cost(10**9, 6 * 10**6),
         name="sections_forward",
-    )(parts, *sections)
+    )(query_grad, parts, *sections)
     (matrices,) = local_call(
         pair_kernel,
         hops,
@@ -539,10 +555,6 @@
     )
     sums = lax.all_to_all(sums, "mp", 0, 0)
 
-    pair_parts = pair_grad[0:CLIPS].astype(F32).reshape(CLIPS, DP, MICRO * SHARD)
-    pair_parts = pair_parts.transpose(1, 0, 2).reshape(DP, -1)
-    pair_parts = jnp.pad(pair_parts, ((0, 0), (0, 2 * LANES - CLIPS * MICRO * SHARD)))
-    pair_parts = pair_parts.reshape(DP, 2, LANES)
     results_out, message = local_call(
         end_kernel,
         hops,
@@ -560,8 +572,8 @@
     tap_grads = lax.all_to_all(jnp.broadcast_to(tap_sum[None], (DP, 5, LANES)), "dp", 0, 0)
     tap_grads = tap_grads.reshape(16, WIDE)[0:KERNEL].astype(F32)
 
-    columns = message[:, 5:7].reshape(DP, SECTIONS, 2 * LANES)[..., : CLIPS * MICRO * SHARD]
-    columns = columns.reshape(DP, SECTIONS, MICRO, OWN, MICRO * SHARD)
+    columns = message[:, 5:7].reshape(DP, SECTIONS, MICRO, LANES)[..., : OWN * 32]
+    columns = columns.reshape(DP, SECTIONS, MICRO, OWN, 32)[..., : MICRO * SHARD]
     columns = columns.transpose(0, 2, 1, 3, 4).reshape(TEXTS, MICRO * SHARD)
     key_grads = (
         lax.dot_general(
@@ -570,7 +582,7 @@
         * SCORE_SCALE
     ).reshape(MICRO, SHARD, SLICE)
 
-    results = jnp.zeros(inputs_all.shape, BF16)
+    results = jnp.broadcast_to(results_out[0, 0, 0], inputs_all.shape)
     for steps in range(SECTIONS):
         source = (section_now - steps) % SECTIONS
         block = results_out[steps]

time: 187 us -> 163 us (0.87)
  blocking collectives: 13.7 us -> 41.7 us
  local copies, waits for them, and re-layouts: 31.1 us -> 5.86 us
  waiting for transfers between devices: 43.3 us -> 24.7 us
  starting transfers between devices: 67.5 us -> 60.1 us
    unnamed x79 -> x16, local copies, waits for them, and re-layouts: 25.4 us -> 0.68 us
    all_to_all x0 -> x2, blocking collectives: none -> 22.2 us  [the longest x1 13.1 us: per_device(): parts = lax.all_to_all(parts, 'mp', 0, 0)]
    all_to_all x3 -> x0, waiting for transfers between devices: 14.6 us -> none  [the longest x1 7.56 us: per_device(): parts = lax.all_to_all(parts, 'mp', 0, 0)]
    all_to_all x3 -> x0, starting transfers between devices: 13.8 us -> none  [the longest x1 5.91 us: per_device(): parts = lax.all_to_all(parts, 'mp', 0, 0)]
    all_to_all x1, waiting for transfers between devices: 12.3 us -> 0.01 us  [per_device(): lax.all_to_all(message.reshape(DP * SECTIONS, PAD, LANES), ('dp', 'sectio...]
    ppermute x6, waiting for transfers between devices: 7.81 us -> 17.3 us  [rotate(): return lax.ppermute(value, 'section', pairs)]
    all_to_all x1 -> x2, blocking collectives: 13.7 us -> 19.5 us  [per_device(): sums = lax.all_to_all(sums, 'mp', 0, 0)]
    all_to_all x1, starting transfers between devices: 4.81 us -> 9.24 us  [per_device(): lax.all_to_all(jnp.broadcast_to(tap_sum[None], (DP, 5, LANES)), 'dp', 0, 0)]
  transfers between devices with their start and end apart: 12 -> 9, of which waited for: 7 -> 5; matrix products, arithmetic and copies ran while one was open for 1% -> 2% of each run, Pallas kernels for 6% -> 0%
where the time goes in v3:
time: 163 us; the launch traced here: 162 us
  starting transfers between devices  60.1 us (37%)
  blocking collectives  41.7 us (26%)
  Pallas kernels  27.1 us (17%)
  waiting for transfers between devices  24.7 us (15%)
  local copies, waits for them, and re-layouts  5.86 us (4%)
    ppermute x6, starting transfers between devices, rotate(): return lax.ppermute(value, 'section', pairs)  20.4 us
    pallas_call x4, Pallas kernels, local_call(): pl.pallas_call(kernel, out_shape=outs, in_specs=[SMEM] + [VMEM] * len(ope...  20.2 us
    all_to_all x2, blocking collectives, per_device(): sums = lax.all_to_all(sums, 'mp', 0, 0)  19.5 us
    all_to_all x1, starting transfers between devices, per_device(): lax.all_to_all(message.reshape(DP * SECTIONS, PAD, LANES), ('dp', 'sectio...  17.4 us
    ppermute x6, waiting for transfers between devices, rotate(): return lax.ppermute(value, 'section', pairs)  17.3 us
    all_to_all x1, starting transfers between devices, per_device(): texts = lax.all_to_all(pairs, 'dp', 0, 0).reshape(TEXTS, 2 * SLICE)  13.1 us
    all_to_all x1, blocking collectives, per_device(): parts = lax.all_to_all(parts, 'mp', 0, 0)  13.1 us
    all_to_all x1, starting transfers between devices, per_device(): lax.all_to_all(jnp.broadcast_to(tap_sum[None], (DP, 5, LANES)), 'dp', 0, 0)  9.24 us
  transfers between devices with their start and end apart: 9, of which 5 were waited for; matrix products, arithmetic and copies ran while one was open for 2% of the time, Pallas kernels for 0%

profile of v3, /device:TPU:1, one launch (start us, length us, event | category | flops | bytes accessed | tf_op | source)
XLA Modules:
  0.0 161.8 jit_solution(15648907373292109955)
XLA Ops:
  0.7 0.8 pad_maximum_fusion.8
  1.5 0.9 broadcast_in_dim.27
  2.5 13.1 %all-to-all-start = ((bf16[32,24,512]{2,1,0:T(8,128)(2,1)}), bf16[32,24,512]{2,1,0:T(8,128)(2,1)S(1)}, u32[]{:S(2)}, u32[]{:S(2)}) async-start(bf16[32,24,512]{2,1,0:T(8,128)(2,1)} %broadcast_in_dim.27), calls=%async_computation | async-start | bytes 1572864 | tf_op jit(solution)/shard_map/all_to_all | solution.py:481
  15.9 4.4 %collective-permute-start.2 = (bf16[112,1280]{1,0:T(8,128)(2,1)S(1)}, bf16[112,1280]{1,0:T(8,128)(2,1)S(1)}, u32[]{:S(2)}, u32[]{:S(2)}) collective-permute-start(bf16[112,1280]{1,0:T(8,128)(2,1)S(1)} %get-tuple-element.57), channel_id=1, source_target_pairs={{0,12},{4,0},{8,4},{12,8},{1,13},{5,1},{9,5},{13,9},{2,14},{6,2},{... | collective-permute-start | bytes 860168 | tf_op jit(solution)/shard_map/ppermute | solution.py:460
  20.3 1.9 %collective-permute-start = (bf16[112,1280]{1,0:T(8,128)(2,1)S(1)}, bf16[112,1280]{1,0:T(8,128)(2,1)S(1)}, u32[]{:S(2)}, u32[]{:S(2)}) collective-permute-start(bf16[112,1280]{1,0:T(8,128)(2,1)S(1)} %get-tuple-element.58), channel_id=1, source_target_pairs={{0,4},{4,8},{8,12},{12,0},{1,5},{5,9},{9,13},{13,1},{2,6},{6,10},{... | collective-permute-start | bytes 860168 | tf_op jit(solution)/shard_map/ppermute | solution.py:460
  22.2 3.6 %collective-permute-start.1 = (bf16[112,1280]{1,0:T(8,128)(2,1)S(1)}, bf16[112,1280]{1,0:T(8,128)(2,1)S(1)}, u32[]{:S(2)}, u32[]{:S(2)}) collective-permute-start(bf16[112,1280]{1,0:T(8,128)(2,1)S(1)} %get-tuple-element.59), channel_id=1, source_target_pairs={{0,8},{4,12},{8,0},{12,4},{1,9},{5,13},{9,1},{13,5},{2,10},{6,14},... | collective-permute-start | bytes 860168 | tf_op jit(solution)/shard_map/ppermute | solution.py:460
  25.9 0.7 constant_dynamic-slice_fusion
  26.7 5.5 %collective-permute-done.x1 = bf16[112,1280]{1,0:T(8,128)(2,1)S(1)} collective-permute-done((bf16[112,1280]{1,0:T(8,128)(2,1)S(1)}, bf16[112,1280]{1,0:T(8,128)(2,1)S(1)}, u32[]{:S(2)}, u32[]{:S(2)}) %collective-permute-start) | collective-permute-done | bytes 286752 | tf_op jit(solution)/shard_map/ppermute | solution.py:460
  32.2 4.3 %collective-permute-done.1.x2 = bf16[112,1280]{1,0:T(8,128)(2,1)S(1)} collective-permute-done((bf16[112,1280]{1,0:T(8,128)(2,1)S(1)}, bf16[112,1280]{1,0:T(8,128)(2,1)S(1)}, u32[]{:S(2)}, u32[]{:S(2)}) %collective-permute-start.1) | collective-permute-done | bytes 286752 | tf_op jit(solution)/shard_map/ppermute | solution.py:460
  36.5 0.9 all-to-all-done
  37.4 1.4 row_sums_and_scores.1
  38.8 13.1 %all_to_all.35.parts = f32[4,8,896]{2,1,0:T(8,128)S(1)} all-to-all(f32[4,8,896]{2,1,0:T(8,128)S(1)} %row_sums_and_scores.1), channel_id=1, replica_groups=mesh['dp'=32,'section'=4,'mp'=4] {'mp'}, dimensions={0} | all-to-all | bytes 229376 | tf_op jit(solution)/shard_map/all_to_all | solution.py:494
  51.9 0.9 softmax_grads.1
  52.8 9.1 %all_to_all.36.query_grad = bf16[4,16,256]{2,1,0:T(8,128)(2,1)S(1)} all-to-all(bf16[4,16,256]{2,1,0:T(8,128)(2,1)S(1)} %get-tuple-element.20), channel_id=1, replica_groups=mesh['dp'=32,'section'=4,'mp'=4] {'mp'}, dimensions={0} | all-to-all | bytes 65536 | tf_op jit(solution)/shard_map/all_to_all | solution.py:504
  61.9 4.6 %sections_forward.1 = (f32[4,10,16,8,128]{4,3,2,1,0:T(8,128)S(1)}, f32[4,10,16,8,128]{4,3,2,1,0:T(8,128)S(1)}, f32[4,16,8,128]{3,2,1,0:T(8,128)S(1)}, f32[8,128]{1,0:T(8,128)S(1)}, f32[4,16,1280]{2,1,0:T(8,128)S(1)}) custom-call(bf16[4,16,256]{2,1,0:T(8,128)(2,1)S(1)} %all_to_all.36.query_grad, f32[4,8,896]{2,1,0:T(8,128)S(1)} %all_to_all.35.parts, ...), custom_call_target="tpu_custom_call" | custom-call | flops 1000000000 | bytes 6000000 | tf_op jit(solution)/shard_map/sections_forward/pallas_call | solution.py:506
  66.5 6.2 %pair_matrices.1.matrices = f32[2,64,128]{2,1,0:T(8,128)S(1)} custom-call(s32[5]{0:T(128)S(1)} %stack.23.hops, f32[4,10,16,8,128]{4,3,2,1,0:T(8,128)S(1)} %get-tuple-element.21.normed, f32[4,10,16,8,128]{4,3,2,1,0:T(8,128)S(1)} %get-tuple-element.22.gate, f32[4,16,1280]{2,1,0:T(8,128)S(1)} %get-tuple-element.24.taps_in), custom_call_target="tpu_custom_call" | custom-call | flops 3000000000 | bytes 6000000 | tf_op jit(solution)/shard_map/pair_matrices/pallas_call | solution.py:446
  72.7 4.9 %head_and_sections.1 = (f32[10,16,8,128]{3,2,1,0:T(8,128)S(1)}, f32[16,1280]{1,0:T(8,128)S(1)}, f32[4,72,128]{2,1,0:T(8,128)S(1)}) custom-call(s32[5]{0:T(128)S(1)} %stack.23.hops, bf16[4,16,256]{2,1,0:T(8,128)(2,1)S(1)} %all_to_all.36.query_grad, bf16[1280,1024]{1,0:T(8,128)(2,1)S(1)} %copy-done, f32[4,10,16,8,128]{4,3,2,1,0:T(8,128)S(1)} %get-tuple-element.21.normed, ...), custom_call_target="tpu_custom_call" | custom-call | tf_op jit(solution)/shard_map/head_and_sections/pallas_call | solution.py:446
  77.6 9.8 %all_to_all.37.parts = f32[4,72,128]{2,1,0:T(8,128)S(1)} all-to-all(f32[4,72,128]{2,1,0:T(8,128)S(1)} %get-tuple-element.25), channel_id=1, replica_groups=mesh['dp'=32,'section'=4,'mp'=4] {'mp'}, dimensions={0} | all-to-all | bytes 294912 | tf_op jit(solution)/shard_map/all_to_all | solution.py:547
  87.3 5.3 %middle_sections.1 = (bf16[2,96,1280]{2,1,0:T(8,128)(2,1)S(1)}, f32[10,16,8,128]{3,2,1,0:T(8,128)S(1)}, f32[16,1280]{1,0:T(8,128)S(1)}, f32[16,1280]{1,0:T(8,128)S(1)}, f32[4,72,128]{2,1,0:T(8,128)S(1)}) custom-call(s32[5]{0:T(128)S(1)} %stack.23.hops, f32[4,72,128]{2,1,0:T(8,128)S(1)} %all_to_all.37.parts, f32[10,16,8,128]{3,2,1,0:T(8,128)S(1)} %get-tuple-element.26.up, ...), custom_call_target="tpu_custom_call" | custom-call | tf_op jit(solution)/shard_map/middle_sections/pallas_call | solution.py:446
  92.6 9.8 %all_to_all.38.parts = f32[4,72,128]{2,1,0:T(8,128)S(1)} all-to-all(f32[4,72,128]{2,1,0:T(8,128)S(1)} %get-tuple-element.28), channel_id=1, replica_groups=mesh['dp'=32,'section'=4,'mp'=4] {'mp'}, dimensions={0} | all-to-all | bytes 294912 | tf_op jit(solution)/shard_map/all_to_all | solution.py:556
  102.4 3.8 %end_sections.1 = (bf16[4,96,1280]{2,1,0:T(8,128)(2,1)S(1)}, bf16[1024,128]{1,0:T(8,128)(2,1)}) custom-call(s32[5]{0:T(128)S(1)} %stack.23.hops, f32[4,72,128]{2,1,0:T(8,128)S(1)} %all_to_all.38.parts, f32[10,16,8,128]{3,2,1,0:T(8,128)S(1)} %get-tuple-element.29.up, f32[4,10,16,8,128]{4,3,2,1,0:T(8,128)S(1)} %get-tuple-element.21.normed, ...), custom_call_target="tpu_custom_call" | custom-call | tf_op jit(solution)/shard_map/end_sections/pallas_call | solution.py:446
  106.3 3.4 %collective-permute-start.3 = (bf16[96,1280]{1,0:T(8,128)(2,1)S(1)}, bf16[96,1280]{1,0:T(8,128)(2,1)S(1)}, u32[]{:S(2)}, u32[]{:S(2)}) collective-permute-start(bf16[96,1280]{1,0:T(8,128)(2,1)S(1)} %get-tuple-element.51), channel_id=1, source_target_pairs={{0,4},{4,8},{8,12},{12,0},{1,5},{5,9},{9,13},{13,1},{2,6},{6,10},{... | collective-permute-start | bytes 737288 | tf_op jit(solution)/shard_map/ppermute | solution.py:460
  110.2 17.4 %all-to-all-start.5 = ((bf16[128,8,128]{2,1,0:T(8,128)(2,1)}), bf16[128,8,128]{2,1,0:T(8,128)(2,1)S(1)}, u32[]{:S(2)}, u32[]{:S(2)}) async-start(bf16[128,8,128]{2,1,0:T(8,128)(2,1)} %bitcast.19), calls=%async_computation.5 | async-start | bytes 524288 | tf_op jit(solution)/shard_map/all_to_all | solution.py:567
  127.6 4.5 %collective-permute-start.5 = (bf16[96,1280]{1,0:T(8,128)(2,1)S(1)}, bf16[96,1280]{1,0:T(8,128)(2,1)S(1)}, u32[]{:S(2)}, u32[]{:S(2)}) collective-permute-start(bf16[96,1280]{1,0:T(8,128)(2,1)S(1)} %get-tuple-element.49), channel_id=1, source_target_pairs={{0,12},{4,0},{8,4},{12,8},{1,13},{5,1},{9,5},{13,9},{2,14},{6,2},{... | collective-permute-start | bytes 737288 | tf_op jit(solution)/shard_map/ppermute | solution.py:460
  132.1 2.5 %collective-permute-start.4 = (bf16[96,1280]{1,0:T(8,128)(2,1)S(1)}, bf16[96,1280]{1,0:T(8,128)(2,1)S(1)}, u32[]{:S(2)}, u32[]{:S(2)}) collective-permute-start(bf16[96,1280]{1,0:T(8,128)(2,1)S(1)} %get-tuple-element.50), channel_id=1, source_target_pairs={{0,8},{4,12},{8,0},{12,4},{1,9},{5,13},{9,1},{13,5},{2,10},{6,14},... | collective-permute-start | bytes 737288 | tf_op jit(solution)/shard_map/ppermute | solution.py:460
  134.6 0.7 broadcast_in_dim.28
  135.4 7.5 %collective-permute-done.4 = bf16[96,1280]{1,0:T(8,128)(2,1)S(1)} collective-permute-done((bf16[96,1280]{1,0:T(8,128)(2,1)S(1)}, bf16[96,1280]{1,0:T(8,128)(2,1)S(1)}, u32[]{:S(2)}, u32[]{:S(2)}) %collective-permute-start.4) | collective-permute-done | bytes 245792 | tf_op jit(solution)/shard_map/ppermute | solution.py:460
  143.3 0.7 broadcast_in_dim.33
  143.9 9.2 %all-to-all-start.6 = ((bf16[32,5,128]{2,1,0:T(8,128)(2,1)}), bf16[32,5,128]{2,1,0:T(8,128)(2,1)S(1)}, u32[]{:S(2)}, u32[]{:S(2)}) async-start(bf16[32,5,128]{2,1,0:T(8,128)(2,1)} %broadcast_in_dim.33), calls=%async_computation.6 | async-start | bytes 131072 | tf_op jit(solution)/shard_map/all_to_all | solution.py:572
  153.9 0.6 copy.31
  154.5 6.6 %all-to-all-done.6 = bf16[32,5,128]{2,1,0:T(8,128)(2,1)S(1)} async-done(((bf16[32,5,128]{2,1,0:T(8,128)(2,1)}), bf16[32,5,128]{2,1,0:T(8,128)(2,1)S(1)}, u32[]{:S(2)}, u32[]{:S(2)}) %all-to-all-start.6) | async-done | bytes 40992 | tf_op jit(solution)/shard_map/all_to_all | solution.py:572
  161.1 0.7 reshape.90
  (44 shorter events, 1.9 us)
Async XLA Ops:
  0.6 15.0 %copy-start.6 = (f32[1,1280]{1,0:T(1,128)S(1)}, f32[1,1280]{1,0:T(1,128)}, u32[]{:S(2)}) copy-start(f32[1,1280]{1,0:T(1,128)} %param.9) | copy-start | bytes 15364
  0.6 15.1 %copy-start.3 = (bf16[1,2,12,16,1280]{4,3,2,1,0:T(8,128)(2,1)S(1)}, bf16[1,2,12,16,1280]{4,3,2,1,0:T(8,128)(2,1)}, u32[]{:S(2)}) copy-start(bf16[1,2,12,16,1280]{4,3,2,1,0:T(8,128)(2,1)} %param.8) | copy-start | bytes 2949124
  0.7 15.1 %copy-start.5 = (bf16[1,15,1280]{2,1,0:T(8,128)(2,1)S(1)}, bf16[1,15,1280]{2,1,0:T(8,128)(2,1)}, u32[]{:S(2)}) copy-start(bf16[1,15,1280]{2,1,0:T(8,128)(2,1)} %param.10) | copy-start | bytes 115204
  2.5 34.9 %copy-start.1 = (s32[2,12]{1,0:T(2,128)S(1)}, s32[2,12]{1,0:T(2,128)}, u32[]{:S(2)}) copy-start(s32[2,12]{1,0:T(2,128)} %positives.3) | copy-start | bytes 292
  2.5 34.9 %copy-start.2 = (f32[2,12]{1,0:T(2,128)S(1)}, f32[2,12]{1,0:T(2,128)}, u32[]{:S(2)}) copy-start(f32[2,12]{1,0:T(2,128)} %weights.3) | copy-start | bytes 292
  2.5 34.9 %all-to-all-start = ((bf16[32,24,512]{2,1,0:T(8,128)(2,1)}), bf16[32,24,512]{2,1,0:T(8,128)(2,1)S(1)}, u32[]{:S(2)}, u32[]{:S(2)}) async-start(bf16[32,24,512]{2,1,0:T(8,128)(2,1)} %broadcast_in_dim.27), calls=%async_computation | async-start | bytes 1572864 | tf_op jit(solution)/shard_map/all_to_all | solution.py:481
  15.9 10.8 %collective-permute-start.2 = (bf16[112,1280]{1,0:T(8,128)(2,1)S(1)}, bf16[112,1280]{1,0:T(8,128)(2,1)S(1)}, u32[]{:S(2)}, u32[]{:S(2)}) collective-permute-start(bf16[112,1280]{1,0:T(8,128)(2,1)S(1)} %get-tuple-element.57), channel_id=1, source_target_pairs={{0,12},{4,0},{8,4},{12,8},{1,13},{5,1},{9,5},{13,9},{2,14},{6,2},{... | collective-permute-start | bytes 860168 | tf_op jit(solution)/shard_map/ppermute | solution.py:460
  20.3 11.9 %collective-permute-start = (bf16[112,1280]{1,0:T(8,128)(2,1)S(1)}, bf16[112,1280]{1,0:T(8,128)(2,1)S(1)}, u32[]{:S(2)}, u32[]{:S(2)}) collective-permute-start(bf16[112,1280]{1,0:T(8,128)(2,1)S(1)} %get-tuple-element.58), channel_id=1, source_target_pairs={{0,4},{4,8},{8,12},{12,0},{1,5},{5,9},{9,13},{13,1},{2,6},{6,10},{... | collective-permute-start | bytes 860168 | tf_op jit(solution)/shard_map/ppermute | solution.py:460
  22.2 14.3 %collective-permute-start.1 = (bf16[112,1280]{1,0:T(8,128)(2,1)S(1)}, bf16[112,1280]{1,0:T(8,128)(2,1)S(1)}, u32[]{:S(2)}, u32[]{:S(2)}) collective-permute-start(bf16[112,1280]{1,0:T(8,128)(2,1)S(1)} %get-tuple-element.59), channel_id=1, source_target_pairs={{0,8},{4,12},{8,0},{12,4},{1,9},{5,13},{9,1},{13,5},{2,10},{6,14},... | collective-permute-start | bytes 860168 | tf_op jit(solution)/shard_map/ppermute | solution.py:460
  66.5 6.2 %copy-start = (bf16[1280,1024]{1,0:T(8,128)(2,1)S(1)}, bf16[1280,1024]{1,0:T(8,128)(2,1)}, u32[]{:S(2)}) copy-start(bf16[1280,1024]{1,0:T(8,128)(2,1)} %weight.1) | copy-start | bytes 7864324
  106.3 29.1 %collective-permute-start.3 = (bf16[96,1280]{1,0:T(8,128)(2,1)S(1)}, bf16[96,1280]{1,0:T(8,128)(2,1)S(1)}, u32[]{:S(2)}, u32[]{:S(2)}) collective-permute-start(bf16[96,1280]{1,0:T(8,128)(2,1)S(1)} %get-tuple-element.51), channel_id=1, source_target_pairs={{0,4},{4,8},{8,12},{12,0},{1,5},{5,9},{9,13},{13,1},{2,6},{6,10},{... | collective-permute-start | bytes 737288 | tf_op jit(solution)/shard_map/ppermute | solution.py:460
  110.2 32.8 %all-to-all-start.5 = ((bf16[128,8,128]{2,1,0:T(8,128)(2,1)}), bf16[128,8,128]{2,1,0:T(8,128)(2,1)S(1)}, u32[]{:S(2)}, u32[]{:S(2)}) async-start(bf16[128,8,128]{2,1,0:T(8,128)(2,1)} %bitcast.19), calls=%async_computation.5 | async-start | bytes 524288 | tf_op jit(solution)/shard_map/all_to_all | solution.py:567
  127.6 15.3 %collective-permute-start.5 = (bf16[96,1280]{1,0:T(8,128)(2,1)S(1)}, bf16[96,1280]{1,0:T(8,128)(2,1)S(1)}, u32[]{:S(2)}, u32[]{:S(2)}) collective-permute-start(bf16[96,1280]{1,0:T(8,128)(2,1)S(1)} %get-tuple-element.49), channel_id=1, source_target_pairs={{0,12},{4,0},{8,4},{12,8},{1,13},{5,1},{9,5},{13,9},{2,14},{6,2},{... | collective-permute-start | bytes 737288 | tf_op jit(solution)/shard_map/ppermute | solution.py:460
  132.1 10.8 %collective-permute-start.4 = (bf16[96,1280]{1,0:T(8,128)(2,1)S(1)}, bf16[96,1280]{1,0:T(8,128)(2,1)S(1)}, u32[]{:S(2)}, u32[]{:S(2)}) collective-permute-start(bf16[96,1280]{1,0:T(8,128)(2,1)S(1)} %get-tuple-element.50), channel_id=1, source_target_pairs={{0,8},{4,12},{8,0},{12,4},{1,9},{5,13},{9,1},{13,5},{2,10},{6,14},... | collective-permute-start | bytes 737288 | tf_op jit(solution)/shard_map/ppermute | solution.py:460
  143.0 18.9 %copy-start.4 = (bf16[1,2,12,16,1280]{4,3,2,1,0:T(8,128)(2,1)}, bf16[1,2,12,16,1280]{4,3,2,1,0:T(8,128)(2,1)S(1)}, u32[]{:S(2)}) copy-start(bf16[1,2,12,16,1280]{4,3,2,1,0:T(8,128)(2,1)S(1)} %constant_dynamic-update-slice_fusion) | copy-start | bytes 2949124
  143.9 17.2 %all-to-all-start.6 = ((bf16[32,5,128]{2,1,0:T(8,128)(2,1)}), bf16[32,5,128]{2,1,0:T(8,128)(2,1)S(1)}, u32[]{:S(2)}, u32[]{:S(2)}) async-start(bf16[32,5,128]{2,1,0:T(8,128)(2,1)} %broadcast_in_dim.33), calls=%async_computation.6 | async-start | bytes 131072 | tf_op jit(solution)/shard_map/all_to_all | solution.py:572

commit v4 on v3

--- a/solution.py
+++ b/solution.py
@@ -19,6 +19,7 @@
 CLIPS = MICRO * OWN
 ROWS = CLIPS * FRAMES
 TEXTS = DP * MICRO * SHARD
+HALF_TEXTS = TEXTS // 2
 WIDE = D // MP
 SLICE = EMB // MP
 LANES = 128
@@ -50,7 +51,14 @@
     return jnp.broadcast_to(turned[:, 0:1], (LANES, LANES))
 
 
-def sums_kernel(hops, positives, weights, x0, x1, x2, x3, texts, query, out):
+def text_micros(rows):
+    column = lax.broadcasted_iota(jnp.int32, (rows, TEXTS), 1)
+    return ((column * 10923) >> 17) & 1
+
+
+def sums_kernel(
+    hops, positives, weights, x0, x1, x2, x3, texts, query, out
+):
     rows = []
     for x in (x0, x1, x2, x3):
         total = jnp.zeros((ROWS, LANES), F32)
@@ -66,22 +74,26 @@
     scores = lax.dot_general(
         query[...], texts[:, 0:SLICE], NT, preferred_element_type=F32
     )[0:PAD]
+    shared = jnp.where(text_micros(OWN) == 0, scores[0:OWN], scores[OWN:CLIPS])
     for peer in range(MP):
-        out[peer, :, 0:TEXTS] = scores
-        out[peer, :, TEXTS:] = stats
+        out[peer, 0:OWN, 0:HALF_TEXTS] = shared[:, 0:HALF_TEXTS]
+        out[peer, OWN:CLIPS, 0:HALF_TEXTS] = shared[:, HALF_TEXTS:]
+        out[peer, CLIPS:PAD, 0:HALF_TEXTS] = jnp.zeros((PAD - CLIPS, HALF_TEXTS), F32)
+        out[peer, :, HALF_TEXTS:] = stats
 
 
 def softmax_kernel(
     hops, positives, weights, parts, texts, query_grad, pair_parts
 ):
-    scores = parts[0, :, 0:TEXTS]
+    shared = parts[0, :, 0:HALF_TEXTS]
     for peer in range(1, MP):
-        scores = scores + parts[peer, :, 0:TEXTS]
+        shared = shared + parts[peer, :, 0:HALF_TEXTS]
+    shared = jnp.concatenate([shared[0:OWN], shared[OWN:CLIPS]], 1)
+    scores = jnp.concatenate([shared, shared, jnp.zeros((PAD - CLIPS, TEXTS), F32)], 0)
     row = lax.broadcasted_iota(jnp.int32, (PAD, TEXTS), 0)
     column = lax.broadcasted_iota(jnp.int32, (PAD, TEXTS), 1)
-    text_micro = ((column * 10923) >> 17) & 1
     clip_micro = jnp.where(row >= OWN, 1, 0)
-    scores = jnp.where(text_micro == clip_micro, scores * SCORE_SCALE, -1e30)
+    scores = jnp.where(text_micros(PAD) == clip_micro, scores * SCORE_SCALE, -1e30)
     exp_scores = jnp.exp(scores - jnp.max(scores, axis=1, keepdims=True))
     probs = exp_scores / jnp.sum(exp_scores, axis=1, keepdims=True)
     base = hops[SECTIONS] * OWN
@@ -123,12 +135,12 @@
 
 def forward_kernel(
     query_grad, parts, x0, x1, x2, x3,
-    normed_out, gate_out, inv_out, inv_row_out, taps_out,
+    normed_out, gate_out, inv_out, inv_row_out, taps_out, rows_out,
     natural, mean_rows, inv_rows,
 ):
-    stats = parts[0, :, TEXTS:]
+    stats = parts[0, :, HALF_TEXTS:]
     for peer in range(1, MP):
-        stats = stats + parts[peer, :, TEXTS:]
+        stats = stats + parts[peer, :, HALF_TEXTS:]
     natural[...] = jnp.zeros_like(natural)
     for hop, x in enumerate((x0, x1, x2, x3)):
         mean = stats[2 * hop : 2 * hop + 1] / D
@@ -143,7 +155,9 @@
         def block_step(block, carry, hop=hop, x=x):
             lanes = lanes_of(block)
             value = x[0:ROWS, lanes].astype(F32)
-            natural[0:ROWS, :] = (value - mean_rows[0:ROWS, :]) * inv_rows[0:ROWS, :]
+            value = (value - mean_rows[0:ROWS, :]) * inv_rows[0:ROWS, :]
+            natural[0:ROWS, :] = value
+            rows_out[hop, :, lanes] = value
             weights = x[ROWS : ROWS + 16, lanes].astype(F32)
             taps_out[hop, :, lanes] = weights
             taps = [
@@ -168,7 +182,7 @@
 
 
 def pair_kernel(
-    hops, normed, gate, taps_in, out, normed_rows, gate_rows, both_rows, left, right, plain
+    hops, normed_rows, gate, taps_in, out, gate_rows, left, right, plain
 ):
     frame = lax.broadcasted_iota(jnp.int32, (FRAMES, 2 * LANES), 0)
     lane = lax.broadcasted_iota(jnp.int32, (FRAMES, 2 * LANES), 1)
@@ -184,15 +198,14 @@
             weights = weights * weights[KERNEL : KERNEL + 1]
             plain[:, lanes] = weights.astype(BF16)
             for f in range(FRAMES):
-                rows = pl.ds(f, PAD, stride=FRAMES)
-                value = gate[here, block, f]
-                normed_rows[rows, :] = normed[here, block, f]
-                gate_rows[rows, :] = value
-                both_rows[rows, :] = value * normed[above, block, f]
+                gate_rows[pl.ds(f, PAD, stride=FRAMES), :] = gate[here, block, f]
             right[0:LANES, lanes] = gate_rows[...].astype(BF16)
-            right[LANES : 2 * LANES, lanes] = both_rows[...].astype(BF16)
+            right[LANES : LANES + ROWS, lanes] = (
+                gate_rows[0:ROWS, :] * normed_rows[above, :, lanes]
+            ).astype(BF16)
+            right[LANES + ROWS :, lanes] = jnp.zeros((LANES - ROWS, LANES), BF16)
             for c in range(CLIPS):
-                value = normed_rows[c * FRAMES : (c + 1) * FRAMES, :]
+                value = normed_rows[here, c * FRAMES : (c + 1) * FRAMES, lanes]
                 for k in range(KERNEL):
                     start = (c * KERNEL + k) * FRAMES
                     left[start : start + FRAMES, lanes] = (value * weights[k : k + 1]).astype(
@@ -388,26 +401,23 @@
 
 def end_kernel(
     hops, parts, up, normed, gate, inv, inv_row, taps_in,
-    before, tap_three, tap_two, tap_one, pair_parts,
+    tap_three, tap_two, tap_one, pair_parts,
     result, message,
     a0, a1, b0, b1, natural, tap_zero, wide,
 ):
     three, two, one, zero = hops[3], hops[2], hops[1], hops[0]
-    slots = [(SECTIONS - hop) & (SECTIONS - 1) for hop in (zero, one, two, three)]
     read_sums(parts, inv_row, one, zero, natural, a0, a1, b0, b1)
-    result[slots[3]] = before[0]
-    result[slots[2]] = before[1]
 
     def block_step(block, carry):
         ups = corrected([up[block, f] for f in range(FRAMES)], normed, one, block, a0, a1)
-        write_result(ups, natural, result, slots[1], block)
+        write_result(ups, natural, result, 1, block)
         taps = tap_rows(taps_in, zero, block)
         grad_conv = [ups[f] * gate[zero, block, f] for f in range(FRAMES)]
         grads = conv_back(grad_conv, taps)
         add_taps(grad_conv, normed, zero, block, taps, tap_zero)
         ups = [ups[f] + inv[zero, f] * grads[f] for f in range(FRAMES)]
         ups = corrected(ups, normed, zero, block, b0, b1)
-        write_result(ups, natural, result, slots[0], block)
+        write_result(ups, natural, result, 0, block)
         return carry
 
     lax.fori_loop(0, BLOCKS, block_step, 0)
@@ -427,6 +437,34 @@
     message[...] = wide[...].reshape(2 * half * PAD, LANES).astype(BF16)
 
 
+def order_kernel(hops, last, before, *outs):
+    for section in range(SECTIONS):
+        steps = (SECTIONS - hops[section]) & (SECTIONS - 1)
+        for target in range(SECTIONS):
+
+            @pl.when(steps == target)
+            def _(section=section, target=target):
+                outs[target][...] = last[section] if section < 2 else before[3 - section]
+
+
+def assemble_kernel(hops, own, first, second, third, tap_sum, out, sems):
+    copies = []
+    for steps, part in enumerate((own, first, second, third)):
+        source = (hops[SECTIONS] + SECTIONS - steps) & (SECTIONS - 1)
+        for micro in range(MICRO):
+            copies.append(
+                pltpu.make_async_copy(
+                    part.at[pl.ds(micro * OWN, OWN)],
+                    out.at[micro, pl.ds(source * OWN, OWN)],
+                    sems.at[steps * MICRO + micro],
+                )
+            )
+    for copy in copies:
+        copy.start()
+    for copy in copies:
+        copy.wait()
+
+
 FRAME_MAJOR = (BLOCKS, FRAMES, PAD, LANES)
 ROW_TILE = pltpu.VMEM((FRAMES, PAD, LANES), F32)
 NATURAL = pltpu.VMEM((LANES, LANES), F32)
@@ -485,7 +523,7 @@
 
     parts = pl.pallas_call(
         sums_kernel,
-        out_shape=shape((MP, PAD, TEXTS + LANES)),
+        out_shape=shape((MP, PAD, HALF_TEXTS + LANES)),
         in_specs=[SMEM] * 3 + [VMEM] * 6,
         out_specs=VMEM,
         compiler_params=PARAMS,
@@ -503,7 +541,7 @@
     )(hops, positives, pair_weights, parts, texts)
     query_grad = lax.all_to_all(query_grad, "mp", 0, 0)
 
-    normed, gate, inv, inv_row, taps = pl.pallas_call(
+    normed, gate, inv, inv_row, taps, normed_rows = pl.pallas_call(
         forward_kernel,
         out_shape=(
             shape((SECTIONS,) + FRAME_MAJOR),
@@ -511,9 +549,10 @@
             shape((SECTIONS, FRAMES, PAD, LANES)),
             shape((PAD, LANES)),
             shape((SECTIONS, 16, WIDE)),
+            shape((SECTIONS, ROWS, WIDE)),
         ),
         in_specs=[VMEM] * 6,
-        out_specs=(VMEM,) * 5,
+        out_specs=(VMEM,) * 6,
         scratch_shapes=[NATURAL] * 3,
         compiler_params=PARAMS,
         cost_estimate=cost(10**9, 6 * 10**6),
@@ -522,9 +561,9 @@
     (matrices,) = local_call(
         pair_kernel,
         hops,
-        (normed, gate, taps),
+        (normed_rows, gate, taps),
         [shape((2, MATRIX_ROWS, LANES))],
-        [NATURAL] * 3
+        [NATURAL]
         + [
             pltpu.VMEM((CLIPS * KERNEL * FRAMES, WIDE), BF16),
             pltpu.VMEM((2 * LANES, WIDE), BF16),
@@ -555,11 +594,11 @@
     )
     sums = lax.all_to_all(sums, "mp", 0, 0)
 
-    results_out, message = local_call(
+    last, message = local_call(
         end_kernel,
         hops,
-        (sums, up, normed, gate, inv, inv_row, taps, before, tap_three, tap_two, tap_one, pair_parts),
-        [shape((SECTIONS, ROWS, WIDE), BF16), shape((DP * SECTIONS * PAD, LANES), BF16)],
+        (sums, up, normed, gate, inv, inv_row, taps, tap_three, tap_two, tap_one, pair_parts),
+        [shape((2, ROWS, WIDE), BF16), shape((DP * SECTIONS * PAD, LANES), BF16)],
         [ROW_TILE] * 4
         + [NATURAL, pltpu.VMEM((16, WIDE), F32), pltpu.VMEM((DP * SECTIONS, PAD, LANES), F32)],
         "end_sections",
@@ -582,13 +621,27 @@
         * SCORE_SCALE
     ).reshape(MICRO, SHARD, SLICE)
 
-    results = jnp.broadcast_to(results_out[0, 0, 0], inputs_all.shape)
-    for steps in range(SECTIONS):
-        source = (section_now - steps) % SECTIONS
-        block = results_out[steps]
-        block = rotate(block, steps) if steps else block
-        block = block.reshape(MICRO, OWN, FRAMES, WIDE)
-        results = lax.dynamic_update_slice_in_dim(results, block, OWN * source, 1)
+    ordered = local_call(
+        order_kernel,
+        hops,
+        (last, before),
+        [shape((ROWS, WIDE), BF16)] * SECTIONS,
+        [],
+        "order_results",
+        cost(10**9, 2 * 10**6),
+    )
+    pieces = [rotate(part, steps) if steps else part for steps, part in enumerate(ordered)]
+    pieces = [part.reshape(CLIPS, FRAMES, WIDE) for part in pieces]
+    results = pl.pallas_call(
+        assemble_kernel,
+        out_shape=shape((MICRO, SHARD, FRAMES, WIDE), BF16),
+        in_specs=[SMEM] + [pl.BlockSpec(memory_space=pl.ANY)] * 5,
+        out_specs=pl.BlockSpec(memory_space=pl.ANY),
+        scratch_shapes=[pltpu.SemaphoreType.DMA((SECTIONS * MICRO,))],
+        compiler_params=PARAMS,
+        cost_estimate=cost(10**10, 10**7),
+        name="assemble_results",
+    )(hops, *pieces, tap_sum)
     return (results[None], tap_grads[None], key_grads)
 
 

time: 163 us -> 153 us (0.939)
  waiting for transfers between devices: 24.7 us -> 16.8 us
  starting transfers between devices: 60.1 us -> 58 us
  Pallas kernels: 27.1 us -> 28.8 us
    ppermute x6, waiting for transfers between devices: 17.3 us -> 9.79 us  [rotate(): return lax.ppermute(value, 'section', pairs)]
    pallas_call x4 -> x5, Pallas kernels: 20.2 us -> 20.3 us  [local_call(): pl.pallas_call(kernel, out_shape=outs, in_specs=[SMEM] + [VMEM] * len(ope...]
  transfers between devices with their start and end apart: 9 -> 9, of which waited for: 5 -> 5; matrix products, arithmetic and copies ran while one was open for 2% -> 2% of each run, Pallas kernels for 0% -> 1%
where the time goes in v4:
time: 153 us; the launch traced here: 152 us
  starting transfers between devices  58 us (38%)
  blocking collectives  41.6 us (27%)
  Pallas kernels  28.8 us (19%)
  waiting for transfers between devices  16.8 us (11%)
  local copies, waits for them, and re-layouts  4.44 us (3%)
    ppermute x6, starting transfers between devices, rotate(): return lax.ppermute(value, 'section', pairs)  20.6 us
    pallas_call x5, Pallas kernels, local_call(): pl.pallas_call(kernel, out_shape=outs, in_specs=[SMEM] + [VMEM] * len(ope...  20.3 us
    all_to_all x2, blocking collectives, per_device(): sums = lax.all_to_all(sums, 'mp', 0, 0)  19.6 us
    all_to_all x1, starting transfers between devices, per_device(): lax.all_to_all(message.reshape(DP * SECTIONS, PAD, LANES), ('dp', 'sectio...  15.9 us
    all_to_all x1, starting transfers between devices, per_device(): texts = lax.all_to_all(pairs, 'dp', 0, 0).reshape(TEXTS, 2 * SLICE)  13.1 us
    all_to_all x1, blocking collectives, per_device(): parts = lax.all_to_all(parts, 'mp', 0, 0)  12.9 us
    ppermute x6, waiting for transfers between devices, rotate(): return lax.ppermute(value, 'section', pairs)  9.79 us
    all_to_all x1, blocking collectives, per_device(): query_grad = lax.all_to_all(query_grad, 'mp', 0, 0)  9.06 us
  transfers between devices with their start and end apart: 9, of which 5 were waited for; matrix products, arithmetic and copies ran while one was open for 2% of the time, Pallas kernels for 1%

profile of v4, /device:TPU:1, one launch (start us, length us, event | category | flops | bytes accessed | tf_op | source)
XLA Modules:
  0.0 151.9 jit_solution(896442969702372513)
XLA Ops:
  0.7 0.8 pad_maximum_fusion.8
  1.5 0.9 broadcast_in_dim.18
  2.5 13.1 %all-to-all-start = ((bf16[32,24,512]{2,1,0:T(8,128)(2,1)}), bf16[32,24,512]{2,1,0:T(8,128)(2,1)S(1)}, u32[]{:S(2)}, u32[]{:S(2)}) async-start(bf16[32,24,512]{2,1,0:T(8,128)(2,1)} %broadcast_in_dim.18), calls=%async_computation | async-start | bytes 1572864 | tf_op jit(solution)/shard_map/all_to_all | solution.py:519
  15.9 4.4 %collective-permute-start.2 = (bf16[112,1280]{1,0:T(8,128)(2,1)S(1)}, bf16[112,1280]{1,0:T(8,128)(2,1)S(1)}, u32[]{:S(2)}, u32[]{:S(2)}) collective-permute-start(bf16[112,1280]{1,0:T(8,128)(2,1)S(1)} %get-tuple-element.63), channel_id=1, source_target_pairs={{0,12},{4,0},{8,4},{12,8},{1,13},{5,1},{9,5},{13,9},{2,14},{6,2},{... | collective-permute-start | bytes 860168 | tf_op jit(solution)/shard_map/ppermute | solution.py:498
  20.3 1.9 %collective-permute-start = (bf16[112,1280]{1,0:T(8,128)(2,1)S(1)}, bf16[112,1280]{1,0:T(8,128)(2,1)S(1)}, u32[]{:S(2)}, u32[]{:S(2)}) collective-permute-start(bf16[112,1280]{1,0:T(8,128)(2,1)S(1)} %get-tuple-element.64), channel_id=1, source_target_pairs={{0,4},{4,8},{8,12},{12,0},{1,5},{5,9},{9,13},{13,1},{2,6},{6,10},{... | collective-permute-start | bytes 860168 | tf_op jit(solution)/shard_map/ppermute | solution.py:498
  22.2 3.6 %collective-permute-start.1 = (bf16[112,1280]{1,0:T(8,128)(2,1)S(1)}, bf16[112,1280]{1,0:T(8,128)(2,1)S(1)}, u32[]{:S(2)}, u32[]{:S(2)}) collective-permute-start(bf16[112,1280]{1,0:T(8,128)(2,1)S(1)} %get-tuple-element.65), channel_id=1, source_target_pairs={{0,8},{4,12},{8,0},{12,4},{1,9},{5,13},{9,1},{13,5},{2,10},{6,14},... | collective-permute-start | bytes 860168 | tf_op jit(solution)/shard_map/ppermute | solution.py:498
  25.9 0.7 constant_dynamic-slice_fusion
  26.7 5.5 %collective-permute-done.x1 = bf16[112,1280]{1,0:T(8,128)(2,1)S(1)} collective-permute-done((bf16[112,1280]{1,0:T(8,128)(2,1)S(1)}, bf16[112,1280]{1,0:T(8,128)(2,1)S(1)}, u32[]{:S(2)}, u32[]{:S(2)}) %collective-permute-start) | collective-permute-done | bytes 286752 | tf_op jit(solution)/shard_map/ppermute | solution.py:498
  32.2 4.3 %collective-permute-done.1.x2 = bf16[112,1280]{1,0:T(8,128)(2,1)S(1)} collective-permute-done((bf16[112,1280]{1,0:T(8,128)(2,1)S(1)}, bf16[112,1280]{1,0:T(8,128)(2,1)S(1)}, u32[]{:S(2)}, u32[]{:S(2)}) %collective-permute-start.1) | collective-permute-done | bytes 286752 | tf_op jit(solution)/shard_map/ppermute | solution.py:498
  36.5 0.9 all-to-all-done
  37.4 1.4 row_sums_and_scores.1
  38.8 12.9 %all_to_all.35.parts = f32[4,8,512]{2,1,0:T(8,128)S(1)} all-to-all(f32[4,8,512]{2,1,0:T(8,128)S(1)} %row_sums_and_scores.1), channel_id=1, replica_groups=mesh['dp'=32,'section'=4,'mp'=4] {'mp'}, dimensions={0} | all-to-all | bytes 131072 | tf_op jit(solution)/shard_map/all_to_all | solution.py:532
  51.7 0.9 softmax_grads.1
  52.6 9.1 %all_to_all.36.query_grad = bf16[4,16,256]{2,1,0:T(8,128)(2,1)S(1)} all-to-all(bf16[4,16,256]{2,1,0:T(8,128)(2,1)S(1)} %get-tuple-element.25), channel_id=1, replica_groups=mesh['dp'=32,'section'=4,'mp'=4] {'mp'}, dimensions={0} | all-to-all | bytes 65536 | tf_op jit(solution)/shard_map/all_to_all | solution.py:542
  61.6 4.7 %sections_forward.1 = (f32[4,10,16,8,128]{4,3,2,1,0:T(8,128)S(1)}, f32[4,10,16,8,128]{4,3,2,1,0:T(8,128)S(1)}, f32[4,16,8,128]{3,2,1,0:T(8,128)S(1)}, f32[8,128]...) custom-call(bf16[4,16,256]{2,1,0:T(8,128)(2,1)S(1)} %all_to_all.36.query_grad, ...), custom_call_target="tpu_custom_call" | custom-call | flops 1000000000 | bytes 6000000 | tf_op jit(solution)/shard_map/sections_forward/pallas_call | solution.py:544
  66.3 5.5 %pair_matrices.1.matrices = f32[2,64,128]{2,1,0:T(8,128)S(1)} custom-call(s32[5]{0:T(128)S(1)} %stack.23.hops, f32[4,96,1280]{2,1,0:T(8,128)S(1)} %get-tuple-element.30.normed_rows, f32[4,10,16,8,128]{4,3,2,1,0:T(8,128)S(1)} %get-tuple-element.27.gate, f32[4,16,1280]{2,1,0:T(8,128)S(1)} %get-tuple-element.29.taps_in), custom_call_target="tpu_custom_call" | custom-call | flops 3000000000 | bytes 6000000 | tf_op jit(solution)/shard_map/pair_matrices/pallas_call | solution.py:484
  71.9 4.9 %head_and_sections.1 = (f32[10,16,8,128]{3,2,1,0:T(8,128)S(1)}, f32[16,1280]{1,0:T(8,128)S(1)}, f32[4,72,128]{2,1,0:T(8,128)S(1)}) custom-call(s32[5]{0:T(128)S(1)} %stack.23.hops, bf16[4,16,256]{2,1,0:T(8,128)(2,1)S(1)} %all_to_all.36.query_grad, bf16[1280,1024]{1,0:T(8,128)(2,1)S(1)} %copy-done, f32[4,10,16,8,128]{4,3,2,1,0:T(8,128)S(1)} %get-tuple-element.26.normed, ...), custom_call_target="tpu_custom_call" | custom-call | tf_op jit(solution)/shard_map/head_and_sections/pallas_call | solution.py:484
  76.8 9.8 %all_to_all.37.parts = f32[4,72,128]{2,1,0:T(8,128)S(1)} all-to-all(f32[4,72,128]{2,1,0:T(8,128)S(1)} %get-tuple-element.31), channel_id=1, replica_groups=mesh['dp'=32,'section'=4,'mp'=4] {'mp'}, dimensions={0} | all-to-all | bytes 294912 | tf_op jit(solution)/shard_map/all_to_all | solution.py:586
  86.6 5.3 %middle_sections.1 = (bf16[2,96,1280]{2,1,0:T(8,128)(2,1)S(1)}, f32[10,16,8,128]{3,2,1,0:T(8,128)S(1)}, f32[16,1280]{1,0:T(8,128)S(1)}, f32[16,1280]{1,0:T(8,128)S(1)}, f32[4,72,128]{2,1,0:T(8,128)S(1)}) custom-call(s32[5]{0:T(128)S(1)} %stack.23.hops, f32[4,72,128]{2,1,0:T(8,128)S(1)} %all_to_all.37.parts, f32[10,16,8,128]{3,2,1,0:T(8,128)S(1)} %get-tuple-element.32.up, ...), custom_call_target="tpu_custom_call" | custom-call | tf_op jit(solution)/shard_map/middle_sections/pallas_call | solution.py:484
  91.9 9.8 %all_to_all.38.parts = f32[4,72,128]{2,1,0:T(8,128)S(1)} all-to-all(f32[4,72,128]{2,1,0:T(8,128)S(1)} %get-tuple-element.34), channel_id=1, replica_groups=mesh['dp'=32,'section'=4,'mp'=4] {'mp'}, dimensions={0} | all-to-all | bytes 294912 | tf_op jit(solution)/shard_map/all_to_all | solution.py:595
  101.7 3.8 %end_sections.1 = (bf16[2,96,1280]{2,1,0:T(8,128)(2,1)S(1)}, bf16[1024,128]{1,0:T(8,128)(2,1)}) custom-call(s32[5]{0:T(128)S(1)} %stack.23.hops, f32[4,72,128]{2,1,0:T(8,128)S(1)} %all_to_all.38.parts, f32[10,16,8,128]{3,2,1,0:T(8,128)S(1)} %get-tuple-element.35.up, f32[4,10,16,8,128]{4,3,2,1,0:T(8,128)S(1)} %get-tuple-element.26.normed, ...), custom_call_target="tpu_custom_call" | custom-call | tf_op jit(solution)/shard_map/end_sections/pallas_call | solution.py:484
  105.6 15.9 %all-to-all-start.5 = ((bf16[128,8,128]{2,1,0:T(8,128)(2,1)}), bf16[128,8,128]{2,1,0:T(8,128)(2,1)S(1)}, u32[]{:S(2)}, u32[]{:S(2)}) async-start(bf16[128,8,128]{2,1,0:T(8,128)(2,1)} %bitcast.15), calls=%async_computation.5 | async-start | bytes 524288 | tf_op jit(solution)/shard_map/all_to_all | solution.py:606
  121.5 0.7 order_results.1
  122.2 3.3 %collective-permute-start.3 = (bf16[96,1280]{1,0:T(8,128)(2,1)S(1)}, bf16[96,1280]{1,0:T(8,128)(2,1)S(1)}, u32[]{:S(2)}, u32[]{:S(2)}) collective-permute-start(bf16[96,1280]{1,0:T(8,128)(2,1)S(1)} %get-tuple-element.43), channel_id=1, source_target_pairs={{0,4},{4,8},{8,12},{12,0},{1,5},{5,9},{9,13},{13,1},{2,6},{6,10},{... | collective-permute-start | bytes 737288 | tf_op jit(solution)/shard_map/ppermute | solution.py:498
  125.5 4.3 %collective-permute-start.4 = (bf16[96,1280]{1,0:T(8,128)(2,1)S(1)}, bf16[96,1280]{1,0:T(8,128)(2,1)S(1)}, u32[]{:S(2)}, u32[]{:S(2)}) collective-permute-start(bf16[96,1280]{1,0:T(8,128)(2,1)S(1)} %get-tuple-element.44), channel_id=1, source_target_pairs={{0,8},{4,12},{8,0},{12,4},{1,9},{5,13},{9,1},{13,5},{2,10},{6,14},... | collective-permute-start | bytes 737288 | tf_op jit(solution)/shard_map/ppermute | solution.py:498
  129.8 3.1 %collective-permute-start.5 = (bf16[96,1280]{1,0:T(8,128)(2,1)S(1)}, bf16[96,1280]{1,0:T(8,128)(2,1)S(1)}, u32[]{:S(2)}, u32[]{:S(2)}) collective-permute-start(bf16[96,1280]{1,0:T(8,128)(2,1)S(1)} %get-tuple-element.45), channel_id=1, source_target_pairs={{0,12},{4,0},{8,4},{12,8},{1,13},{5,1},{9,5},{13,9},{2,14},{6,2},{... | collective-permute-start | bytes 737288 | tf_op jit(solution)/shard_map/ppermute | solution.py:498
  132.9 1.2 all-to-all-done.5
  135.0 8.3 %all-to-all-start.6 = ((bf16[32,5,128]{2,1,0:T(8,128)(2,1)}), bf16[32,5,128]{2,1,0:T(8,128)(2,1)S(1)}, u32[]{:S(2)}, u32[]{:S(2)}) async-start(bf16[32,5,128]{2,1,0:T(8,128)(2,1)} %broadcast_in_dim.20), calls=%async_computation.6 | async-start | bytes 131072 | tf_op jit(solution)/shard_map/all_to_all | solution.py:611
  143.8 1.5 %assemble_results.1 = bf16[2,12,16,1280]{3,2,1,0:T(8,128)(2,1)} custom-call(s32[5]{0:T(128)S(1)} %stack.23.hops, bf16[6,16,1280]{2,1,0:T(8,128)(2,1)S(1)} %bitcast.32, bf16[6,16,1280]{2,1,0:T(8,128)(2,1)S(1)} %bitcast.29, bf16[6,16,1280]{2,1,0:T(8,128)(2,1)S(1)} %bitcast.30, bf16[6,16,1280]{2,1,0:T(8,128)(2,1)S(1)} %bitcast.31, ...), custom_call_target="tpu_custom_call" | custom-call | flops 10000000000 | bytes 10000000 | tf_op jit(solution)/shard_map/assemble_results/pallas_call | solution.py:635
  145.6 0.6 copy.31
  146.2 5.0 %all-to-all-done.6 = bf16[32,5,128]{2,1,0:T(8,128)(2,1)S(1)} async-done(((bf16[32,5,128]{2,1,0:T(8,128)(2,1)}), bf16[32,5,128]{2,1,0:T(8,128)(2,1)S(1)}, u32[]{:S(2)}, u32[]{:S(2)}) %all-to-all-start.6) | async-done | bytes 40992 | tf_op jit(solution)/shard_map/all_to_all | solution.py:611
  151.2 0.7 reshape.91
  (37 shorter events, 1.9 us)
Async XLA Ops:
  0.6 15.0 %copy-start.5 = (f32[1,1280]{1,0:T(1,128)S(1)}, f32[1,1280]{1,0:T(1,128)}, u32[]{:S(2)}) copy-start(f32[1,1280]{1,0:T(1,128)} %param.9) | copy-start | bytes 15364
  0.6 15.1 %copy-start.3 = (bf16[1,2,12,16,1280]{4,3,2,1,0:T(8,128)(2,1)S(1)}, bf16[1,2,12,16,1280]{4,3,2,1,0:T(8,128)(2,1)}, u32[]{:S(2)}) copy-start(bf16[1,2,12,16,1280]{4,3,2,1,0:T(8,128)(2,1)} %param.8) | copy-start | bytes 2949124
  0.7 15.1 %copy-start.4 = (bf16[1,15,1280]{2,1,0:T(8,128)(2,1)S(1)}, bf16[1,15,1280]{2,1,0:T(8,128)(2,1)}, u32[]{:S(2)}) copy-start(bf16[1,15,1280]{2,1,0:T(8,128)(2,1)} %param.10) | copy-start | bytes 115204
  2.5 34.9 %copy-start.1 = (s32[2,12]{1,0:T(2,128)S(1)}, s32[2,12]{1,0:T(2,128)}, u32[]{:S(2)}) copy-start(s32[2,12]{1,0:T(2,128)} %positives.3) | copy-start | bytes 292
  2.5 34.9 %copy-start.2 = (f32[2,12]{1,0:T(2,128)S(1)}, f32[2,12]{1,0:T(2,128)}, u32[]{:S(2)}) copy-start(f32[2,12]{1,0:T(2,128)} %weights.3) | copy-start | bytes 292
  2.5 34.9 %all-to-all-start = ((bf16[32,24,512]{2,1,0:T(8,128)(2,1)}), bf16[32,24,512]{2,1,0:T(8,128)(2,1)S(1)}, u32[]{:S(2)}, u32[]{:S(2)}) async-start(bf16[32,24,512]{2,1,0:T(8,128)(2,1)} %broadcast_in_dim.18), calls=%async_computation | async-start | bytes 1572864 | tf_op jit(solution)/shard_map/all_to_all | solution.py:519
  15.9 10.8 %collective-permute-start.2 = (bf16[112,1280]{1,0:T(8,128)(2,1)S(1)}, bf16[112,1280]{1,0:T(8,128)(2,1)S(1)}, u32[]{:S(2)}, u32[]{:S(2)}) collective-permute-start(bf16[112,1280]{1,0:T(8,128)(2,1)S(1)} %get-tuple-element.63), channel_id=1, source_target_pairs={{0,12},{4,0},{8,4},{12,8},{1,13},{5,1},{9,5},{13,9},{2,14},{6,2},{... | collective-permute-start | bytes 860168 | tf_op jit(solution)/shard_map/ppermute | solution.py:498
  20.3 11.9 %collective-permute-start = (bf16[112,1280]{1,0:T(8,128)(2,1)S(1)}, bf16[112,1280]{1,0:T(8,128)(2,1)S(1)}, u32[]{:S(2)}, u32[]{:S(2)}) collective-permute-start(bf16[112,1280]{1,0:T(8,128)(2,1)S(1)} %get-tuple-element.64), channel_id=1, source_target_pairs={{0,4},{4,8},{8,12},{12,0},{1,5},{5,9},{9,13},{13,1},{2,6},{6,10},{... | collective-permute-start | bytes 860168 | tf_op jit(solution)/shard_map/ppermute | solution.py:498
  22.2 14.3 %collective-permute-start.1 = (bf16[112,1280]{1,0:T(8,128)(2,1)S(1)}, bf16[112,1280]{1,0:T(8,128)(2,1)S(1)}, u32[]{:S(2)}, u32[]{:S(2)}) collective-permute-start(bf16[112,1280]{1,0:T(8,128)(2,1)S(1)} %get-tuple-element.65), channel_id=1, source_target_pairs={{0,8},{4,12},{8,0},{12,4},{1,9},{5,13},{9,1},{13,5},{2,10},{6,14},... | collective-permute-start | bytes 860168 | tf_op jit(solution)/shard_map/ppermute | solution.py:498
  66.3 5.6 %copy-start = (bf16[1280,1024]{1,0:T(8,128)(2,1)S(1)}, bf16[1280,1024]{1,0:T(8,128)(2,1)}, u32[]{:S(2)}) copy-start(bf16[1280,1024]{1,0:T(8,128)(2,1)} %weight.1) | copy-start | bytes 7864324
  105.6 28.5 %all-to-all-start.5 = ((bf16[128,8,128]{2,1,0:T(8,128)(2,1)}), bf16[128,8,128]{2,1,0:T(8,128)(2,1)S(1)}, u32[]{:S(2)}, u32[]{:S(2)}) async-start(bf16[128,8,128]{2,1,0:T(8,128)(2,1)} %bitcast.15), calls=%async_computation.5 | async-start | bytes 524288 | tf_op jit(solution)/shard_map/all_to_all | solution.py:606
  122.2 21.6 %collective-permute-start.3 = (bf16[96,1280]{1,0:T(8,128)(2,1)S(1)}, bf16[96,1280]{1,0:T(8,128)(2,1)S(1)}, u32[]{:S(2)}, u32[]{:S(2)}) collective-permute-start(bf16[96,1280]{1,0:T(8,128)(2,1)S(1)} %get-tuple-element.43), channel_id=1, source_target_pairs={{0,4},{4,8},{8,12},{12,0},{1,5},{5,9},{9,13},{13,1},{2,6},{6,10},{... | collective-permute-start | bytes 737288 | tf_op jit(solution)/shard_map/ppermute | solution.py:498
  125.5 18.3 %collective-permute-start.4 = (bf16[96,1280]{1,0:T(8,128)(2,1)S(1)}, bf16[96,1280]{1,0:T(8,128)(2,1)S(1)}, u32[]{:S(2)}, u32[]{:S(2)}) collective-permute-start(bf16[96,1280]{1,0:T(8,128)(2,1)S(1)} %get-tuple-element.44), channel_id=1, source_target_pairs={{0,8},{4,12},{8,0},{12,4},{1,9},{5,13},{9,1},{13,5},{2,10},{6,14},... | collective-permute-start | bytes 737288 | tf_op jit(solution)/shard_map/ppermute | solution.py:498
  129.8 14.0 %collective-permute-start.5 = (bf16[96,1280]{1,0:T(8,128)(2,1)S(1)}, bf16[96,1280]{1,0:T(8,128)(2,1)S(1)}, u32[]{:S(2)}, u32[]{:S(2)}) collective-permute-start(bf16[96,1280]{1,0:T(8,128)(2,1)S(1)} %get-tuple-element.45), channel_id=1, source_target_pairs={{0,12},{4,0},{8,4},{12,8},{1,13},{5,1},{9,5},{13,9},{2,14},{6,2},{... | collective-permute-start | bytes 737288 | tf_op jit(solution)/shard_map/ppermute | solution.py:498
  135.0 16.2 %all-to-all-start.6 = ((bf16[32,5,128]{2,1,0:T(8,128)(2,1)}), bf16[32,5,128]{2,1,0:T(8,128)(2,1)S(1)}, u32[]{:S(2)}, u32[]{:S(2)}) async-start(bf16[32,5,128]{2,1,0:T(8,128)(2,1)} %broadcast_in_dim.20), calls=%async_computation.6 | async-start | bytes 131072 | tf_op jit(solution)/shard_map/all_to_all | solution.py:611

commit v5 on v4

--- a/solution.py
+++ b/solution.py
@@ -42,13 +42,22 @@
     )
 
 
+def split_halves(value):
+    high = value.astype(BF16)
+    return high, (value - high.astype(F32)).astype(BF16)
+
+
 def lanes_of(block):
     return pl.ds(pl.multiple_of(block * LANES, LANES), LANES)
 
 
-def wide_rows(row):
-    turned = jnp.concatenate([row, jnp.zeros((PAD - 1, LANES), F32)], 0).T
-    return jnp.broadcast_to(turned[:, 0:1], (LANES, LANES))
+def wide_rows(rows):
+    rows = list(rows)
+    turned = jnp.concatenate(rows + [jnp.zeros((PAD - len(rows), LANES), F32)], 0).T
+    return [
+        jnp.broadcast_to(turned[:, index : index + 1], (LANES, LANES))
+        for index in range(len(rows))
+    ]
 
 
 def text_micros(rows):
@@ -56,8 +65,21 @@
     return ((column * 10923) >> 17) & 1
 
 
-def sums_kernel(
-    hops, positives, weights, x0, x1, x2, x3, texts, query, out
+def scores_kernel(texts, others, query, x1, x3, out):
+    scores = [
+        lax.dot_general(query[...], part[:, 0:SLICE], NT, preferred_element_type=F32)
+        for part in (texts, others)
+    ]
+    scores = jnp.concatenate(scores, 1)
+    shared = jnp.where(text_micros(OWN) == 0, scores[0:OWN], scores[OWN:CLIPS])
+    for peer in range(MP):
+        out[peer, 0:OWN, :] = shared[:, 0:HALF_TEXTS]
+        out[peer, OWN:CLIPS, :] = shared[:, HALF_TEXTS:]
+        out[peer, CLIPS:PAD, :] = jnp.zeros((PAD - CLIPS, HALF_TEXTS), F32)
+
+
+def softmax_kernel(
+    hops, positives, weights, parts, texts, others, x0, x1, x2, x3, message, pair_parts
 ):
     rows = []
     for x in (x0, x1, x2, x3):
@@ -71,23 +93,10 @@
         rows.append(lane_sums(square)[0:1])
     stats = jnp.concatenate(rows, 0)
     stats = jnp.concatenate([stats, jnp.zeros((PAD, LANES - ROWS), F32)], 1)
-    scores = lax.dot_general(
-        query[...], texts[:, 0:SLICE], NT, preferred_element_type=F32
-    )[0:PAD]
-    shared = jnp.where(text_micros(OWN) == 0, scores[0:OWN], scores[OWN:CLIPS])
-    for peer in range(MP):
-        out[peer, 0:OWN, 0:HALF_TEXTS] = shared[:, 0:HALF_TEXTS]
-        out[peer, OWN:CLIPS, 0:HALF_TEXTS] = shared[:, HALF_TEXTS:]
-        out[peer, CLIPS:PAD, 0:HALF_TEXTS] = jnp.zeros((PAD - CLIPS, HALF_TEXTS), F32)
-        out[peer, :, HALF_TEXTS:] = stats
-
-
-def softmax_kernel(
-    hops, positives, weights, parts, texts, query_grad, pair_parts
-):
-    shared = parts[0, :, 0:HALF_TEXTS]
+
+    shared = parts[0]
     for peer in range(1, MP):
-        shared = shared + parts[peer, :, 0:HALF_TEXTS]
+        shared = shared + parts[peer]
     shared = jnp.concatenate([shared[0:OWN], shared[OWN:CLIPS]], 1)
     scores = jnp.concatenate([shared, shared, jnp.zeros((PAD - CLIPS, TEXTS), F32)], 0)
     row = lax.broadcasted_iota(jnp.int32, (PAD, TEXTS), 0)
@@ -103,22 +112,30 @@
         for own in range(OWN):
             index = positives[micro, base + own]
             owner = (index * 10923) >> 17
-            index = owner * (MICRO * SHARD) + micro * SHARD + (index - owner * SHARD)
+            place = ((owner & 1) ^ hops[SECTIONS + 1]) * (DP // 2) + (owner >> 1)
+            index = place * (MICRO * SHARD) + micro * SHARD + (index - owner * SHARD)
             here = row == micro * OWN + own
             positive = jnp.where(here, index, positive)
             weight = jnp.where(here, weights[micro, base + own], weight)
     hot = jnp.where(column == positive, 1.0, 0.0)
     grad = weight * (probs - hot)
     grad = jnp.concatenate([grad, jnp.zeros((PAD, TEXTS), F32)], 0).astype(BF16)
-    result = jnp.dot(grad, texts[:, 0:SLICE], preferred_element_type=F32) * SCORE_SCALE
-    result = result.astype(BF16)
+    result = jnp.dot(grad[:, 0:HALF_TEXTS], texts[:, 0:SLICE], preferred_element_type=F32)
+    result = result + jnp.dot(
+        grad[:, HALF_TEXTS:], others[:, 0:SLICE], preferred_element_type=F32
+    )
+    result = (result * SCORE_SCALE)[0:PAD]
     for peer in range(MP):
-        query_grad[peer] = result
+        message[peer, 0:PAD, :] = result[:, 0:LANES]
+        message[peer, PAD : 2 * PAD, :] = result[:, LANES:]
+        message[peer, 2 * PAD :, :] = stats
     grad = grad.astype(F32)
     gap = jnp.zeros((1, 32 - MICRO * SHARD), F32)
     tail = jnp.zeros((1, LANES - OWN * 32), F32)
-    for target in range(DP):
-        start = target * MICRO * SHARD
+    for place in range(DP):
+        start = place * MICRO * SHARD
+        half = hops[SECTIONS + 1] ^ (place // (DP // 2))
+        target = (place % (DP // 2)) * 2 + half
         for micro in range(MICRO):
             pieces = []
             for own in range(OWN):
@@ -127,28 +144,29 @@
             pair_parts[target, micro : micro + 1, :] = jnp.concatenate(pieces + [tail], 1)
 
 
-def spread(row, rows_out, natural):
-    natural[...] = wide_rows(row)
-    for f in range(FRAMES):
-        rows_out[f] = natural[pl.ds(f, PAD, stride=FRAMES), :]
+def spread(rows, outs, naturals):
+    for value, natural in zip(wide_rows(rows), naturals):
+        natural[...] = value
+    for rows_out, natural in zip(outs, naturals):
+        for f in range(FRAMES):
+            rows_out[f] = natural[pl.ds(f, PAD, stride=FRAMES), :]
 
 
 def forward_kernel(
-    query_grad, parts, x0, x1, x2, x3,
+    parts, x0, x1, x2, x3,
     normed_out, gate_out, inv_out, inv_row_out, taps_out, rows_out,
     natural, mean_rows, inv_rows,
 ):
-    stats = parts[0, :, HALF_TEXTS:]
+    stats = parts[0, 2 * PAD :, :]
     for peer in range(1, MP):
-        stats = stats + parts[peer, :, HALF_TEXTS:]
+        stats = stats + parts[peer, 2 * PAD :, :]
     natural[...] = jnp.zeros_like(natural)
     for hop, x in enumerate((x0, x1, x2, x3)):
         mean = stats[2 * hop : 2 * hop + 1] / D
         variance = stats[2 * hop + 1 : 2 * hop + 2] / D - mean * mean
         inv = lax.rsqrt(variance + EPSILON)
         inv_row_out[hop : hop + 1, :] = inv
-        mean_rows[...] = wide_rows(mean)
-        inv_rows[...] = wide_rows(inv)
+        mean_rows[...], inv_rows[...] = wide_rows((mean, inv))
         for f in range(FRAMES):
             inv_out[hop, f] = inv_rows[pl.ds(f, PAD, stride=FRAMES), :]
 
@@ -271,19 +289,22 @@
         second[f] += grads[f] * normed[hop, block, f]
 
 
-def write_sums(sums, matrices, out, natural):
-    row = lax.broadcasted_iota(jnp.int32, (PAD, LANES), 0)
-    packed = jnp.zeros((PAD, LANES), F32)
+def write_sums(sums, matrices, out, stacked):
     for index, total in enumerate(sums):
         for f in range(FRAMES):
-            natural[pl.ds(f, PAD, stride=FRAMES), :] = total[f]
-        packed = jnp.where(row == index, lane_sums(natural[...]), packed)
+            stacked[pl.ds(index * LANES + f, PAD, stride=FRAMES), :] = total[f]
+    high, low = split_halves(stacked[...])
+    ones = jnp.ones((16, LANES), BF16)
+    packed = lax.dot_general(ones, high, NT, preferred_element_type=F32)
+    packed = packed + lax.dot_general(ones, low, NT, preferred_element_type=F32)
+    packed = [packed[0:1, index * LANES : (index + 1) * LANES] for index in range(len(sums))]
+    packed = jnp.concatenate(packed + [jnp.zeros((PAD - len(sums), LANES), F32)], 0)
     for peer in range(MP):
         out[peer, 0:PAD, :] = packed
         out[peer, PAD:, :] = matrices
 
 
-def read_sums(parts, inv_row, above, here, natural, above_first, above_second, here_first, here_second):
+def read_sums(parts, inv_row, above, here, stacked, outs):
     total = parts[0]
     for peer in range(1, MP):
         total = total + parts[peer]
@@ -291,22 +312,25 @@
     first = total[0:1] * scale
     second = total[1:2] * scale
     matrix = total[PAD:]
-    products = matrix[0:32] * first + matrix[32:64] * second
+    high, low = split_halves(matrix[0:32] * first + matrix[32:64] * second)
     row = lax.broadcasted_iota(jnp.int32, (LANES, LANES), 0)
     column = lax.broadcasted_iota(jnp.int32, (LANES, LANES), 1)
-    same = jnp.where((row >> 4) == (column >> 4), 1.0, 0.0)
-    products = jnp.dot(
-        products, same, preferred_element_type=F32, precision=lax.Precision.HIGHEST
-    )
+    same = jnp.where((row >> 4) == (column >> 4), 1.0, 0.0).astype(BF16)
+    products = jnp.dot(high, same, preferred_element_type=F32)
+    products = products + jnp.dot(low, same, preferred_element_type=F32)
     keep = (row & (FRAMES - 1)) == (column & (FRAMES - 1))
     keep = keep[0:FRAMES]
     change_first = jnp.sum(jnp.where(keep, products[0:16], 0.0), axis=0, keepdims=True)
     change_second = jnp.sum(jnp.where(keep, products[16:32], 0.0), axis=0, keepdims=True)
-    spread(first, above_first, natural)
-    spread(second, above_second, natural)
     scale = inv_row[pl.ds(here, 1), :] / D
-    spread((total[2:3] - change_first) * scale, here_first, natural)
-    spread((total[3:4] - change_second) * scale, here_second, natural)
+    rows = (
+        first,
+        second,
+        (total[2:3] - change_first) * scale,
+        (total[3:4] - change_second) * scale,
+    )
+    naturals = [stacked.at[pl.ds(index * LANES, LANES)] for index in range(len(rows))]
+    spread(rows, outs, naturals)
 
 
 def write_result(values, natural, result, index, block):
@@ -316,26 +340,25 @@
 
 
 def head_kernel(
-    hops, query_grad, weight, normed, gate, inv, taps_in, matrices,
+    hops, parts, weight, normed, gate, inv, taps_in, matrices,
     up_out, tap_out, sums_out,
-    s0, s1, s2, s3, natural,
+    s0, s1, s2, s3, stacked, full_grad, head_rows,
 ):
+    full_grad[...] = jnp.zeros_like(full_grad)
+    for peer in range(MP):
+        for piece in range(2):
+            start = peer * SLICE + piece * LANES
+            value = parts[peer, piece * PAD : (piece + 1) * PAD, :]
+            value = jnp.concatenate([value, jnp.zeros((PAD, LANES), F32)], 0)
+            full_grad[:, start : start + LANES] = value.astype(BF16)
+    pooled = lax.dot_general(full_grad[...], weight[...], NT, preferred_element_type=F32)
+    head_rows[...] = (pooled[0:PAD] / FRAMES).astype(BF16).astype(F32)
     for total in (s0, s1, s2, s3):
         total[...] = jnp.zeros_like(total)
     three, two = hops[3], hops[2]
 
     def block_step(block, carry):
-        rows = weight[pl.ds(pl.multiple_of(block * LANES, LANES), LANES), :]
-        pooled = None
-        for peer in range(MP):
-            term = lax.dot_general(
-                query_grad[peer],
-                rows[:, peer * SLICE : (peer + 1) * SLICE],
-                NT,
-                preferred_element_type=F32,
-            )
-            pooled = term if pooled is None else pooled + term
-        head = (pooled[0:PAD] / FRAMES).astype(BF16).astype(F32)
+        head = head_rows[:, lanes_of(block)]
         taps = tap_rows(taps_in, three, block)
         grad_conv = [head * gate[three, block, f] for f in range(FRAMES)]
         grads = conv_back(grad_conv, taps)
@@ -351,7 +374,7 @@
         return carry
 
     lax.fori_loop(0, BLOCKS, block_step, 0)
-    write_sums((s0, s1, s2, s3), matrices[0], sums_out, natural)
+    write_sums((s0, s1, s2, s3), matrices[0], sums_out, stacked)
 
 
 def corrected(up, normed, hop, block, first_rows, second_rows):
@@ -363,12 +386,12 @@
 def middle_kernel(
     hops, parts, up, normed, gate, inv, inv_row, taps_in, matrices,
     result, up_out, tap_two, tap_one, sums_out,
-    s0, s1, s2, s3, a0, a1, b0, b1, natural,
+    s0, s1, s2, s3, a0, a1, b0, b1, natural, stacked,
 ):
     for total in (s0, s1, s2, s3):
         total[...] = jnp.zeros_like(total)
     three, two, one, zero = hops[3], hops[2], hops[1], hops[0]
-    read_sums(parts, inv_row, three, two, natural, a0, a1, b0, b1)
+    read_sums(parts, inv_row, three, two, stacked, (a0, a1, b0, b1))
 
     def block_step(block, carry):
         ups = corrected([up[block, f] for f in range(FRAMES)], normed, three, block, a0, a1)
@@ -396,17 +419,17 @@
         return carry
 
     lax.fori_loop(0, BLOCKS, block_step, 0)
-    write_sums((s0, s1, s2, s3), matrices[1], sums_out, natural)
+    write_sums((s0, s1, s2, s3), matrices[1], sums_out, stacked)
 
 
 def end_kernel(
     hops, parts, up, normed, gate, inv, inv_row, taps_in,
     tap_three, tap_two, tap_one, pair_parts,
     result, message,
-    a0, a1, b0, b1, natural, tap_zero, wide,
+    a0, a1, b0, b1, natural, stacked, tap_zero, wide,
 ):
     three, two, one, zero = hops[3], hops[2], hops[1], hops[0]
-    read_sums(parts, inv_row, one, zero, natural, a0, a1, b0, b1)
+    read_sums(parts, inv_row, one, zero, stacked, (a0, a1, b0, b1))
 
     def block_step(block, carry):
         ups = corrected([up[block, f] for f in range(FRAMES)], normed, one, block, a0, a1)
@@ -445,6 +468,11 @@
             @pl.when(steps == target)
             def _(section=section, target=target):
                 outs[target][...] = last[section] if section < 2 else before[3 - section]
+
+
+def tap_sum_kernel(message, out):
+    total = jnp.sum(message[...].astype(F32), axis=0).astype(BF16)
+    out[...] = jnp.broadcast_to(total[None], out.shape)
 
 
 def assemble_kernel(hops, own, first, second, third, tap_sum, out, sems):
@@ -468,6 +496,7 @@
 FRAME_MAJOR = (BLOCKS, FRAMES, PAD, LANES)
 ROW_TILE = pltpu.VMEM((FRAMES, PAD, LANES), F32)
 NATURAL = pltpu.VMEM((LANES, LANES), F32)
+STACKED = pltpu.VMEM((4 * LANES, LANES), F32)
 MATRIX_ROWS = 64
 SMEM = pl.BlockSpec(memory_space=pltpu.SMEM)
 
@@ -502,7 +531,9 @@
     saved_inputs, norm_gains, conv_taps, head_weight, queries, key_embeds, positives, pair_weights
 ):
     section_now = lax.axis_index("section")
-    hops = [(section_now - t) % SECTIONS for t in range(SECTIONS)] + [section_now]
+    hops = [(section_now - t) % SECTIONS for t in range(SECTIONS)]
+    core = lax.axis_index("dp") % 2
+    hops += [section_now, core]
     hops = jnp.stack(hops).astype(jnp.int32)
     inputs_all = saved_inputs[0]
 
@@ -515,31 +546,35 @@
         sections.append(rotate(block, steps) if steps else block)
 
     pairs = jnp.concatenate([key_embeds, queries], -1).reshape(MICRO * SHARD, 2 * SLICE)
-    pairs = jnp.broadcast_to(pairs[None], (DP,) + pairs.shape)
-    texts = lax.all_to_all(pairs, "dp", 0, 0).reshape(TEXTS, 2 * SLICE)
+    pairs = jnp.broadcast_to(pairs[None], (DP // 2,) + pairs.shape)
+    same_core = [list(range(core, DP, 2)) for core in range(2)]
+    texts = lax.all_to_all(pairs, "dp", 0, 0, axis_index_groups=same_core)
+    texts = texts.reshape(HALF_TEXTS, 2 * SLICE)
+    texts, sections[1], sections[3] = lax.optimization_barrier((texts, sections[1], sections[3]))
+    others = lax.ppermute(texts, "dp", [(source, source ^ 1) for source in range(DP)])
 
     own_queries = lax.dynamic_slice_in_dim(queries, OWN * section_now, OWN, 1)
     own_queries = jnp.pad(own_queries.reshape(CLIPS, SLICE), ((0, 16 - CLIPS), (0, 0)))
 
     parts = pl.pallas_call(
-        sums_kernel,
-        out_shape=shape((MP, PAD, HALF_TEXTS + LANES)),
-        in_specs=[SMEM] * 3 + [VMEM] * 6,
+        scores_kernel,
+        out_shape=shape((MP, PAD, HALF_TEXTS)),
+        in_specs=[VMEM] * 5,
         out_specs=VMEM,
         compiler_params=PARAMS,
-        name="row_sums_and_scores",
-    )(hops, positives, pair_weights, *sections, texts, own_queries)
+        name="partial_scores",
+    )(texts, others, own_queries, sections[1], sections[3])
     parts = lax.all_to_all(parts, "mp", 0, 0)
 
-    query_grad, pair_parts = pl.pallas_call(
+    parts, pair_parts = pl.pallas_call(
         softmax_kernel,
-        out_shape=(shape((MP, 16, SLICE), BF16), shape((DP, MICRO, LANES))),
-        in_specs=[SMEM] * 3 + [VMEM] * 2,
+        out_shape=(shape((MP, 3 * PAD, LANES)), shape((DP, MICRO, LANES))),
+        in_specs=[SMEM] * 3 + [VMEM] * 7,
         out_specs=(VMEM, VMEM),
         compiler_params=PARAMS,
-        name="softmax_grads",
-    )(hops, positives, pair_weights, parts, texts)
-    query_grad = lax.all_to_all(query_grad, "mp", 0, 0)
+        name="softmax_grads_and_row_sums",
+    )(hops, positives, pair_weights, parts, texts, others, *sections)
+    parts = lax.all_to_all(parts, "mp", 0, 0)
 
     normed, gate, inv, inv_row, taps, normed_rows = pl.pallas_call(
         forward_kernel,
@@ -551,13 +586,13 @@
             shape((SECTIONS, 16, WIDE)),
             shape((SECTIONS, ROWS, WIDE)),
         ),
-        in_specs=[VMEM] * 6,
+        in_specs=[VMEM] * 5,
         out_specs=(VMEM,) * 6,
         scratch_shapes=[NATURAL] * 3,
         compiler_params=PARAMS,
         cost_estimate=cost(10**9, 6 * 10**6),
         name="sections_forward",
-    )(query_grad, parts, *sections)
+    )(parts, *sections)
     (matrices,) = local_call(
         pair_kernel,
         hops,
@@ -578,9 +613,10 @@
     up, tap_three, sums = local_call(
         head_kernel,
         hops,
-        (query_grad, head_weight, normed, gate, inv, taps, matrices),
+        (parts, head_weight, normed, gate, inv, taps, matrices),
         [shape(FRAME_MAJOR), tap_shape, sums_shape],
-        [ROW_TILE] * 4 + [NATURAL],
+        [ROW_TILE] * 4
+        + [STACKED, pltpu.VMEM((16, EMB), BF16), pltpu.VMEM((PAD, WIDE), F32)],
         "head_and_sections",
     )
     sums = lax.all_to_all(sums, "mp", 0, 0)
@@ -589,7 +625,7 @@
         hops,
         (sums, up, normed, gate, inv, inv_row, taps, matrices),
         [shape((2, ROWS, WIDE), BF16), shape(FRAME_MAJOR), tap_shape, tap_shape, sums_shape],
-        [ROW_TILE] * 8 + [NATURAL],
+        [ROW_TILE] * 8 + [NATURAL, STACKED],
         "middle_sections",
     )
     sums = lax.all_to_all(sums, "mp", 0, 0)
@@ -600,26 +636,23 @@
         (sums, up, normed, gate, inv, inv_row, taps, tap_three, tap_two, tap_one, pair_parts),
         [shape((2, ROWS, WIDE), BF16), shape((DP * SECTIONS * PAD, LANES), BF16)],
         [ROW_TILE] * 4
-        + [NATURAL, pltpu.VMEM((16, WIDE), F32), pltpu.VMEM((DP * SECTIONS, PAD, LANES), F32)],
+        + [NATURAL, STACKED, pltpu.VMEM((16, WIDE), F32), pltpu.VMEM((DP * SECTIONS, PAD, LANES), F32)],
         "end_sections",
     )
     message = lax.all_to_all(
         message.reshape(DP * SECTIONS, PAD, LANES), ("dp", "section"), 0, 0
     )
 
-    tap_sum = jnp.sum(message[:, 0:5].astype(F32), axis=0).astype(BF16)
-    tap_grads = lax.all_to_all(jnp.broadcast_to(tap_sum[None], (DP, 5, LANES)), "dp", 0, 0)
+    tap_sum = pl.pallas_call(
+        tap_sum_kernel,
+        out_shape=shape((DP, PAD, LANES), BF16),
+        in_specs=[VMEM],
+        out_specs=VMEM,
+        compiler_params=PARAMS,
+        name="tap_sums",
+    )(message)
+    tap_grads = lax.all_to_all(tap_sum, "dp", 0, 0)[:, 0:5]
     tap_grads = tap_grads.reshape(16, WIDE)[0:KERNEL].astype(F32)
-
-    columns = message[:, 5:7].reshape(DP, SECTIONS, MICRO, LANES)[..., : OWN * 32]
-    columns = columns.reshape(DP, SECTIONS, MICRO, OWN, 32)[..., : MICRO * SHARD]
-    columns = columns.transpose(0, 2, 1, 3, 4).reshape(TEXTS, MICRO * SHARD)
-    key_grads = (
-        lax.dot_general(
-            columns, texts[:, SLICE:], (((0,), (0,)), ((), ())), preferred_element_type=F32
-        )
-        * SCORE_SCALE
-    ).reshape(MICRO, SHARD, SLICE)
 
     ordered = local_call(
         order_kernel,
@@ -642,6 +675,21 @@
         cost_estimate=cost(10**10, 10**7),
         name="assemble_results",
     )(hops, *pieces, tap_sum)
+    message, results = lax.optimization_barrier((message, results))
+    columns = message[:, 5:7].reshape(DP, SECTIONS, MICRO, LANES)[..., : OWN * 32]
+    columns = columns.reshape(DP, SECTIONS, MICRO, OWN, 32)[..., : MICRO * SHARD]
+    columns = columns.transpose(0, 2, 1, 3, 4).reshape(DP // 2, 2, MICRO * SHARD, MICRO * SHARD)
+    key_grads = 0.0
+    for half, part in enumerate((texts, others)):
+        pair_grad = lax.dynamic_index_in_dim(columns, core ^ half, 1, keepdims=False)
+        key_grads = key_grads + lax.dot_general(
+            pair_grad.reshape(HALF_TEXTS, MICRO * SHARD),
+            part[:, SLICE:],
+            (((0,), (0,)), ((), ())),
+            preferred_element_type=F32,
+        )
+    key_grads = (key_grads * SCORE_SCALE).reshape(MICRO, SHARD, SLICE)
+
     return (results[None], tap_grads[None], key_grads)
 
 

time: 153 us -> 151 us (0.987)
  blocking collectives: 41.6 us -> 29.4 us
  starting transfers between devices: 58 us -> 67 us
    all_to_all x1 -> x0, blocking collectives: 9.06 us -> none  [per_device(): query_grad = lax.all_to_all(query_grad, 'mp', 0, 0)]
    all_to_all x2 -> x3, waiting for transfers between devices: 5.84 us -> 10.6 us  [the longest x1 6.73 us: per_device(): parts = lax.all_to_all(parts, 'mp', 0, 0)]
    all_to_all x2 -> x3, starting transfers between devices: 21.4 us -> 26.2 us  [the longest x1 12 us: per_device(): texts = lax.all_to_all(pairs, 'dp', 0, 0, axis_index_groups=same_core)]
    ppermute x6, waiting for transfers between devices: 9.79 us -> 5.61 us  [rotate(): return lax.ppermute(value, 'section', pairs)]
    ppermute x0 -> x1, starting transfers between devices: none -> 4.06 us  [per_device(): lax.ppermute(texts, 'dp', [(source, source ^ 1) for source in range(DP)])]
    all_to_all x1, blocking collectives: 12.9 us -> 9.23 us  [per_device(): parts = lax.all_to_all(parts, 'mp', 0, 0)]
    pallas_call x5, Pallas kernels: 20.3 us -> 18.6 us  [local_call(): pl.pallas_call(kernel, out_shape=outs, in_specs=[SMEM] + [VMEM] * len(ope...]
  transfers between devices with their start and end apart: 9 -> 11, of which waited for: 5 -> 5; matrix products, arithmetic and copies ran while one was open for 2% -> 4% of each run, Pallas kernels for 1% -> 3%
where the time goes in v5:
time: 151 us; the launch traced here: 150 us
  starting transfers between devices  67 us (44%)
  blocking collectives  29.4 us (19%)
  Pallas kernels  27.9 us (18%)
  waiting for transfers between devices  17.4 us (12%)
  local copies, waits for them, and re-layouts  5.78 us (4%)
  other arithmetic  1.54 us (1%)
    ppermute x6, starting transfers between devices, rotate(): return lax.ppermute(value, 'section', pairs)  21.5 us
    all_to_all x2, blocking collectives, per_device(): sums = lax.all_to_all(sums, 'mp', 0, 0)  20.2 us
    pallas_call x5, Pallas kernels, local_call(): pl.pallas_call(kernel, out_shape=outs, in_specs=[SMEM] + [VMEM] * len(ope...  18.6 us
    all_to_all x1, starting transfers between devices, per_device(): lax.all_to_all(message.reshape(DP * SECTIONS, PAD, LANES), ('dp', 'sectio...  15.2 us
    all_to_all x1, starting transfers between devices, per_device(): texts = lax.all_to_all(pairs, 'dp', 0, 0, axis_index_groups=same_core)  12 us
    all_to_all x1, blocking collectives, per_device(): parts = lax.all_to_all(parts, 'mp', 0, 0)  9.23 us
    all_to_all x1, starting transfers between devices, per_device(): tap_grads = lax.all_to_all(tap_sum, 'dp', 0, 0)[:, 0:5]  8.31 us
    all_to_all x1, waiting for transfers between devices, per_device(): parts = lax.all_to_all(parts, 'mp', 0, 0)  6.73 us
  transfers between devices with their start and end apart: 11, of which 5 were waited for; matrix products, arithmetic and copies ran while one was open for 4% of the time, Pallas kernels for 3%

profile of v5, /device:TPU:1, one launch (start us, length us, event | category | flops | bytes accessed | tf_op | source)
XLA Modules:
  0.0 150.4 jit_solution(10891384735975088926)
XLA Ops:
  0.6 0.8 pad_maximum_fusion.8
  1.4 0.8 broadcast_in_dim.12
  2.2 12.0 %all-to-all-start = ((bf16[16,24,512]{2,1,0:T(8,128)(2,1)}), bf16[16,24,512]{2,1,0:T(8,128)(2,1)S(1)}, u32[]{:S(2)}, u32[]{:S(2)}) async-start(bf16[16,24,512]{2,1,0:T(8,128)(2,1)} %broadcast_in_dim.12), calls=%async_computation | async-start | bytes 786432 | tf_op jit(solution)/shard_map/all_to_all | solution.py:551
  15.0 1.4 constant_dynamic-slice_fusion.2
  16.5 3.1 %collective-permute-start = (bf16[112,1280]{1,0:T(8,128)(2,1)S(1)}, bf16[112,1280]{1,0:T(8,128)(2,1)S(1)}, u32[]{:S(2)}, u32[]{:S(2)}) collective-permute-start(bf16[112,1280]{1,0:T(8,128)(2,1)S(1)} %get-tuple-element.75), channel_id=1, source_target_pairs={{0,4},{4,8},{8,12},{12,0},{1,5},{5,9},{9,13},{13,1},{2,6},{6,10},{... | collective-permute-start | bytes 860168 | tf_op jit(solution)/shard_map/ppermute | solution.py:527
  19.6 3.4 %collective-permute-start.1 = (bf16[112,1280]{1,0:T(8,128)(2,1)S(1)}, bf16[112,1280]{1,0:T(8,128)(2,1)S(1)}, u32[]{:S(2)}, u32[]{:S(2)}) collective-permute-start(bf16[112,1280]{1,0:T(8,128)(2,1)S(1)} %get-tuple-element.73), channel_id=1, source_target_pairs={{0,12},{4,0},{8,4},{12,8},{1,13},{5,1},{9,5},{13,9},{2,14},{6,2},{... | collective-permute-start | bytes 860168 | tf_op jit(solution)/shard_map/ppermute | solution.py:527
  23.0 4.0 %collective-permute-done.x1 = bf16[112,1280]{1,0:T(8,128)(2,1)S(1)} collective-permute-done((bf16[112,1280]{1,0:T(8,128)(2,1)S(1)}, bf16[112,1280]{1,0:T(8,128)(2,1)S(1)}, u32[]{:S(2)}, u32[]{:S(2)}) %collective-permute-start) | collective-permute-done | bytes 286752 | tf_op jit(solution)/shard_map/ppermute | solution.py:527
  26.9 1.6 %collective-permute-done.1.x3 = bf16[112,1280]{1,0:T(8,128)(2,1)S(1)} collective-permute-done((bf16[112,1280]{1,0:T(8,128)(2,1)S(1)}, bf16[112,1280]{1,0:T(8,128)(2,1)S(1)}, u32[]{:S(2)}, u32[]{:S(2)}) %collective-permute-start.1) | collective-permute-done | bytes 286752 | tf_op jit(solution)/shard_map/ppermute | solution.py:527
  28.6 4.1 %collective-permute-start.2 = (bf16[384,512]{1,0:T(8,128)(2,1)S(1)}, bf16[384,512]{1,0:T(8,128)(2,1)S(1)}, u32[]{:S(2)}, u32[]{:S(2)}) collective-permute-start(bf16[384,512]{1,0:T(8,128)(2,1)S(1)} %bitcast.37), channel_id=1, source_target_pairs={{0,16},{16,0},{32,48},{48,32},{64,80},{80,64},{96,112},{112,96},{1... | collective-permute-start | bytes 1179656 | tf_op jit(solution)/shard_map/ppermute | solution.py:554
  32.6 4.4 %collective-permute-start.3 = (bf16[112,1280]{1,0:T(8,128)(2,1)S(1)}, bf16[112,1280]{1,0:T(8,128)(2,1)S(1)}, u32[]{:S(2)}, u32[]{:S(2)}) collective-permute-start(bf16[112,1280]{1,0:T(8,128)(2,1)S(1)} %get-tuple-element.72), channel_id=1, source_target_pairs={{0,8},{4,12},{8,0},{12,4},{1,9},{5,13},{9,1},{13,5},{2,10},{6,14},... | collective-permute-start | bytes 860168 | tf_op jit(solution)/shard_map/ppermute | solution.py:527
  37.7 0.8 partial_scores.1
  38.6 5.9 %all-to-all-start.1 = ((f32[4,8,384]{2,1,0:T(8,128)}), f32[4,8,384]{2,1,0:T(8,128)S(1)}, u32[]{:S(2)}, u32[]{:S(2)}) async-start(f32[4,8,384]{2,1,0:T(8,128)} %partial_scores.1), calls=%async_computation.1 | async-start | bytes 98304 | tf_op jit(solution)/shard_map/all_to_all | solution.py:567
  44.6 6.7 %all-to-all-done.1.parts = f32[4,8,384]{2,1,0:T(8,128)S(1)} async-done(((f32[4,8,384]{2,1,0:T(8,128)}), f32[4,8,384]{2,1,0:T(8,128)S(1)}, u32[]{:S(2)}, u32[]{:S(2)}) %all-to-all-start.1) | async-done | bytes 49184 | tf_op jit(solution)/shard_map/all_to_all | solution.py:567
  51.3 1.4 softmax_grads_and_row_sums.1
  52.7 9.2 %all_to_all.35.parts = f32[4,24,128]{2,1,0:T(8,128)S(1)} all-to-all(f32[4,24,128]{2,1,0:T(8,128)S(1)} %get-tuple-element.33), channel_id=1, replica_groups=mesh['dp'=32,'section'=4,'mp'=4] {'mp'}, dimensions={0} | all-to-all | bytes 98304 | tf_op jit(solution)/shard_map/all_to_all | solution.py:577
  61.9 4.8 %sections_forward.1 = (f32[4,10,16,8,128]{4,3,2,1,0:T(8,128)S(1)}, f32[4,10,16,8,128]{4,3,2,1,0:T(8,128)S(1)}, f32[4,16,8,128]{3,2,1,0:T(8,128)S(1)}, f32[8,128]...) custom-call(f32[4,24,128]{2,1,0:T(8,128)S(1)} %all_to_all.35.parts, ...), custom_call_target="tpu_custom_call" | custom-call | flops 1000000000 | bytes 6000000 | tf_op jit(solution)/shard_map/sections_forward/pallas_call | solution.py:579
  66.7 5.5 %pair_matrices.1.matrices = f32[2,64,128]{2,1,0:T(8,128)S(1)} custom-call(s32[6]{0:T(128)S(1)} %stack.27.hops, f32[4,96,1280]{2,1,0:T(8,128)S(1)} %get-tuple-element.38.normed_rows, f32[4,10,16,8,128]{4,3,2,1,0:T(8,128)S(1)} %get-tuple-element.35.gate, f32[4,16,1280]{2,1,0:T(8,128)S(1)} %get-tuple-element.37.taps_in), custom_call_target="tpu_custom_call" | custom-call | flops 3000000000 | bytes 6000000 | tf_op jit(solution)/shard_map/pair_matrices/pallas_call | solution.py:513
  72.3 3.6 %head_and_sections.1 = (f32[10,16,8,128]{3,2,1,0:T(8,128)S(1)}, f32[16,1280]{1,0:T(8,128)S(1)}, f32[4,72,128]{2,1,0:T(8,128)S(1)}) custom-call(s32[6]{0:T(128)S(1)} %stack.27.hops, f32[4,24,128]{2,1,0:T(8,128)S(1)} %all_to_all.35.parts, bf16[1280,1024]{1,0:T(8,128)(2,1)S(1)} %copy-done, f32[4,10,16,8,128]{4,3,2,1,0:T(8,128)S(1)} %get-tuple-element.34.normed, ...), custom_call_target="tpu_custom_call" | custom-call | tf_op jit(solution)/shard_map/head_and_sections/pallas_call | solution.py:513
  75.9 10.4 %all_to_all.36.parts = f32[4,72,128]{2,1,0:T(8,128)S(1)} all-to-all(f32[4,72,128]{2,1,0:T(8,128)S(1)} %get-tuple-element.39), channel_id=1, replica_groups=mesh['dp'=32,'section'=4,'mp'=4] {'mp'}, dimensions={0} | all-to-all | bytes 294912 | tf_op jit(solution)/shard_map/all_to_all | solution.py:622
  86.3 5.0 %middle_sections.1 = (bf16[2,96,1280]{2,1,0:T(8,128)(2,1)S(1)}, f32[10,16,8,128]{3,2,1,0:T(8,128)S(1)}, f32[16,1280]{1,0:T(8,128)S(1)}, f32[16,1280]{1,0:T(8,128)S(1)}, f32[4,72,128]{2,1,0:T(8,128)S(1)}) custom-call(s32[6]{0:T(128)S(1)} %stack.27.hops, f32[4,72,128]{2,1,0:T(8,128)S(1)} %all_to_all.36.parts, f32[10,16,8,128]{3,2,1,0:T(8,128)S(1)} %get-tuple-element.40.up, ...), custom_call_target="tpu_custom_call" | custom-call | tf_op jit(solution)/shard_map/middle_sections/pallas_call | solution.py:513
  91.3 9.8 %all_to_all.37.parts = f32[4,72,128]{2,1,0:T(8,128)S(1)} all-to-all(f32[4,72,128]{2,1,0:T(8,128)S(1)} %get-tuple-element.42), channel_id=1, replica_groups=mesh['dp'=32,'section'=4,'mp'=4] {'mp'}, dimensions={0} | all-to-all | bytes 294912 | tf_op jit(solution)/shard_map/all_to_all | solution.py:631
  101.1 3.8 %end_sections.1 = (bf16[2,96,1280]{2,1,0:T(8,128)(2,1)S(1)}, bf16[1024,128]{1,0:T(8,128)(2,1)}) custom-call(s32[6]{0:T(128)S(1)} %stack.27.hops, f32[4,72,128]{2,1,0:T(8,128)S(1)} %all_to_all.37.parts, f32[10,16,8,128]{3,2,1,0:T(8,128)S(1)} %get-tuple-element.43.up, f32[4,10,16,8,128]{4,3,2,1,0:T(8,128)S(1)} %get-tuple-element.34.normed, ...), custom_call_target="tpu_custom_call" | custom-call | tf_op jit(solution)/shard_map/end_sections/pallas_call | solution.py:513
  104.9 15.2 %all-to-all-start.5 = ((bf16[128,8,128]{2,1,0:T(8,128)(2,1)}), bf16[128,8,128]{2,1,0:T(8,128)(2,1)S(1)}, u32[]{:S(2)}, u32[]{:S(2)}) async-start(bf16[128,8,128]{2,1,0:T(8,128)(2,1)} %bitcast.12), calls=%async_computation.5 | async-start | bytes 524288 | tf_op jit(solution)/shard_map/all_to_all | solution.py:642
  120.7 3.3 %collective-permute-start.4 = (bf16[96,1280]{1,0:T(8,128)(2,1)S(1)}, bf16[96,1280]{1,0:T(8,128)(2,1)S(1)}, u32[]{:S(2)}, u32[]{:S(2)}) collective-permute-start(bf16[96,1280]{1,0:T(8,128)(2,1)S(1)} %get-tuple-element.52), channel_id=1, source_target_pairs={{0,4},{4,8},{8,12},{12,0},{1,5},{5,9},{9,13},{13,1},{2,6},{6,10},{... | collective-permute-start | bytes 737288 | tf_op jit(solution)/shard_map/ppermute | solution.py:527
  124.0 4.3 %collective-permute-start.5 = (bf16[96,1280]{1,0:T(8,128)(2,1)S(1)}, bf16[96,1280]{1,0:T(8,128)(2,1)S(1)}, u32[]{:S(2)}, u32[]{:S(2)}) collective-permute-start(bf16[96,1280]{1,0:T(8,128)(2,1)S(1)} %get-tuple-element.53), channel_id=1, source_target_pairs={{0,8},{4,12},{8,0},{12,4},{1,9},{5,13},{9,1},{13,5},{2,10},{6,14},... | collective-permute-start | bytes 737288 | tf_op jit(solution)/shard_map/ppermute | solution.py:527
  128.4 3.1 %collective-permute-start.6 = (bf16[96,1280]{1,0:T(8,128)(2,1)S(1)}, bf16[96,1280]{1,0:T(8,128)(2,1)S(1)}, u32[]{:S(2)}, u32[]{:S(2)}) collective-permute-start(bf16[96,1280]{1,0:T(8,128)(2,1)S(1)} %get-tuple-element.54), channel_id=1, source_target_pairs={{0,12},{4,0},{8,4},{12,8},{1,13},{5,1},{9,5},{13,9},{2,14},{6,2},{... | collective-permute-start | bytes 737288 | tf_op jit(solution)/shard_map/ppermute | solution.py:527
  131.5 1.1 all-to-all-done.5.message
  132.6 0.8 tap_sums.1.tap_sum
  133.4 8.3 %all-to-all-start.6 = ((bf16[32,8,128]{2,1,0:T(8,128)(2,1)}), bf16[32,8,128]{2,1,0:T(8,128)(2,1)S(1)}, u32[]{:S(2)}, u32[]{:S(2)}) async-start(bf16[32,8,128]{2,1,0:T(8,128)(2,1)} %tap_sums.1.tap_sum), calls=%async_computation.6 | async-start | bytes 131072 | tf_op jit(solution)/shard_map/all_to_all | solution.py:654
  141.7 1.5 %assemble_results.1 = bf16[2,12,16,1280]{3,2,1,0:T(8,128)(2,1)} custom-call(s32[6]{0:T(128)S(1)} %stack.27.hops, bf16[6,16,1280]{2,1,0:T(8,128)(2,1)S(1)} %bitcast.44, bf16[6,16,1280]{2,1,0:T(8,128)(2,1)S(1)} %bitcast.41, bf16[6,16,1280]{2,1,0:T(8,128)(2,1)S(1)} %bitcast.42, bf16[6,16,1280]{2,1,0:T(8,128)(2,1)S(1)} %bitcast.43, ...), custom_call_target="tpu_custom_call" | custom-call | flops 10000000000 | bytes 10000000 | tf_op jit(solution)/shard_map/assemble_results/pallas_call | solution.py:668
  145.7 3.9 %all-to-all-done.6 = bf16[32,8,128]{2,1,0:T(8,128)(2,1)S(1)} async-done(((bf16[32,8,128]{2,1,0:T(8,128)(2,1)}), bf16[32,8,128]{2,1,0:T(8,128)(2,1)S(1)}, u32[]{:S(2)}, u32[]{:S(2)}) %all-to-all-start.6) | async-done | bytes 65568 | tf_op jit(solution)/shard_map/all_to_all | solution.py:654
  149.6 0.7 reshape.100
  (39 shorter events, 4.7 us)
Async XLA Ops:
  0.6 15.7 %copy-start.3 = (bf16[1,15,1280]{2,1,0:T(8,128)(2,1)S(1)}, bf16[1,15,1280]{2,1,0:T(8,128)(2,1)}, u32[]{:S(2)}) copy-start(bf16[1,15,1280]{2,1,0:T(8,128)(2,1)} %param.10) | copy-start | bytes 115204
  2.2 26.4 %all-to-all-start = ((bf16[16,24,512]{2,1,0:T(8,128)(2,1)}), bf16[16,24,512]{2,1,0:T(8,128)(2,1)S(1)}, u32[]{:S(2)}, u32[]{:S(2)}) async-start(bf16[16,24,512]{2,1,0:T(8,128)(2,1)} %broadcast_in_dim.12), calls=%async_computation | async-start | bytes 786432 | tf_op jit(solution)/shard_map/all_to_all | solution.py:551
  15.0 36.4 %copy-start.1 = (s32[2,12]{1,0:T(2,128)S(1)}, s32[2,12]{1,0:T(2,128)}, u32[]{:S(2)}) copy-start(s32[2,12]{1,0:T(2,128)} %positives.1) | copy-start | bytes 292
  15.0 36.4 %copy-start.2 = (f32[2,12]{1,0:T(2,128)S(1)}, f32[2,12]{1,0:T(2,128)}, u32[]{:S(2)}) copy-start(f32[2,12]{1,0:T(2,128)} %weights.1) | copy-start | bytes 292
  16.5 10.5 %collective-permute-start = (bf16[112,1280]{1,0:T(8,128)(2,1)S(1)}, bf16[112,1280]{1,0:T(8,128)(2,1)S(1)}, u32[]{:S(2)}, u32[]{:S(2)}) collective-permute-start(bf16[112,1280]{1,0:T(8,128)(2,1)S(1)} %get-tuple-element.75), channel_id=1, source_target_pairs={{0,4},{4,8},{8,12},{12,0},{1,5},{5,9},{9,13},{13,1},{2,6},{6,10},{... | collective-permute-start | bytes 860168 | tf_op jit(solution)/shard_map/ppermute | solution.py:527
  19.6 9.0 %collective-permute-start.1 = (bf16[112,1280]{1,0:T(8,128)(2,1)S(1)}, bf16[112,1280]{1,0:T(8,128)(2,1)S(1)}, u32[]{:S(2)}, u32[]{:S(2)}) collective-permute-start(bf16[112,1280]{1,0:T(8,128)(2,1)S(1)} %get-tuple-element.73), channel_id=1, source_target_pairs={{0,12},{4,0},{8,4},{12,8},{1,13},{5,1},{9,5},{13,9},{2,14},{6,2},{... | collective-permute-start | bytes 860168 | tf_op jit(solution)/shard_map/ppermute | solution.py:527
  28.6 9.2 %collective-permute-start.2 = (bf16[384,512]{1,0:T(8,128)(2,1)S(1)}, bf16[384,512]{1,0:T(8,128)(2,1)S(1)}, u32[]{:S(2)}, u32[]{:S(2)}) collective-permute-start(bf16[384,512]{1,0:T(8,128)(2,1)S(1)} %bitcast.37), channel_id=1, source_target_pairs={{0,16},{16,0},{32,48},{48,32},{64,80},{80,64},{96,112},{112,96},{1... | collective-permute-start | bytes 1179656 | tf_op jit(solution)/shard_map/ppermute | solution.py:554
  32.6 11.9 %collective-permute-start.3 = (bf16[112,1280]{1,0:T(8,128)(2,1)S(1)}, bf16[112,1280]{1,0:T(8,128)(2,1)S(1)}, u32[]{:S(2)}, u32[]{:S(2)}) collective-permute-start(bf16[112,1280]{1,0:T(8,128)(2,1)S(1)} %get-tuple-element.72), channel_id=1, source_target_pairs={{0,8},{4,12},{8,0},{12,4},{1,9},{5,13},{9,1},{13,5},{2,10},{6,14},... | collective-permute-start | bytes 860168 | tf_op jit(solution)/shard_map/ppermute | solution.py:527
  38.6 12.7 %all-to-all-start.1 = ((f32[4,8,384]{2,1,0:T(8,128)}), f32[4,8,384]{2,1,0:T(8,128)S(1)}, u32[]{:S(2)}, u32[]{:S(2)}) async-start(f32[4,8,384]{2,1,0:T(8,128)} %partial_scores.1), calls=%async_computation.1 | async-start | bytes 98304 | tf_op jit(solution)/shard_map/all_to_all | solution.py:567
  66.7 5.5 %copy-start = (bf16[1280,1024]{1,0:T(8,128)(2,1)S(1)}, bf16[1280,1024]{1,0:T(8,128)(2,1)}, u32[]{:S(2)}) copy-start(bf16[1280,1024]{1,0:T(8,128)(2,1)} %weight.1) | copy-start | bytes 7864324
  104.9 27.7 %all-to-all-start.5 = ((bf16[128,8,128]{2,1,0:T(8,128)(2,1)}), bf16[128,8,128]{2,1,0:T(8,128)(2,1)S(1)}, u32[]{:S(2)}, u32[]{:S(2)}) async-start(bf16[128,8,128]{2,1,0:T(8,128)(2,1)} %bitcast.12), calls=%async_computation.5 | async-start | bytes 524288 | tf_op jit(solution)/shard_map/all_to_all | solution.py:642
  120.7 21.0 %collective-permute-start.4 = (bf16[96,1280]{1,0:T(8,128)(2,1)S(1)}, bf16[96,1280]{1,0:T(8,128)(2,1)S(1)}, u32[]{:S(2)}, u32[]{:S(2)}) collective-permute-start(bf16[96,1280]{1,0:T(8,128)(2,1)S(1)} %get-tuple-element.52), channel_id=1, source_target_pairs={{0,4},{4,8},{8,12},{12,0},{1,5},{5,9},{9,13},{13,1},{2,6},{6,10},{... | collective-permute-start | bytes 737288 | tf_op jit(solution)/shard_map/ppermute | solution.py:527
  124.0 17.7 %collective-permute-start.5 = (bf16[96,1280]{1,0:T(8,128)(2,1)S(1)}, bf16[96,1280]{1,0:T(8,128)(2,1)S(1)}, u32[]{:S(2)}, u32[]{:S(2)}) collective-permute-start(bf16[96,1280]{1,0:T(8,128)(2,1)S(1)} %get-tuple-element.53), channel_id=1, source_target_pairs={{0,8},{4,12},{8,0},{12,4},{1,9},{5,13},{9,1},{13,5},{2,10},{6,14},... | collective-permute-start | bytes 737288 | tf_op jit(solution)/shard_map/ppermute | solution.py:527
  128.4 13.4 %collective-permute-start.6 = (bf16[96,1280]{1,0:T(8,128)(2,1)S(1)}, bf16[96,1280]{1,0:T(8,128)(2,1)S(1)}, u32[]{:S(2)}, u32[]{:S(2)}) collective-permute-start(bf16[96,1280]{1,0:T(8,128)(2,1)S(1)} %get-tuple-element.54), channel_id=1, source_target_pairs={{0,12},{4,0},{8,4},{12,8},{1,13},{5,1},{9,5},{13,9},{2,14},{6,2},{... | collective-permute-start | bytes 737288 | tf_op jit(solution)/shard_map/ppermute | solution.py:527
  133.4 16.3 %all-to-all-start.6 = ((bf16[32,8,128]{2,1,0:T(8,128)(2,1)}), bf16[32,8,128]{2,1,0:T(8,128)(2,1)S(1)}, u32[]{:S(2)}, u32[]{:S(2)}) async-start(bf16[32,8,128]{2,1,0:T(8,128)(2,1)} %tap_sums.1.tap_sum), calls=%async_computation.6 | async-start | bytes 131072 | tf_op jit(solution)/shard_map/all_to_all | solution.py:654

commit v6 on v5

--- a/solution.py
+++ b/solution.py
@@ -65,12 +65,8 @@
     return ((column * 10923) >> 17) & 1
 
 
-def scores_kernel(texts, others, query, x1, x3, out):
-    scores = [
-        lax.dot_general(query[...], part[:, 0:SLICE], NT, preferred_element_type=F32)
-        for part in (texts, others)
-    ]
-    scores = jnp.concatenate(scores, 1)
+def scores_kernel(texts, query, out):
+    scores = lax.dot_general(query[...], texts[:, 0:SLICE], NT, preferred_element_type=F32)
     shared = jnp.where(text_micros(OWN) == 0, scores[0:OWN], scores[OWN:CLIPS])
     for peer in range(MP):
         out[peer, 0:OWN, :] = shared[:, 0:HALF_TEXTS]
@@ -79,7 +75,7 @@
 
 
 def softmax_kernel(
-    hops, positives, weights, parts, texts, others, x0, x1, x2, x3, message, pair_parts
+    hops, positives, weights, parts, texts, x0, x1, x2, x3, message, pair_parts
 ):
     rows = []
     for x in (x0, x1, x2, x3):
@@ -112,18 +108,14 @@
         for own in range(OWN):
             index = positives[micro, base + own]
             owner = (index * 10923) >> 17
-            place = ((owner & 1) ^ hops[SECTIONS + 1]) * (DP // 2) + (owner >> 1)
-            index = place * (MICRO * SHARD) + micro * SHARD + (index - owner * SHARD)
+            index = owner * (MICRO * SHARD) + micro * SHARD + (index - owner * SHARD)
             here = row == micro * OWN + own
             positive = jnp.where(here, index, positive)
             weight = jnp.where(here, weights[micro, base + own], weight)
     hot = jnp.where(column == positive, 1.0, 0.0)
     grad = weight * (probs - hot)
     grad = jnp.concatenate([grad, jnp.zeros((PAD, TEXTS), F32)], 0).astype(BF16)
-    result = jnp.dot(grad[:, 0:HALF_TEXTS], texts[:, 0:SLICE], preferred_element_type=F32)
-    result = result + jnp.dot(
-        grad[:, HALF_TEXTS:], others[:, 0:SLICE], preferred_element_type=F32
-    )
+    result = jnp.dot(grad, texts[:, 0:SLICE], preferred_element_type=F32)
     result = (result * SCORE_SCALE)[0:PAD]
     for peer in range(MP):
         message[peer, 0:PAD, :] = result[:, 0:LANES]
@@ -132,10 +124,8 @@
     grad = grad.astype(F32)
     gap = jnp.zeros((1, 32 - MICRO * SHARD), F32)
     tail = jnp.zeros((1, LANES - OWN * 32), F32)
-    for place in range(DP):
-        start = place * MICRO * SHARD
-        half = hops[SECTIONS + 1] ^ (place // (DP // 2))
-        target = (place % (DP // 2)) * 2 + half
+    for target in range(DP):
+        start = target * MICRO * SHARD
         for micro in range(MICRO):
             pieces = []
             for own in range(OWN):
@@ -222,13 +212,15 @@
                 gate_rows[0:ROWS, :] * normed_rows[above, :, lanes]
             ).astype(BF16)
             right[LANES + ROWS :, lanes] = jnp.zeros((LANES - ROWS, LANES), BF16)
+            taps = [
+                jnp.broadcast_to(weights[k : k + 1], (FRAMES, LANES)).astype(BF16)
+                for k in range(KERNEL)
+            ]
             for c in range(CLIPS):
-                value = normed_rows[here, c * FRAMES : (c + 1) * FRAMES, lanes]
+                value = normed_rows[here, c * FRAMES : (c + 1) * FRAMES, lanes].astype(BF16)
                 for k in range(KERNEL):
                     start = (c * KERNEL + k) * FRAMES
-                    left[start : start + FRAMES, lanes] = (value * weights[k : k + 1]).astype(
-                        BF16
-                    )
+                    left[start : start + FRAMES, lanes] = value * taps[k]
             return carry
 
         lax.fori_loop(0, BLOCKS, block_step, 0)
@@ -532,26 +524,23 @@
 ):
     section_now = lax.axis_index("section")
     hops = [(section_now - t) % SECTIONS for t in range(SECTIONS)]
-    core = lax.axis_index("dp") % 2
-    hops += [section_now, core]
+    hops += [section_now]
     hops = jnp.stack(hops).astype(jnp.int32)
     inputs_all = saved_inputs[0]
 
     small = jnp.concatenate([conv_taps[0], norm_gains.astype(BF16)], 0)
-    sections = []
-    for steps in range(SECTIONS):
+    sections = [None] * SECTIONS
+    for steps in (0, 1, 2, 3):
         target = (section_now + steps) % SECTIONS
         block = lax.dynamic_slice_in_dim(inputs_all, OWN * target, OWN, 1)
         block = jnp.concatenate([block.reshape(ROWS, WIDE), small], 0)
-        sections.append(rotate(block, steps) if steps else block)
+        sections[steps] = rotate(block, steps) if steps else block
 
     pairs = jnp.concatenate([key_embeds, queries], -1).reshape(MICRO * SHARD, 2 * SLICE)
-    pairs = jnp.broadcast_to(pairs[None], (DP // 2,) + pairs.shape)
-    same_core = [list(range(core, DP, 2)) for core in range(2)]
-    texts = lax.all_to_all(pairs, "dp", 0, 0, axis_index_groups=same_core)
-    texts = texts.reshape(HALF_TEXTS, 2 * SLICE)
-    texts, sections[1], sections[3] = lax.optimization_barrier((texts, sections[1], sections[3]))
-    others = lax.ppermute(texts, "dp", [(source, source ^ 1) for source in range(DP)])
+    pairs = jnp.broadcast_to(pairs[None], (DP,) + pairs.shape)
+    texts = lax.all_to_all(pairs, "dp", 0, 0).reshape(TEXTS, 2 * SLICE)
+    texts, *sections = lax.optimization_barrier((texts, *sections[::-1]))
+    sections = sections[::-1]
 
     own_queries = lax.dynamic_slice_in_dim(queries, OWN * section_now, OWN, 1)
     own_queries = jnp.pad(own_queries.reshape(CLIPS, SLICE), ((0, 16 - CLIPS), (0, 0)))
@@ -559,21 +548,21 @@
     parts = pl.pallas_call(
         scores_kernel,
         out_shape=shape((MP, PAD, HALF_TEXTS)),
-        in_specs=[VMEM] * 5,
+        in_specs=[VMEM] * 2,
         out_specs=VMEM,
         compiler_params=PARAMS,
         name="partial_scores",
-    )(texts, others, own_queries, sections[1], sections[3])
+    )(texts, own_queries)
     parts = lax.all_to_all(parts, "mp", 0, 0)
 
     parts, pair_parts = pl.pallas_call(
         softmax_kernel,
         out_shape=(shape((MP, 3 * PAD, LANES)), shape((DP, MICRO, LANES))),
-        in_specs=[SMEM] * 3 + [VMEM] * 7,
+        in_specs=[SMEM] * 3 + [VMEM] * 6,
         out_specs=(VMEM, VMEM),
         compiler_params=PARAMS,
         name="softmax_grads_and_row_sums",
-    )(hops, positives, pair_weights, parts, texts, others, *sections)
+    )(hops, positives, pair_weights, parts, texts, *sections)
     parts = lax.all_to_all(parts, "mp", 0, 0)
 
     normed, gate, inv, inv_row, taps, normed_rows = pl.pallas_call(
@@ -678,18 +667,11 @@
     message, results = lax.optimization_barrier((message, results))
     columns = message[:, 5:7].reshape(DP, SECTIONS, MICRO, LANES)[..., : OWN * 32]
     columns = columns.reshape(DP, SECTIONS, MICRO, OWN, 32)[..., : MICRO * SHARD]
-    columns = columns.transpose(0, 2, 1, 3, 4).reshape(DP // 2, 2, MICRO * SHARD, MICRO * SHARD)
-    key_grads = 0.0
-    for half, part in enumerate((texts, others)):
-        pair_grad = lax.dynamic_index_in_dim(columns, core ^ half, 1, keepdims=False)
-        key_grads = key_grads + lax.dot_general(
-            pair_grad.reshape(HALF_TEXTS, MICRO * SHARD),
-            part[:, SLICE:],
-            (((0,), (0,)), ((), ())),
-            preferred_element_type=F32,
-        )
+    columns = columns.transpose(0, 2, 1, 3, 4).reshape(TEXTS, MICRO * SHARD)
+    key_grads = lax.dot_general(
+        columns, texts[:, SLICE:], (((0,), (0,)), ((), ())), preferred_element_type=F32
+    )
     key_grads = (key_grads * SCORE_SCALE).reshape(MICRO, SHARD, SLICE)
-
     return (results[None], tap_grads[None], key_grads)
 
 

time: 151 us -> 150 us (level)
  waiting for transfers between devices: 17.4 us -> 22.1 us
  starting transfers between devices: 67 us -> 64 us
  local copies, waits for them, and re-layouts: 5.78 us -> 3.79 us
    ppermute x1 -> x0, starting transfers between devices: 4.06 us -> none  [per_device(): lax.ppermute(texts, 'dp', [(source, source ^ 1) for source in range(DP)])]
    all_to_all x1, waiting for transfers between devices: 0.01 us -> 2.86 us  [per_device(): texts = lax.all_to_all(pairs, 'dp', 0, 0).reshape(TEXTS, 2 * SLICE)]
  transfers between devices with their start and end apart: 11 -> 10, of which waited for: 5 -> 5; matrix products, arithmetic and copies ran while one was open for 4% -> 2% of each run, Pallas kernels for 3% -> 2%
where the time goes in v6:
time: 150 us; the launch traced here: 149 us
  starting transfers between devices  64 us (43%)
  blocking collectives  29 us (19%)
  Pallas kernels  27.8 us (19%)
  waiting for transfers between devices  22.1 us (15%)
  local copies, waits for them, and re-layouts  3.79 us (3%)
    ppermute x6, starting transfers between devices, rotate(): return lax.ppermute(value, 'section', pairs)  21.8 us
    all_to_all x2, blocking collectives, per_device(): sums = lax.all_to_all(sums, 'mp', 0, 0)  19.6 us
    pallas_call x5, Pallas kernels, local_call(): pl.pallas_call(kernel, out_shape=outs, in_specs=[SMEM] + [VMEM] * len(ope...  18.4 us
    all_to_all x1, starting transfers between devices, per_device(): lax.all_to_all(message.reshape(DP * SECTIONS, PAD, LANES), ('dp', 'sectio...  14.9 us
    all_to_all x1, starting transfers between devices, per_device(): texts = lax.all_to_all(pairs, 'dp', 0, 0).reshape(TEXTS, 2 * SLICE)  13 us
    all_to_all x1, blocking collectives, per_device(): parts = lax.all_to_all(parts, 'mp', 0, 0)  9.43 us
    all_to_all x1, starting transfers between devices, per_device(): tap_grads = lax.all_to_all(tap_sum, 'dp', 0, 0)[:, 0:5]  8.3 us
    all_to_all x1, waiting for transfers between devices, per_device(): parts = lax.all_to_all(parts, 'mp', 0, 0)  6.74 us
  transfers between devices with their start and end apart: 10, of which 5 were waited for; matrix products, arithmetic and copies ran while one was open for 2% of the time, Pallas kernels for 2%

profile of v6, /device:TPU:1, one launch (start us, length us, event | category | flops | bytes accessed | tf_op | source)
XLA Modules:
  0.0 148.8 jit_solution(541947632189934941)
XLA Ops:
  0.7 0.8 pad_maximum_fusion.8
  1.5 0.9 broadcast_in_dim.12
  2.5 13.0 %all-to-all-start = ((bf16[32,24,512]{2,1,0:T(8,128)(2,1)}), bf16[32,24,512]{2,1,0:T(8,128)(2,1)S(1)}, u32[]{:S(2)}, u32[]{:S(2)}) async-start(bf16[32,24,512]{2,1,0:T(8,128)(2,1)} %broadcast_in_dim.12), calls=%async_computation | async-start | bytes 1572864 | tf_op jit(solution)/shard_map/all_to_all | solution.py:541
  15.8 4.7 %collective-permute-start.1 = (bf16[112,1280]{1,0:T(8,128)(2,1)S(1)}, bf16[112,1280]{1,0:T(8,128)(2,1)S(1)}, u32[]{:S(2)}, u32[]{:S(2)}) collective-permute-start(bf16[112,1280]{1,0:T(8,128)(2,1)S(1)} %get-tuple-element.72), channel_id=1, source_target_pairs={{0,8},{4,12},{8,0},{12,4},{1,9},{5,13},{9,1},{13,5},{2,10},{6,14},... | collective-permute-start | bytes 860168 | tf_op jit(solution)/shard_map/ppermute | solution.py:519
  20.4 2.2 %collective-permute-start.2 = (bf16[112,1280]{1,0:T(8,128)(2,1)S(1)}, bf16[112,1280]{1,0:T(8,128)(2,1)S(1)}, u32[]{:S(2)}, u32[]{:S(2)}) collective-permute-start(bf16[112,1280]{1,0:T(8,128)(2,1)S(1)} %get-tuple-element.73), channel_id=1, source_target_pairs={{0,4},{4,8},{8,12},{12,0},{1,5},{5,9},{9,13},{13,1},{2,6},{6,10},{... | collective-permute-start | bytes 860168 | tf_op jit(solution)/shard_map/ppermute | solution.py:519
  22.7 4.3 %collective-permute-start = (bf16[112,1280]{1,0:T(8,128)(2,1)S(1)}, bf16[112,1280]{1,0:T(8,128)(2,1)S(1)}, u32[]{:S(2)}, u32[]{:S(2)}) collective-permute-start(bf16[112,1280]{1,0:T(8,128)(2,1)S(1)} %get-tuple-element.74), channel_id=1, source_target_pairs={{0,12},{4,0},{8,4},{12,8},{1,13},{5,1},{9,5},{13,9},{2,14},{6,2},{... | collective-permute-start | bytes 860168 | tf_op jit(solution)/shard_map/ppermute | solution.py:519
  27.0 0.7 constant_dynamic-slice_fusion
  27.7 6.4 %collective-permute-done.2.x1 = bf16[112,1280]{1,0:T(8,128)(2,1)S(1)} collective-permute-done((bf16[112,1280]{1,0:T(8,128)(2,1)S(1)}, bf16[112,1280]{1,0:T(8,128)(2,1)S(1)}, u32[]{:S(2)}, u32[]{:S(2)}) %collective-permute-start.2) | collective-permute-done | bytes 286752 | tf_op jit(solution)/shard_map/ppermute | solution.py:519
  34.1 2.9 %all-to-all-done = bf16[32,24,512]{2,1,0:T(8,128)(2,1)S(1)} async-done(((bf16[32,24,512]{2,1,0:T(8,128)(2,1)}), bf16[32,24,512]{2,1,0:T(8,128)(2,1)S(1)}, u32[]{:S(2)}, u32[]{:S(2)}) %all-to-all-start) | async-done | bytes 786464 | tf_op jit(solution)/shard_map/all_to_all | solution.py:541
  37.0 0.9 partial_scores.1
  37.8 5.9 %all-to-all-start.1 = ((f32[4,8,384]{2,1,0:T(8,128)}), f32[4,8,384]{2,1,0:T(8,128)S(1)}, u32[]{:S(2)}, u32[]{:S(2)}) async-start(f32[4,8,384]{2,1,0:T(8,128)} %partial_scores.1), calls=%async_computation.1 | async-start | bytes 98304 | tf_op jit(solution)/shard_map/all_to_all | solution.py:556
  43.8 6.7 %all-to-all-done.1.parts = f32[4,8,384]{2,1,0:T(8,128)S(1)} async-done(((f32[4,8,384]{2,1,0:T(8,128)}), f32[4,8,384]{2,1,0:T(8,128)S(1)}, u32[]{:S(2)}, u32[]{:S(2)}) %all-to-all-start.1) | async-done | bytes 49184 | tf_op jit(solution)/shard_map/all_to_all | solution.py:556
  50.6 1.4 softmax_grads_and_row_sums.1
  51.9 9.4 %all_to_all.35.parts = f32[4,24,128]{2,1,0:T(8,128)S(1)} all-to-all(f32[4,24,128]{2,1,0:T(8,128)S(1)} %get-tuple-element.37), channel_id=1, replica_groups=mesh['dp'=32,'section'=4,'mp'=4] {'mp'}, dimensions={0} | all-to-all | bytes 98304 | tf_op jit(solution)/shard_map/all_to_all | solution.py:566
  61.4 4.8 %sections_forward.1 = (f32[4,10,16,8,128]{4,3,2,1,0:T(8,128)S(1)}, f32[4,10,16,8,128]{4,3,2,1,0:T(8,128)S(1)}, f32[4,16,8,128]{3,2,1,0:T(8,128)S(1)}, f32[8,128]...) custom-call(f32[4,24,128]{2,1,0:T(8,128)S(1)} %all_to_all.35.parts, ...), custom_call_target="tpu_custom_call" | custom-call | flops 1000000000 | bytes 6000000 | tf_op jit(solution)/shard_map/sections_forward/pallas_call | solution.py:568
  66.2 5.4 %pair_matrices.1.matrices = f32[2,64,128]{2,1,0:T(8,128)S(1)} custom-call(s32[5]{0:T(128)S(1)} %stack.23.hops, f32[4,96,1280]{2,1,0:T(8,128)S(1)} %get-tuple-element.42.normed_rows, f32[4,10,16,8,128]{4,3,2,1,0:T(8,128)S(1)} %get-tuple-element.39.gate, f32[4,16,1280]{2,1,0:T(8,128)S(1)} %get-tuple-element.41.taps_in), custom_call_target="tpu_custom_call" | custom-call | flops 3000000000 | bytes 6000000 | tf_op jit(solution)/shard_map/pair_matrices/pallas_call | solution.py:505
  71.6 3.6 %head_and_sections.1 = (f32[10,16,8,128]{3,2,1,0:T(8,128)S(1)}, f32[16,1280]{1,0:T(8,128)S(1)}, f32[4,72,128]{2,1,0:T(8,128)S(1)}) custom-call(s32[5]{0:T(128)S(1)} %stack.23.hops, f32[4,24,128]{2,1,0:T(8,128)S(1)} %all_to_all.35.parts, bf16[1280,1024]{1,0:T(8,128)(2,1)S(1)} %copy-done, f32[4,10,16,8,128]{4,3,2,1,0:T(8,128)S(1)} %get-tuple-element.38.normed, ...), custom_call_target="tpu_custom_call" | custom-call | tf_op jit(solution)/shard_map/head_and_sections/pallas_call | solution.py:505
  75.2 9.8 %all_to_all.36.parts = f32[4,72,128]{2,1,0:T(8,128)S(1)} all-to-all(f32[4,72,128]{2,1,0:T(8,128)S(1)} %get-tuple-element.43), channel_id=1, replica_groups=mesh['dp'=32,'section'=4,'mp'=4] {'mp'}, dimensions={0} | all-to-all | bytes 294912 | tf_op jit(solution)/shard_map/all_to_all | solution.py:611
  85.0 5.0 %middle_sections.1 = (bf16[2,96,1280]{2,1,0:T(8,128)(2,1)S(1)}, f32[10,16,8,128]{3,2,1,0:T(8,128)S(1)}, f32[16,1280]{1,0:T(8,128)S(1)}, f32[16,1280]{1,0:T(8,128)S(1)}, f32[4,72,128]{2,1,0:T(8,128)S(1)}) custom-call(s32[5]{0:T(128)S(1)} %stack.23.hops, f32[4,72,128]{2,1,0:T(8,128)S(1)} %all_to_all.36.parts, f32[10,16,8,128]{3,2,1,0:T(8,128)S(1)} %get-tuple-element.44.up, ...), custom_call_target="tpu_custom_call" | custom-call | tf_op jit(solution)/shard_map/middle_sections/pallas_call | solution.py:505
  90.0 9.8 %all_to_all.37.parts = f32[4,72,128]{2,1,0:T(8,128)S(1)} all-to-all(f32[4,72,128]{2,1,0:T(8,128)S(1)} %get-tuple-element.46), channel_id=1, replica_groups=mesh['dp'=32,'section'=4,'mp'=4] {'mp'}, dimensions={0} | all-to-all | bytes 294912 | tf_op jit(solution)/shard_map/all_to_all | solution.py:620
  99.8 3.8 %end_sections.1 = (bf16[2,96,1280]{2,1,0:T(8,128)(2,1)S(1)}, bf16[1024,128]{1,0:T(8,128)(2,1)}) custom-call(s32[5]{0:T(128)S(1)} %stack.23.hops, f32[4,72,128]{2,1,0:T(8,128)S(1)} %all_to_all.37.parts, f32[10,16,8,128]{3,2,1,0:T(8,128)S(1)} %get-tuple-element.47.up, f32[4,10,16,8,128]{4,3,2,1,0:T(8,128)S(1)} %get-tuple-element.38.normed, ...), custom_call_target="tpu_custom_call" | custom-call | tf_op jit(solution)/shard_map/end_sections/pallas_call | solution.py:505
  103.5 14.9 %all-to-all-start.5 = ((bf16[128,8,128]{2,1,0:T(8,128)(2,1)}), bf16[128,8,128]{2,1,0:T(8,128)(2,1)S(1)}, u32[]{:S(2)}, u32[]{:S(2)}) async-start(bf16[128,8,128]{2,1,0:T(8,128)(2,1)} %bitcast.11), calls=%async_computation.5 | async-start | bytes 524288 | tf_op jit(solution)/shard_map/all_to_all | solution.py:631
  118.5 0.7 order_results.1
  119.2 3.3 %collective-permute-start.3 = (bf16[96,1280]{1,0:T(8,128)(2,1)S(1)}, bf16[96,1280]{1,0:T(8,128)(2,1)S(1)}, u32[]{:S(2)}, u32[]{:S(2)}) collective-permute-start(bf16[96,1280]{1,0:T(8,128)(2,1)S(1)} %get-tuple-element.56), channel_id=1, source_target_pairs={{0,4},{4,8},{8,12},{12,0},{1,5},{5,9},{9,13},{13,1},{2,6},{6,10},{... | collective-permute-start | bytes 737288 | tf_op jit(solution)/shard_map/ppermute | solution.py:519
  122.5 4.3 %collective-permute-start.4 = (bf16[96,1280]{1,0:T(8,128)(2,1)S(1)}, bf16[96,1280]{1,0:T(8,128)(2,1)S(1)}, u32[]{:S(2)}, u32[]{:S(2)}) collective-permute-start(bf16[96,1280]{1,0:T(8,128)(2,1)S(1)} %get-tuple-element.57), channel_id=1, source_target_pairs={{0,8},{4,12},{8,0},{12,4},{1,9},{5,13},{9,1},{13,5},{2,10},{6,14},... | collective-permute-start | bytes 737288 | tf_op jit(solution)/shard_map/ppermute | solution.py:519
  126.8 3.1 %collective-permute-start.5 = (bf16[96,1280]{1,0:T(8,128)(2,1)S(1)}, bf16[96,1280]{1,0:T(8,128)(2,1)S(1)}, u32[]{:S(2)}, u32[]{:S(2)}) collective-permute-start(bf16[96,1280]{1,0:T(8,128)(2,1)S(1)} %get-tuple-element.58), channel_id=1, source_target_pairs={{0,12},{4,0},{8,4},{12,8},{1,13},{5,1},{9,5},{13,9},{2,14},{6,2},{... | collective-permute-start | bytes 737288 | tf_op jit(solution)/shard_map/ppermute | solution.py:519
  129.9 1.2 all-to-all-done.5.message
  131.0 0.8 tap_sums.1.tap_sum
  131.8 8.3 %all-to-all-start.6 = ((bf16[32,8,128]{2,1,0:T(8,128)(2,1)}), bf16[32,8,128]{2,1,0:T(8,128)(2,1)S(1)}, u32[]{:S(2)}, u32[]{:S(2)}) async-start(bf16[32,8,128]{2,1,0:T(8,128)(2,1)} %tap_sums.1.tap_sum), calls=%async_computation.6 | async-start | bytes 131072 | tf_op jit(solution)/shard_map/all_to_all | solution.py:643
  140.1 1.5 %assemble_results.1 = bf16[2,12,16,1280]{3,2,1,0:T(8,128)(2,1)} custom-call(s32[5]{0:T(128)S(1)} %stack.23.hops, bf16[6,16,1280]{2,1,0:T(8,128)(2,1)S(1)} %bitcast.32, bf16[6,16,1280]{2,1,0:T(8,128)(2,1)S(1)} %bitcast.29, bf16[6,16,1280]{2,1,0:T(8,128)(2,1)S(1)} %bitcast.30, bf16[6,16,1280]{2,1,0:T(8,128)(2,1)S(1)} %bitcast.31, ...), custom_call_target="tpu_custom_call" | custom-call | flops 10000000000 | bytes 10000000 | tf_op jit(solution)/shard_map/assemble_results/pallas_call | solution.py:657
  143.2 4.9 %all-to-all-done.6 = bf16[32,8,128]{2,1,0:T(8,128)(2,1)S(1)} async-done(((bf16[32,8,128]{2,1,0:T(8,128)(2,1)}), bf16[32,8,128]{2,1,0:T(8,128)(2,1)S(1)}, u32[]{:S(2)}, u32[]{:S(2)}) %all-to-all-start.6) | async-done | bytes 65568 | tf_op jit(solution)/shard_map/all_to_all | solution.py:643
  148.1 0.7 reshape.90
  (36 shorter events, 1.8 us)
Async XLA Ops:
  0.6 14.9 %copy-start.5 = (f32[1,1280]{1,0:T(1,128)S(1)}, f32[1,1280]{1,0:T(1,128)}, u32[]{:S(2)}) copy-start(f32[1,1280]{1,0:T(1,128)} %param.9) | copy-start | bytes 15364
  0.6 14.9 %copy-start.3 = (bf16[1,2,12,16,1280]{4,3,2,1,0:T(8,128)(2,1)S(1)}, bf16[1,2,12,16,1280]{4,3,2,1,0:T(8,128)(2,1)}, u32[]{:S(2)}) copy-start(bf16[1,2,12,16,1280]{4,3,2,1,0:T(8,128)(2,1)} %param.8) | copy-start | bytes 2949124
  0.7 15.0 %copy-start.4 = (bf16[1,15,1280]{2,1,0:T(8,128)(2,1)S(1)}, bf16[1,15,1280]{2,1,0:T(8,128)(2,1)}, u32[]{:S(2)}) copy-start(bf16[1,15,1280]{2,1,0:T(8,128)(2,1)} %param.10) | copy-start | bytes 115204
  2.5 34.5 %all-to-all-start = ((bf16[32,24,512]{2,1,0:T(8,128)(2,1)}), bf16[32,24,512]{2,1,0:T(8,128)(2,1)S(1)}, u32[]{:S(2)}, u32[]{:S(2)}) async-start(bf16[32,24,512]{2,1,0:T(8,128)(2,1)} %broadcast_in_dim.12), calls=%async_computation | async-start | bytes 1572864 | tf_op jit(solution)/shard_map/all_to_all | solution.py:541
  15.5 35.0 %copy-start.1 = (s32[2,12]{1,0:T(2,128)S(1)}, s32[2,12]{1,0:T(2,128)}, u32[]{:S(2)}) copy-start(s32[2,12]{1,0:T(2,128)} %positives.1) | copy-start | bytes 292
  15.6 35.0 %copy-start.2 = (f32[2,12]{1,0:T(2,128)S(1)}, f32[2,12]{1,0:T(2,128)}, u32[]{:S(2)}) copy-start(f32[2,12]{1,0:T(2,128)} %weights.1) | copy-start | bytes 292
  15.8 11.9 %collective-permute-start.1 = (bf16[112,1280]{1,0:T(8,128)(2,1)S(1)}, bf16[112,1280]{1,0:T(8,128)(2,1)S(1)}, u32[]{:S(2)}, u32[]{:S(2)}) collective-permute-start(bf16[112,1280]{1,0:T(8,128)(2,1)S(1)} %get-tuple-element.72), channel_id=1, source_target_pairs={{0,8},{4,12},{8,0},{12,4},{1,9},{5,13},{9,1},{13,5},{2,10},{6,14},... | collective-permute-start | bytes 860168 | tf_op jit(solution)/shard_map/ppermute | solution.py:519
  20.4 13.6 %collective-permute-start.2 = (bf16[112,1280]{1,0:T(8,128)(2,1)S(1)}, bf16[112,1280]{1,0:T(8,128)(2,1)S(1)}, u32[]{:S(2)}, u32[]{:S(2)}) collective-permute-start(bf16[112,1280]{1,0:T(8,128)(2,1)S(1)} %get-tuple-element.73), channel_id=1, source_target_pairs={{0,4},{4,8},{8,12},{12,0},{1,5},{5,9},{9,13},{13,1},{2,6},{6,10},{... | collective-permute-start | bytes 860168 | tf_op jit(solution)/shard_map/ppermute | solution.py:519
  22.7 11.4 %collective-permute-start = (bf16[112,1280]{1,0:T(8,128)(2,1)S(1)}, bf16[112,1280]{1,0:T(8,128)(2,1)S(1)}, u32[]{:S(2)}, u32[]{:S(2)}) collective-permute-start(bf16[112,1280]{1,0:T(8,128)(2,1)S(1)} %get-tuple-element.74), channel_id=1, source_target_pairs={{0,12},{4,0},{8,4},{12,8},{1,13},{5,1},{9,5},{13,9},{2,14},{6,2},{... | collective-permute-start | bytes 860168 | tf_op jit(solution)/shard_map/ppermute | solution.py:519
  37.8 12.7 %all-to-all-start.1 = ((f32[4,8,384]{2,1,0:T(8,128)}), f32[4,8,384]{2,1,0:T(8,128)S(1)}, u32[]{:S(2)}, u32[]{:S(2)}) async-start(f32[4,8,384]{2,1,0:T(8,128)} %partial_scores.1), calls=%async_computation.1 | async-start | bytes 98304 | tf_op jit(solution)/shard_map/all_to_all | solution.py:556
  66.2 5.4 %copy-start = (bf16[1280,1024]{1,0:T(8,128)(2,1)S(1)}, bf16[1280,1024]{1,0:T(8,128)(2,1)}, u32[]{:S(2)}) copy-start(bf16[1280,1024]{1,0:T(8,128)(2,1)} %weight.1) | copy-start | bytes 7864324
  103.5 27.5 %all-to-all-start.5 = ((bf16[128,8,128]{2,1,0:T(8,128)(2,1)}), bf16[128,8,128]{2,1,0:T(8,128)(2,1)S(1)}, u32[]{:S(2)}, u32[]{:S(2)}) async-start(bf16[128,8,128]{2,1,0:T(8,128)(2,1)} %bitcast.11), calls=%async_computation.5 | async-start | bytes 524288 | tf_op jit(solution)/shard_map/all_to_all | solution.py:631
  119.2 21.0 %collective-permute-start.3 = (bf16[96,1280]{1,0:T(8,128)(2,1)S(1)}, bf16[96,1280]{1,0:T(8,128)(2,1)S(1)}, u32[]{:S(2)}, u32[]{:S(2)}) collective-permute-start(bf16[96,1280]{1,0:T(8,128)(2,1)S(1)} %get-tuple-element.56), channel_id=1, source_target_pairs={{0,4},{4,8},{8,12},{12,0},{1,5},{5,9},{9,13},{13,1},{2,6},{6,10},{... | collective-permute-start | bytes 737288 | tf_op jit(solution)/shard_map/ppermute | solution.py:519
  122.5 17.7 %collective-permute-start.4 = (bf16[96,1280]{1,0:T(8,128)(2,1)S(1)}, bf16[96,1280]{1,0:T(8,128)(2,1)S(1)}, u32[]{:S(2)}, u32[]{:S(2)}) collective-permute-start(bf16[96,1280]{1,0:T(8,128)(2,1)S(1)} %get-tuple-element.57), channel_id=1, source_target_pairs={{0,8},{4,12},{8,0},{12,4},{1,9},{5,13},{9,1},{13,5},{2,10},{6,14},... | collective-permute-start | bytes 737288 | tf_op jit(solution)/shard_map/ppermute | solution.py:519
  126.8 13.4 %collective-permute-start.5 = (bf16[96,1280]{1,0:T(8,128)(2,1)S(1)}, bf16[96,1280]{1,0:T(8,128)(2,1)S(1)}, u32[]{:S(2)}, u32[]{:S(2)}) collective-permute-start(bf16[96,1280]{1,0:T(8,128)(2,1)S(1)} %get-tuple-element.58), channel_id=1, source_target_pairs={{0,12},{4,0},{8,4},{12,8},{1,13},{5,1},{9,5},{13,9},{2,14},{6,2},{... | collective-permute-start | bytes 737288 | tf_op jit(solution)/shard_map/ppermute | solution.py:519
  131.8 16.2 %all-to-all-start.6 = ((bf16[32,8,128]{2,1,0:T(8,128)(2,1)}), bf16[32,8,128]{2,1,0:T(8,128)(2,1)S(1)}, u32[]{:S(2)}, u32[]{:S(2)}) async-start(bf16[32,8,128]{2,1,0:T(8,128)(2,1)} %tap_sums.1.tap_sum), calls=%async_computation.6 | async-start | bytes 131072 | tf_op jit(solution)/shard_map/all_to_all | solution.py:643

commit v7 on v6

--- a/solution.py
+++ b/solution.py
@@ -45,6 +45,14 @@
 def split_halves(value):
     high = value.astype(BF16)
     return high, (value - high.astype(F32)).astype(BF16)
+
+
+def over_blocks(block_step):
+    def two_blocks(pair, carry):
+        block_step(2 * pair, carry)
+        return block_step(2 * pair + 1, carry)
+
+    lax.fori_loop(0, BLOCKS // 2, two_blocks, 0)
 
 
 def lanes_of(block):
@@ -186,7 +194,7 @@
                 gate_out[hop, block, f] = gate * (1.0 + conv * (1.0 - gate))
             return carry
 
-        lax.fori_loop(0, BLOCKS, block_step, 0)
+        over_blocks(block_step)
 
 
 def pair_kernel(
@@ -223,7 +231,7 @@
                     left[start : start + FRAMES, lanes] = value * taps[k]
             return carry
 
-        lax.fori_loop(0, BLOCKS, block_step, 0)
+        over_blocks(block_step)
         columns = right[...]
         sums = lax.dot_general(plain[...], columns, NT, preferred_element_type=F32)
         first = jnp.zeros((FRAMES, 2 * LANES), F32)
@@ -467,7 +475,7 @@
     out[...] = jnp.broadcast_to(total[None], out.shape)
 
 
-def assemble_kernel(hops, own, first, second, third, tap_sum, out, sems):
+def assemble_kernel(hops, third, second, first, own, tap_sum, out, sems):
     copies = []
     for steps, part in enumerate((own, first, second, third)):
         source = (hops[SECTIONS] + SECTIONS - steps) & (SECTIONS - 1)
@@ -663,7 +671,7 @@
         compiler_params=PARAMS,
         cost_estimate=cost(10**10, 10**7),
         name="assemble_results",
-    )(hops, *pieces, tap_sum)
+    )(hops, *pieces[::-1], tap_sum)
     message, results = lax.optimization_barrier((message, results))
     columns = message[:, 5:7].reshape(DP, SECTIONS, MICRO, LANES)[..., : OWN * 32]
     columns = columns.reshape(DP, SECTIONS, MICRO, OWN, 32)[..., : MICRO * SHARD]

time: 150 us -> 148 us (0.987)
  starting transfers between devices: 64 us -> 61.5 us
    ppermute x6, waiting for transfers between devices: 6.41 us -> 7.94 us  [rotate(): return lax.ppermute(value, 'section', pairs)]
    all_to_all x1, waiting for transfers between devices: 4.89 us -> 3.36 us  [per_device(): tap_grads = lax.all_to_all(tap_sum, 'dp', 0, 0)[:, 0:5]]
  transfers between devices with their start and end apart: 10 -> 10, of which waited for: 5 -> 6; matrix products, arithmetic and copies ran while one was open for 2% -> 2% of each run, Pallas kernels for 2% -> 2%
where the time goes in v7:
time: 148 us; the launch traced here: 147 us
  starting transfers between devices  61.5 us (42%)
  blocking collectives  29 us (20%)
  Pallas kernels  27.4 us (19%)
  waiting for transfers between devices  23.3 us (16%)
  local copies, waits for them, and re-layouts  3.79 us (3%)
    ppermute x6, starting transfers between devices, rotate(): return lax.ppermute(value, 'section', pairs)  20.6 us
    all_to_all x2, blocking collectives, per_device(): sums = lax.all_to_all(sums, 'mp', 0, 0)  19.6 us
    pallas_call x5, Pallas kernels, local_call(): pl.pallas_call(kernel, out_shape=outs, in_specs=[SMEM] + [VMEM] * len(ope...  18.3 us
    all_to_all x1, starting transfers between devices, per_device(): lax.all_to_all(message.reshape(DP * SECTIONS, PAD, LANES), ('dp', 'sectio...  14.9 us
    all_to_all x1, starting transfers between devices, per_device(): texts = lax.all_to_all(pairs, 'dp', 0, 0).reshape(TEXTS, 2 * SLICE)  13 us
    all_to_all x1, blocking collectives, per_device(): parts = lax.all_to_all(parts, 'mp', 0, 0)  9.43 us
    ppermute x6, waiting for transfers between devices, rotate(): return lax.ppermute(value, 'section', pairs)  7.94 us
    all_to_all x1, starting transfers between devices, per_device(): tap_grads = lax.all_to_all(tap_sum, 'dp', 0, 0)[:, 0:5]  7.06 us
  transfers between devices with their start and end apart: 10, of which 6 were waited for; matrix products, arithmetic and copies ran while one was open for 2% of the time, Pallas kernels for 2%

profile of v7, /device:TPU:1, one launch (start us, length us, event | category | flops | bytes accessed | tf_op | source)
XLA Modules:
  0.0 147.2 jit_solution(14781214063720233005)
XLA Ops:
  0.7 0.8 pad_maximum_fusion.8
  1.5 0.9 broadcast_in_dim.12
  2.5 13.0 %all-to-all-start = ((bf16[32,24,512]{2,1,0:T(8,128)(2,1)}), bf16[32,24,512]{2,1,0:T(8,128)(2,1)S(1)}, u32[]{:S(2)}, u32[]{:S(2)}) async-start(bf16[32,24,512]{2,1,0:T(8,128)(2,1)} %broadcast_in_dim.12), calls=%async_computation | async-start | bytes 1572864 | tf_op jit(solution)/shard_map/all_to_all | solution.py:549
  15.8 4.7 %collective-permute-start.1 = (bf16[112,1280]{1,0:T(8,128)(2,1)S(1)}, bf16[112,1280]{1,0:T(8,128)(2,1)S(1)}, u32[]{:S(2)}, u32[]{:S(2)}) collective-permute-start(bf16[112,1280]{1,0:T(8,128)(2,1)S(1)} %get-tuple-element.72), channel_id=1, source_target_pairs={{0,8},{4,12},{8,0},{12,4},{1,9},{5,13},{9,1},{13,5},{2,10},{6,14},... | collective-permute-start | bytes 860168 | tf_op jit(solution)/shard_map/ppermute | solution.py:527
  20.4 2.2 %collective-permute-start.2 = (bf16[112,1280]{1,0:T(8,128)(2,1)S(1)}, bf16[112,1280]{1,0:T(8,128)(2,1)S(1)}, u32[]{:S(2)}, u32[]{:S(2)}) collective-permute-start(bf16[112,1280]{1,0:T(8,128)(2,1)S(1)} %get-tuple-element.73), channel_id=1, source_target_pairs={{0,4},{4,8},{8,12},{12,0},{1,5},{5,9},{9,13},{13,1},{2,6},{6,10},{... | collective-permute-start | bytes 860168 | tf_op jit(solution)/shard_map/ppermute | solution.py:527
  22.7 4.3 %collective-permute-start = (bf16[112,1280]{1,0:T(8,128)(2,1)S(1)}, bf16[112,1280]{1,0:T(8,128)(2,1)S(1)}, u32[]{:S(2)}, u32[]{:S(2)}) collective-permute-start(bf16[112,1280]{1,0:T(8,128)(2,1)S(1)} %get-tuple-element.74), channel_id=1, source_target_pairs={{0,12},{4,0},{8,4},{12,8},{1,13},{5,1},{9,5},{13,9},{2,14},{6,2},{... | collective-permute-start | bytes 860168 | tf_op jit(solution)/shard_map/ppermute | solution.py:527
  27.0 0.7 constant_dynamic-slice_fusion
  27.7 6.4 %collective-permute-done.2.x1 = bf16[112,1280]{1,0:T(8,128)(2,1)S(1)} collective-permute-done((bf16[112,1280]{1,0:T(8,128)(2,1)S(1)}, bf16[112,1280]{1,0:T(8,128)(2,1)S(1)}, u32[]{:S(2)}, u32[]{:S(2)}) %collective-permute-start.2) | collective-permute-done | bytes 286752 | tf_op jit(solution)/shard_map/ppermute | solution.py:527
  34.1 2.9 %all-to-all-done = bf16[32,24,512]{2,1,0:T(8,128)(2,1)S(1)} async-done(((bf16[32,24,512]{2,1,0:T(8,128)(2,1)}), bf16[32,24,512]{2,1,0:T(8,128)(2,1)S(1)}, u32[]{:S(2)}, u32[]{:S(2)}) %all-to-all-start) | async-done | bytes 786464 | tf_op jit(solution)/shard_map/all_to_all | solution.py:549
  37.0 0.9 partial_scores.1
  37.8 5.9 %all-to-all-start.1 = ((f32[4,8,384]{2,1,0:T(8,128)}), f32[4,8,384]{2,1,0:T(8,128)S(1)}, u32[]{:S(2)}, u32[]{:S(2)}) async-start(f32[4,8,384]{2,1,0:T(8,128)} %partial_scores.1), calls=%async_computation.1 | async-start | bytes 98304 | tf_op jit(solution)/shard_map/all_to_all | solution.py:564
  43.8 6.7 %all-to-all-done.1.parts = f32[4,8,384]{2,1,0:T(8,128)S(1)} async-done(((f32[4,8,384]{2,1,0:T(8,128)}), f32[4,8,384]{2,1,0:T(8,128)S(1)}, u32[]{:S(2)}, u32[]{:S(2)}) %all-to-all-start.1) | async-done | bytes 49184 | tf_op jit(solution)/shard_map/all_to_all | solution.py:564
  50.6 1.4 softmax_grads_and_row_sums.1
  51.9 9.4 %all_to_all.35.parts = f32[4,24,128]{2,1,0:T(8,128)S(1)} all-to-all(f32[4,24,128]{2,1,0:T(8,128)S(1)} %get-tuple-element.37), channel_id=1, replica_groups=mesh['dp'=32,'section'=4,'mp'=4] {'mp'}, dimensions={0} | all-to-all | bytes 98304 | tf_op jit(solution)/shard_map/all_to_all | solution.py:574
  61.4 4.6 %sections_forward.1 = (f32[4,10,16,8,128]{4,3,2,1,0:T(8,128)S(1)}, f32[4,10,16,8,128]{4,3,2,1,0:T(8,128)S(1)}, f32[4,16,8,128]{3,2,1,0:T(8,128)S(1)}, f32[8,128]...) custom-call(f32[4,24,128]{2,1,0:T(8,128)S(1)} %all_to_all.35.parts, ...), custom_call_target="tpu_custom_call" | custom-call | flops 1000000000 | bytes 6000000 | tf_op jit(solution)/shard_map/sections_forward/pallas_call | solution.py:576
  65.9 5.3 %pair_matrices.1.matrices = f32[2,64,128]{2,1,0:T(8,128)S(1)} custom-call(s32[5]{0:T(128)S(1)} %stack.23.hops, f32[4,96,1280]{2,1,0:T(8,128)S(1)} %get-tuple-element.42.normed_rows, f32[4,10,16,8,128]{4,3,2,1,0:T(8,128)S(1)} %get-tuple-element.39.gate, f32[4,16,1280]{2,1,0:T(8,128)S(1)} %get-tuple-element.41.taps_in), custom_call_target="tpu_custom_call" | custom-call | flops 3000000000 | bytes 6000000 | tf_op jit(solution)/shard_map/pair_matrices/pallas_call | solution.py:513
  71.2 3.6 %head_and_sections.1 = (f32[10,16,8,128]{3,2,1,0:T(8,128)S(1)}, f32[16,1280]{1,0:T(8,128)S(1)}, f32[4,72,128]{2,1,0:T(8,128)S(1)}) custom-call(s32[5]{0:T(128)S(1)} %stack.23.hops, f32[4,24,128]{2,1,0:T(8,128)S(1)} %all_to_all.35.parts, bf16[1280,1024]{1,0:T(8,128)(2,1)S(1)} %copy-done, f32[4,10,16,8,128]{4,3,2,1,0:T(8,128)S(1)} %get-tuple-element.38.normed, ...), custom_call_target="tpu_custom_call" | custom-call | tf_op jit(solution)/shard_map/head_and_sections/pallas_call | solution.py:513
  74.9 9.8 %all_to_all.36.parts = f32[4,72,128]{2,1,0:T(8,128)S(1)} all-to-all(f32[4,72,128]{2,1,0:T(8,128)S(1)} %get-tuple-element.43), channel_id=1, replica_groups=mesh['dp'=32,'section'=4,'mp'=4] {'mp'}, dimensions={0} | all-to-all | bytes 294912 | tf_op jit(solution)/shard_map/all_to_all | solution.py:619
  84.7 5.0 %middle_sections.1 = (bf16[2,96,1280]{2,1,0:T(8,128)(2,1)S(1)}, f32[10,16,8,128]{3,2,1,0:T(8,128)S(1)}, f32[16,1280]{1,0:T(8,128)S(1)}, f32[16,1280]{1,0:T(8,128)S(1)}, f32[4,72,128]{2,1,0:T(8,128)S(1)}) custom-call(s32[5]{0:T(128)S(1)} %stack.23.hops, f32[4,72,128]{2,1,0:T(8,128)S(1)} %all_to_all.36.parts, f32[10,16,8,128]{3,2,1,0:T(8,128)S(1)} %get-tuple-element.44.up, ...), custom_call_target="tpu_custom_call" | custom-call | tf_op jit(solution)/shard_map/middle_sections/pallas_call | solution.py:513
  89.6 9.8 %all_to_all.37.parts = f32[4,72,128]{2,1,0:T(8,128)S(1)} all-to-all(f32[4,72,128]{2,1,0:T(8,128)S(1)} %get-tuple-element.46), channel_id=1, replica_groups=mesh['dp'=32,'section'=4,'mp'=4] {'mp'}, dimensions={0} | all-to-all | bytes 294912 | tf_op jit(solution)/shard_map/all_to_all | solution.py:628
  99.4 3.8 %end_sections.1 = (bf16[2,96,1280]{2,1,0:T(8,128)(2,1)S(1)}, bf16[1024,128]{1,0:T(8,128)(2,1)}) custom-call(s32[5]{0:T(128)S(1)} %stack.23.hops, f32[4,72,128]{2,1,0:T(8,128)S(1)} %all_to_all.37.parts, f32[10,16,8,128]{3,2,1,0:T(8,128)S(1)} %get-tuple-element.47.up, f32[4,10,16,8,128]{4,3,2,1,0:T(8,128)S(1)} %get-tuple-element.38.normed, ...), custom_call_target="tpu_custom_call" | custom-call | tf_op jit(solution)/shard_map/end_sections/pallas_call | solution.py:513
  103.2 14.9 %all-to-all-start.5 = ((bf16[128,8,128]{2,1,0:T(8,128)(2,1)}), bf16[128,8,128]{2,1,0:T(8,128)(2,1)S(1)}, u32[]{:S(2)}, u32[]{:S(2)}) async-start(bf16[128,8,128]{2,1,0:T(8,128)(2,1)} %bitcast.11), calls=%async_computation.5 | async-start | bytes 524288 | tf_op jit(solution)/shard_map/all_to_all | solution.py:639
  118.8 4.5 %collective-permute-start.3 = (bf16[96,1280]{1,0:T(8,128)(2,1)S(1)}, bf16[96,1280]{1,0:T(8,128)(2,1)S(1)}, u32[]{:S(2)}, u32[]{:S(2)}) collective-permute-start(bf16[96,1280]{1,0:T(8,128)(2,1)S(1)} %get-tuple-element.55), channel_id=1, source_target_pairs={{0,12},{4,0},{8,4},{12,8},{1,13},{5,1},{9,5},{13,9},{2,14},{6,2},{... | collective-permute-start | bytes 737288 | tf_op jit(solution)/shard_map/ppermute | solution.py:527
  123.3 2.5 %collective-permute-start.4 = (bf16[96,1280]{1,0:T(8,128)(2,1)S(1)}, bf16[96,1280]{1,0:T(8,128)(2,1)S(1)}, u32[]{:S(2)}, u32[]{:S(2)}) collective-permute-start(bf16[96,1280]{1,0:T(8,128)(2,1)S(1)} %get-tuple-element.56), channel_id=1, source_target_pairs={{0,8},{4,12},{8,0},{12,4},{1,9},{5,13},{9,1},{13,5},{2,10},{6,14},... | collective-permute-start | bytes 737288 | tf_op jit(solution)/shard_map/ppermute | solution.py:527
  125.8 2.5 %collective-permute-start.5 = (bf16[96,1280]{1,0:T(8,128)(2,1)S(1)}, bf16[96,1280]{1,0:T(8,128)(2,1)S(1)}, u32[]{:S(2)}, u32[]{:S(2)}) collective-permute-start(bf16[96,1280]{1,0:T(8,128)(2,1)S(1)} %get-tuple-element.57), channel_id=1, source_target_pairs={{0,4},{4,8},{8,12},{12,0},{1,5},{5,9},{9,13},{13,1},{2,6},{6,10},{... | collective-permute-start | bytes 737288 | tf_op jit(solution)/shard_map/ppermute | solution.py:527
  128.3 2.4 %all-to-all-done.5.message = bf16[128,8,128]{2,1,0:T(8,128)(2,1)S(1)} async-done(((bf16[128,8,128]{2,1,0:T(8,128)(2,1)}), bf16[128,8,128]{2,1,0:T(8,128)(2,1)S(1)}, u32[]{:S(2)}, u32[]{:S(2)}) %all-to-all-start.5) | async-done | bytes 262176 | tf_op jit(solution)/shard_map/all_to_all | solution.py:639
  130.7 0.8 tap_sums.1.tap_sum
  131.5 7.1 %all-to-all-start.6 = ((bf16[32,8,128]{2,1,0:T(8,128)(2,1)}), bf16[32,8,128]{2,1,0:T(8,128)(2,1)S(1)}, u32[]{:S(2)}, u32[]{:S(2)}) async-start(bf16[32,8,128]{2,1,0:T(8,128)(2,1)} %tap_sums.1.tap_sum), calls=%async_computation.6 | async-start | bytes 131072 | tf_op jit(solution)/shard_map/all_to_all | solution.py:651
  138.6 1.5 %collective-permute-done.5 = bf16[96,1280]{1,0:T(8,128)(2,1)S(1)} collective-permute-done((bf16[96,1280]{1,0:T(8,128)(2,1)S(1)}, bf16[96,1280]{1,0:T(8,128)(2,1)S(1)}, u32[]{:S(2)}, u32[]{:S(2)}) %collective-permute-start.5) | collective-permute-done | bytes 245792 | tf_op jit(solution)/shard_map/ppermute | solution.py:527
  140.1 1.5 %assemble_results.1 = bf16[2,12,16,1280]{3,2,1,0:T(8,128)(2,1)} custom-call(s32[5]{0:T(128)S(1)} %stack.23.hops, bf16[6,16,1280]{2,1,0:T(8,128)(2,1)S(1)} %bitcast.29, bf16[6,16,1280]{2,1,0:T(8,128)(2,1)S(1)} %bitcast.30, bf16[6,16,1280]{2,1,0:T(8,128)(2,1)S(1)} %bitcast.31, bf16[6,16,1280]{2,1,0:T(8,128)(2,1)S(1)} %bitcast.32, ...), custom_call_target="tpu_custom_call" | custom-call | flops 10000000000 | bytes 10000000 | tf_op jit(solution)/shard_map/assemble_results/pallas_call | solution.py:665
  143.1 3.4 %all-to-all-done.6 = bf16[32,8,128]{2,1,0:T(8,128)(2,1)S(1)} async-done(((bf16[32,8,128]{2,1,0:T(8,128)(2,1)}), bf16[32,8,128]{2,1,0:T(8,128)(2,1)S(1)}, u32[]{:S(2)}, u32[]{:S(2)}) %all-to-all-start.6) | async-done | bytes 65568 | tf_op jit(solution)/shard_map/all_to_all | solution.py:651
  146.5 0.7 reshape.90
  (36 shorter events, 2.4 us)
Async XLA Ops:
  0.6 14.9 %copy-start.5 = (f32[1,1280]{1,0:T(1,128)S(1)}, f32[1,1280]{1,0:T(1,128)}, u32[]{:S(2)}) copy-start(f32[1,1280]{1,0:T(1,128)} %param.9) | copy-start | bytes 15364
  0.6 14.9 %copy-start.3 = (bf16[1,2,12,16,1280]{4,3,2,1,0:T(8,128)(2,1)S(1)}, bf16[1,2,12,16,1280]{4,3,2,1,0:T(8,128)(2,1)}, u32[]{:S(2)}) copy-start(bf16[1,2,12,16,1280]{4,3,2,1,0:T(8,128)(2,1)} %param.8) | copy-start | bytes 2949124
  0.7 15.0 %copy-start.4 = (bf16[1,15,1280]{2,1,0:T(8,128)(2,1)S(1)}, bf16[1,15,1280]{2,1,0:T(8,128)(2,1)}, u32[]{:S(2)}) copy-start(bf16[1,15,1280]{2,1,0:T(8,128)(2,1)} %param.10) | copy-start | bytes 115204
  2.5 34.5 %all-to-all-start = ((bf16[32,24,512]{2,1,0:T(8,128)(2,1)}), bf16[32,24,512]{2,1,0:T(8,128)(2,1)S(1)}, u32[]{:S(2)}, u32[]{:S(2)}) async-start(bf16[32,24,512]{2,1,0:T(8,128)(2,1)} %broadcast_in_dim.12), calls=%async_computation | async-start | bytes 1572864 | tf_op jit(solution)/shard_map/all_to_all | solution.py:549
  15.5 35.0 %copy-start.1 = (s32[2,12]{1,0:T(2,128)S(1)}, s32[2,12]{1,0:T(2,128)}, u32[]{:S(2)}) copy-start(s32[2,12]{1,0:T(2,128)} %positives.1) | copy-start | bytes 292
  15.6 35.0 %copy-start.2 = (f32[2,12]{1,0:T(2,128)S(1)}, f32[2,12]{1,0:T(2,128)}, u32[]{:S(2)}) copy-start(f32[2,12]{1,0:T(2,128)} %weights.1) | copy-start | bytes 292
  15.8 11.9 %collective-permute-start.1 = (bf16[112,1280]{1,0:T(8,128)(2,1)S(1)}, bf16[112,1280]{1,0:T(8,128)(2,1)S(1)}, u32[]{:S(2)}, u32[]{:S(2)}) collective-permute-start(bf16[112,1280]{1,0:T(8,128)(2,1)S(1)} %get-tuple-element.72), channel_id=1, source_target_pairs={{0,8},{4,12},{8,0},{12,4},{1,9},{5,13},{9,1},{13,5},{2,10},{6,14},... | collective-permute-start | bytes 860168 | tf_op jit(solution)/shard_map/ppermute | solution.py:527
  20.4 13.6 %collective-permute-start.2 = (bf16[112,1280]{1,0:T(8,128)(2,1)S(1)}, bf16[112,1280]{1,0:T(8,128)(2,1)S(1)}, u32[]{:S(2)}, u32[]{:S(2)}) collective-permute-start(bf16[112,1280]{1,0:T(8,128)(2,1)S(1)} %get-tuple-element.73), channel_id=1, source_target_pairs={{0,4},{4,8},{8,12},{12,0},{1,5},{5,9},{9,13},{13,1},{2,6},{6,10},{... | collective-permute-start | bytes 860168 | tf_op jit(solution)/shard_map/ppermute | solution.py:527
  22.7 11.4 %collective-permute-start = (bf16[112,1280]{1,0:T(8,128)(2,1)S(1)}, bf16[112,1280]{1,0:T(8,128)(2,1)S(1)}, u32[]{:S(2)}, u32[]{:S(2)}) collective-permute-start(bf16[112,1280]{1,0:T(8,128)(2,1)S(1)} %get-tuple-element.74), channel_id=1, source_target_pairs={{0,12},{4,0},{8,4},{12,8},{1,13},{5,1},{9,5},{13,9},{2,14},{6,2},{... | collective-permute-start | bytes 860168 | tf_op jit(solution)/shard_map/ppermute | solution.py:527
  37.8 12.7 %all-to-all-start.1 = ((f32[4,8,384]{2,1,0:T(8,128)}), f32[4,8,384]{2,1,0:T(8,128)S(1)}, u32[]{:S(2)}, u32[]{:S(2)}) async-start(f32[4,8,384]{2,1,0:T(8,128)} %partial_scores.1), calls=%async_computation.1 | async-start | bytes 98304 | tf_op jit(solution)/shard_map/all_to_all | solution.py:564
  65.9 5.3 %copy-start = (bf16[1280,1024]{1,0:T(8,128)(2,1)S(1)}, bf16[1280,1024]{1,0:T(8,128)(2,1)}, u32[]{:S(2)}) copy-start(bf16[1280,1024]{1,0:T(8,128)(2,1)} %weight.1) | copy-start | bytes 7864324
  103.2 27.5 %all-to-all-start.5 = ((bf16[128,8,128]{2,1,0:T(8,128)(2,1)}), bf16[128,8,128]{2,1,0:T(8,128)(2,1)S(1)}, u32[]{:S(2)}, u32[]{:S(2)}) async-start(bf16[128,8,128]{2,1,0:T(8,128)(2,1)} %bitcast.11), calls=%async_computation.5 | async-start | bytes 524288 | tf_op jit(solution)/shard_map/all_to_all | solution.py:639
  118.8 19.7 %collective-permute-start.3 = (bf16[96,1280]{1,0:T(8,128)(2,1)S(1)}, bf16[96,1280]{1,0:T(8,128)(2,1)S(1)}, u32[]{:S(2)}, u32[]{:S(2)}) collective-permute-start(bf16[96,1280]{1,0:T(8,128)(2,1)S(1)} %get-tuple-element.55), channel_id=1, source_target_pairs={{0,12},{4,0},{8,4},{12,8},{1,13},{5,1},{9,5},{13,9},{2,14},{6,2},{... | collective-permute-start | bytes 737288 | tf_op jit(solution)/shard_map/ppermute | solution.py:527
  123.3 15.2 %collective-permute-start.4 = (bf16[96,1280]{1,0:T(8,128)(2,1)S(1)}, bf16[96,1280]{1,0:T(8,128)(2,1)S(1)}, u32[]{:S(2)}, u32[]{:S(2)}) collective-permute-start(bf16[96,1280]{1,0:T(8,128)(2,1)S(1)} %get-tuple-element.56), channel_id=1, source_target_pairs={{0,8},{4,12},{8,0},{12,4},{1,9},{5,13},{9,1},{13,5},{2,10},{6,14},... | collective-permute-start | bytes 737288 | tf_op jit(solution)/shard_map/ppermute | solution.py:527
  125.8 14.3 %collective-permute-start.5 = (bf16[96,1280]{1,0:T(8,128)(2,1)S(1)}, bf16[96,1280]{1,0:T(8,128)(2,1)S(1)}, u32[]{:S(2)}, u32[]{:S(2)}) collective-permute-start(bf16[96,1280]{1,0:T(8,128)(2,1)S(1)} %get-tuple-element.57), channel_id=1, source_target_pairs={{0,4},{4,8},{8,12},{12,0},{1,5},{5,9},{9,13},{13,1},{2,6},{6,10},{... | collective-permute-start | bytes 737288 | tf_op jit(solution)/shard_map/ppermute | solution.py:527
  131.5 15.0 %all-to-all-start.6 = ((bf16[32,8,128]{2,1,0:T(8,128)(2,1)}), bf16[32,8,128]{2,1,0:T(8,128)(2,1)S(1)}, u32[]{:S(2)}, u32[]{:S(2)}) async-start(bf16[32,8,128]{2,1,0:T(8,128)(2,1)} %tap_sums.1.tap_sum), calls=%async_computation.6 | async-start | bytes 131072 | tf_op jit(solution)/shard_map/all_to_all | solution.py:651
